TPU v7x, 128 devices: a whole 4x4x4 slice. The times are simulated.
128 devices in a mesh: wide: 16 (over z, y), narrow: 8 (over x, core).
Axes of the slice: x: 4, y: 4, z: 4, core: 2. Of those that a mesh axis runs over, the one named last changes fastest.
Arguments:
- text_tokens: bfloat16 [16, 256, 3072], P('wide', 'narrow'), may hold values from -6 to 6
- image_tokens: bfloat16 [16, 512, 3072], P('wide', 'narrow'), may hold values from -6 to 6
- extra_tokens: bfloat16 [16, 128, 3072], P('wide', 'narrow'), may hold values from -6 to 6
- text_pos: int32 [3, 16, 256], P(None, 'wide'), may hold values from 0 to 63
- image_pos: int32 [3, 16, 512], P(None, 'wide'), may hold values from 0 to 63
- extra_pos: int32 [3, 16, 128], P(None, 'wide'), may hold values from 0 to 63
- extra_counts: int32 [128], replicated, may hold values from 1 to 16, 896 in all
- request_group: int32 [16], replicated, may hold values from 0 to 15, each once
- step_index: int32 [17], replicated, may hold values from 0 to 3
- mod_table: float32 [4, 3, 3072], replicated, may hold values from -3 to 3
- final_table: float32 [4, 2, 3072], replicated, may hold values from -3 to 3
- qkv_weight: bfloat16 [3, 3072, 3072], P(None, None, 'narrow'), may hold values from -0.109375 to 0.109375
- q_scale: float32 [128], replicated, may hold values from 1 to 2.5
- k_scale: float32 [128], replicated, may hold values from 1 to 2.5
- attn_out_weight: bfloat16 [3072, 3072], P('narrow'), may hold values from -0.046875 to 0.046875
- mlp_in_weight: bfloat16 [3072, 12288], P('wide', 'narrow'), may hold values from -0.109375 to 0.109375
- mlp_out_weight: bfloat16 [12288, 3072], P('narrow', 'wide'), may hold values from -0.046875 to 0.046875
- proj_weight: bfloat16 [3072, 64], replicated, may hold values from -0.109375 to 0.109375
- stencil: float32 [9, 64], replicated, may hold values from -2 to 2
- latent: float32 [16, 16, 2048], P('wide', 'narrow'), may hold values from -6 to 6
Outputs:
- text_out: bfloat16 [16, 256, 3072], P('wide', 'narrow')
- image_out: bfloat16 [16, 512, 3072], P('wide', 'narrow')
- extra_out: bfloat16 [16, 128, 3072], P('wide', 'narrow')
- latent_next: float32 [16, 16, 2048], P('wide', 'narrow')
Inputs may be any that keep to these rules, and one draw needn't show every extreme that they name: extra_counts[d] live slots of the split request on device d (devices ordered along wide, then narrow); they sum to 896, and some device holds exactly 16. `request_group`: a permutation of the requests.
All inputs are finite; a program needn't handle non-finite values.
Results may differ from a plain program's by a relative error of at most 0.01.
Values may be sent and summed in bfloat16 or wider, within the bound.
No kernel may reach another device: no remote copies, remote signals or barrier semaphores. Data moves between devices by JAX's collectives and lax.ppermute only.
A program may use at most 128 MiB of HBM per device.

v0:
```python
import math

import jax
import jax.numpy as jnp
from jax import lax
from jax.sharding import PartitionSpec as P

STEPS = 4


EPSILON = 1e-06
ROPE_BASE = 10000.0


def extended(cells, sides, width):
    for axis, dim in sides:
        count = lax.axis_size(axis)
        ends = count - 1
        head = lax.slice_in_dim(cells, 0, width, axis=dim)
        tail = lax.slice_in_dim(cells, cells.shape[dim] - width, cells.shape[dim], axis=dim)
        cells = jnp.concatenate(
            [
                lax.ppermute(tail, axis, [(i, (i + 1) % count) for i in range(ends)]),
                cells,
                lax.ppermute(head, axis, [((i + 1) % count, i) for i in range(ends)]),
            ],
            axis=dim,
        )
    return cells


def layer_norm(values):
    centre = jnp.mean(values, axis=-1, keepdims=True)
    centred = values - centre
    spread = jnp.mean(centred * centred, axis=-1, keepdims=True)
    return centred * lax.rsqrt(spread + EPSILON)


def modulate(tokens, shift_vec, scale_vec):
    return layer_norm(tokens.astype(jnp.float32)) * (1.0 + scale_vec) + shift_vec


def section_widths(head_dim):
    return (head_dim // 8, 7 * head_dim // 16, 7 * head_dim // 16)


def rope_tables(positions, head_dim):
    angle_list = []
    for axis_id, section in enumerate(section_widths(head_dim)):
        half_width = section // 2
        exponent = -2.0 * jnp.arange(half_width, dtype=jnp.float32) / section
        frequency = jnp.power(jnp.float32(ROPE_BASE), exponent)
        angles = positions[axis_id].astype(jnp.float32)[:, None] * frequency[None, :]
        angle_list.append(angles)
        angle_list.append(angles)
    angles = jnp.concatenate(angle_list, axis=1)
    return (jnp.cos(angles), jnp.sin(angles))


def rotate(head_rows, cosine, sine_vals):
    pieces = []
    offset = 0
    for section in section_widths(head_rows.shape[-1]):
        half_width = section // 2
        first_half = head_rows[..., offset : offset + half_width]
        second = head_rows[..., offset + half_width : offset + section]
        pieces.append(-second)
        pieces.append(first_half)
        offset += section
    partner = jnp.concatenate(pieces, axis=-1)
    return head_rows * cosine[:, None, :] + partner * sine_vals[:, None, :]


def head_norm(head_rows, gain_vec):
    square = jnp.mean(head_rows * head_rows, axis=-1, keepdims=True)
    return head_rows * lax.rsqrt(square + EPSILON) * gain_vec


def project_heads(modulated, qkv_parts, q_scale, k_scale, positions):
    head_dim = q_scale.shape[0]
    row_total = modulated.shape[0]
    cosine, sine_vals = rope_tables(positions, head_dim)
    outputs = []
    for which in range(3):
        projected = jnp.dot(modulated, qkv_parts[which], preferred_element_type=jnp.float32)
        projected = projected.reshape(row_total, -1, head_dim)
        if which == 0:
            projected = rotate(head_norm(projected, q_scale), cosine, sine_vals)
        if which == 1:
            projected = rotate(head_norm(projected, k_scale), cosine, sine_vals)
        outputs.append(projected.astype(jnp.bfloat16))
    return outputs


def attend(queries, key_rows, value_rows, live_mask):
    factor = 1.0 / math.sqrt(queries.shape[-1])
    query_heads = jnp.transpose(queries, (1, 0, 2))
    key_heads = jnp.transpose(key_rows, (1, 0, 2))
    value_heads = jnp.transpose(value_rows, (1, 0, 2))

    def per_head(head_items):
        query_h, key_h, value_h = head_items
        scores = jnp.dot(query_h, key_h.T, preferred_element_type=jnp.float32) * factor
        weights = jnp.exp(scores)
        if live_mask is not None:
            weights = jnp.where(live_mask[None, :], weights, 0.0)
        running = jnp.sum(weights, axis=1)
        accumulated = jnp.dot(
            weights.astype(jnp.bfloat16), value_h, preferred_element_type=jnp.float32
        )
        return (accumulated, running)

    return lax.map(per_head, (query_heads, key_heads, value_heads))


def finish(accumulated, running):
    normed = accumulated / running[..., None]
    normed = jnp.transpose(normed, (1, 0, 2))
    return normed.reshape(normed.shape[0], -1).astype(jnp.bfloat16)


def noise_level(step_value):
    level = 1.0 - step_value.astype(jnp.float32) / STEPS
    return 3.0 * level / (1.0 + 2.0 * level)


def final_velocity(hidden_rows, final_mod, proj_weight):
    normed = modulate(hidden_rows, final_mod[0], final_mod[1]).astype(jnp.bfloat16)
    return jnp.dot(normed, proj_weight, preferred_element_type=jnp.float32)


def smooth(padded_rows, stencil, grid_width):
    channels = stencil.shape[1]
    row_total = padded_rows.shape[0] - 2
    cells = padded_rows.reshape(row_total + 2, grid_width, channels)
    cells = jnp.pad(cells, ((0, 0), (1, 1), (0, 0)))
    result = jnp.zeros((row_total, grid_width, channels), jnp.float32)
    for row_tap in range(3):
        for col_tap in range(3):
            result = (
                result
                + stencil[3 * row_tap + col_tap]
                * cells[row_tap : row_tap + row_total, col_tap : col_tap + grid_width]
            )
    return result.reshape(row_total, grid_width * channels)


def table_row(table, step_value):
    one_hot = (jnp.arange(table.shape[0], dtype=jnp.int32) == step_value).astype(jnp.float32)
    return jnp.einsum("s,skd->kd", one_hot, table, precision=lax.Precision.HIGHEST)


def per_device(
    text_tokens,
    image_tokens,
    extra_tokens,
    text_pos,
    image_pos,
    extra_pos,
    extra_counts,
    request_group,
    step_index,
    mod_table,
    final_table,
    qkv_weight,
    q_scale,
    k_scale,
    attn_out_weight,
    mlp_in_weight,
    mlp_out_weight,
    proj_weight,
    stencil,
    latent,
):
    group_index = lax.axis_index("wide")
    narrow_index = lax.axis_index("narrow")
    narrow_count = lax.axis_size("narrow")
    group_ids = jnp.arange(request_group.shape[0], dtype=jnp.int32)
    request_here = jnp.sum(jnp.where(group_ids == group_index, request_group, 0))
    step_ids = jnp.arange(step_index.shape[0], dtype=jnp.int32)
    step_here = jnp.sum(jnp.where(step_ids == request_here, step_index, 0))
    extra_step_value = step_index[step_index.shape[0] - 1]
    modulation = table_row(mod_table, step_here)
    extra_mod = table_row(mod_table, extra_step_value)
    final_mod = table_row(final_table, step_here)
    text_own = text_tokens[0]
    image_own = image_tokens[0]
    extra_own = extra_tokens[0]
    text_all, image_all, extra_all = (
        lax.all_gather(text_own, "narrow", axis=0, tiled=True),
        lax.all_gather(image_own, "narrow", axis=0, tiled=True),
        lax.all_gather(extra_own, "narrow", axis=0, tiled=True),
    )
    text_count = text_all.shape[0]
    request_count = text_count + image_all.shape[0]
    request_rows = jnp.concatenate([text_all, image_all], axis=0)
    modulated = jnp.concatenate(
        [
            modulate(request_rows, modulation[0], modulation[1]),
            modulate(extra_all, extra_mod[0], extra_mod[1]),
        ],
        axis=0,
    ).astype(jnp.bfloat16)
    positions = jnp.concatenate([text_pos[:, 0], image_pos[:, 0], extra_pos[:, 0]], axis=1)
    queries, key_rows, value_rows = project_heads(
        modulated, qkv_weight, q_scale, k_scale, positions
    )
    accumulated, running = attend(
        queries[:request_count], key_rows[:request_count], value_rows[:request_count], None
    )
    attn_request = finish(accumulated, running)
    extra_queries = queries[request_count:]
    slot_cap = extra_own.shape[0]
    device_ids = jnp.arange(extra_counts.shape[0], dtype=jnp.int32)
    key_part = lax.all_gather(key_rows[request_count:], "wide", axis=0, tiled=True)
    value_part = lax.all_gather(value_rows[request_count:], "wide", axis=0, tiled=True)
    slot_ids = jnp.arange(key_part.shape[0], dtype=jnp.int32)
    owner_ids = slot_ids // slot_cap
    live_count = jnp.sum(
        jnp.where(owner_ids[:, None] == device_ids[None, :], extra_counts[None, :], 0), axis=1
    )
    live_mask = slot_ids % slot_cap < live_count
    accum_part, running_part = attend(extra_queries, key_part, value_part, live_mask)
    attn_rows = jnp.concatenate([attn_request, finish(accum_part, running_part)], axis=0)
    mlp_pre = jnp.dot(
        modulated,
        lax.all_gather(mlp_in_weight, "wide", axis=0, tiled=True),
        preferred_element_type=jnp.float32,
    )
    mlp_act = jax.nn.gelu(mlp_pre, approximate=True).astype(jnp.bfloat16)
    mlp_tail = jnp.dot(
        mlp_act,
        lax.all_gather(mlp_out_weight, "wide", axis=1, tiled=True),
        preferred_element_type=jnp.float32,
    )
    partial_value = (
        jnp.dot(attn_rows, attn_out_weight, preferred_element_type=jnp.float32) + mlp_tail
    )
    text_part = partial_value[:text_count]
    image_part = partial_value[text_count:request_count]
    extra_part = partial_value[request_count:]
    channels = proj_weight.shape[1]
    grid_width = latent.shape[2] // channels
    sum_text, sum_image, sum_extra = (
        lax.psum_scatter(
            text_part.astype(jnp.bfloat16), "narrow", scatter_dimension=0, tiled=True
        ).astype(jnp.float32),
        lax.psum_scatter(
            image_part.astype(jnp.bfloat16), "narrow", scatter_dimension=0, tiled=True
        ).astype(jnp.float32),
        lax.psum_scatter(
            extra_part.astype(jnp.bfloat16), "narrow", scatter_dimension=0, tiled=True
        ).astype(jnp.float32),
    )
    image_hidden = image_own.astype(jnp.float32) + modulation[2] * sum_image
    velocity = final_velocity(image_hidden, final_mod, proj_weight).reshape(
        -1, grid_width * channels
    )
    padded = extended(velocity, (("narrow", 0),), 1)
    text_hidden = text_own.astype(jnp.float32) + modulation[2] * sum_text
    extra_hidden = extra_own.astype(jnp.float32) + extra_mod[2] * sum_extra
    device_here = group_index * narrow_count + narrow_index
    own_count = jnp.sum(jnp.where(device_ids == device_here, extra_counts, 0))
    own_live = jnp.arange(slot_cap, dtype=jnp.int32) < own_count
    extra_hidden = jnp.where(own_live[:, None], extra_hidden, 0.0)
    time_delta = noise_level(step_here + 1) - noise_level(step_here)
    latent_next = latent[0] + time_delta * smooth(padded, stencil, grid_width)
    return (
        text_hidden.astype(jnp.bfloat16)[None],
        image_hidden.astype(jnp.bfloat16)[None],
        extra_hidden.astype(jnp.bfloat16)[None],
        latent_next[None],
    )


def solution(mesh):
    return jax.shard_map(
        per_device,
        mesh=mesh,
        in_specs=(
            P("wide", "narrow", None),
            P("wide", "narrow", None),
            P("wide", "narrow", None),
            P(None, "wide", None),
            P(None, "wide", None),
            P(None, "wide", None),
            P(),
            P(),
            P(),
            P(),
            P(),
            P(None, None, "narrow"),
            P(),
            P(),
            P("narrow", None),
            P("wide", "narrow"),
            P("narrow", "wide"),
            P(),
            P(),
            P("wide", "narrow", None),
        ),
        out_specs=(
            P("wide", "narrow", None),
            P("wide", "narrow", None),
            P("wide", "narrow", None),
            P("wide", "narrow", None),
        ),
        check_vma=False,
    )
```

profile of v0, /device:TPU:1, one launch (start us, length us, event | category | flops | bytes accessed | tf_op | source)
XLA Modules:
  0.0 507.4 jit_solution(17555227779035927348)
XLA Ops:
  8.7 1.2 slice.184
  9.9 1.8 fusion.99
  11.8 1.3 fusion.109
  13.1 2.0 fusion.110
  15.1 1.9 fusion.102
  17.6 6.3 %slice_bitcast_fusion = (bf16[384,3072]{0,1:T(8,128)(2,1)}, bf16[384,3072]{0,1:T(8,128)(2,1)}, bf16[384,3072]{0,1:T(8,128)(2,1)}) fusion(bf16[3,3072,384]{2,1,0:T(8,128)(2,1)} %param.35), kind=kLoop, calls=%fused_computation.61 | loop fusion | bytes 14155776 | tf_op jit(solution)/shard_map/dot_general | solution.py:85
  23.9 4.3 copy.41
  28.3 4.3 copy.40
  33.2 15.1 %all-gather.2 = bf16[1,128,3072]{2,1,0:T(8,128)(2,1)S(1)} all-gather(bf16[1,16,3072]{2,1,0:T(8,128)(2,1)S(1)} %copy-done.15), channel_id=4, replica_groups=mesh['wide'=16,'narrow'=8] {'narrow'}, dimensions={1}, use_global_device_ids=true | all-gather | bytes 884736 | tf_op jit(solution)/shard_map/all_gather | solution.py:192
  48.9 2.5 fusion.127
  52.6 1.3 fusion.59
  54.0 13.5 %all-gather.20.cloned.1.call-done = bf16[1,512,3072]{2,1,0:T(8,128)(2,1)} async-done(((bf16[1,64,3072]{2,1,0:T(8,128)(2,1)}), bf16[1,512,3072]{2,1,0:T(8,128)(2,1)}) %all-gather.20.cloned.1.call-update) | async-done | bytes 3145744 | tf_op jit(solution)/shard_map/all_gather | solution.py:191
  67.5 3.2 convert_reduce_fusion
  71.3 2.5 fusion.29
  73.8 4.8 fusion.32
  78.6 2.7 multiply_reduce_fusion
  82.2 1.0 fusion.123
  83.8 2.7 multiply_reduce_fusion.1
  86.8 0.9 fusion.126
  87.7 1.2 fusion.125
  88.9 10.4 %concatenate.51 = f32[896,3,128]{0,2,1:T(8,128)} concatenate(f32[896,3,8]{0,2,1:T(8,128)} %get-tuple-element.159, f32[896,3,8]{0,2,1:T(8,128)} %get-tuple-element.158, f32[896,3,28]{0,2,1:T(8,128)} %get-tuple-element.157, f32[896,3,28]{0,2,1:T(8,128)} %get-tuple-element.156, f32[896,3,28]{0,2,1:T(8,128)S(1)} %get-tuple-element.155, f32[896,3,28]{0,2,1:T(8,128)S(1)} %get-tuple-element.154), dimensions={2} | concatenate | bytes 2752512 | tf_op jit(solution)/shard_map/concatenate | solution.py:70
  99.3 11.5 %concatenate.50 = f32[896,3,128]{0,2,1:T(8,128)} concatenate(f32[896,3,8]{0,2,1:T(8,128)} %get-tuple-element.165, f32[896,3,8]{0,2,1:T(8,128)} %get-tuple-element.164, f32[896,3,28]{0,2,1:T(8,128)} %get-tuple-element.163, f32[896,3,28]{0,2,1:T(8,128)} %get-tuple-element.162, f32[896,3,28]{0,2,1:T(8,128)} %get-tuple-element.161, f32[896,3,28]{0,2,1:T(8,128)} %get-tuple-element.160), dimensions={2} | concatenate | bytes 2752512 | tf_op jit(solution)/shard_map/concatenate | solution.py:70
  110.8 3.4 add_convert_fusion.1
  115.8 4.3 copy.42
  120.1 6.4 %fusion.60 = bf16[896,3,128]{2,0,1:T(8,128)(2,1)S(1)} fusion(bf16[3,128,3072]{2,1,0:T(8,128)(2,1)} %bitcast.216, bf16[128,3072]{1,0:T(8,128)(2,1)} %fusion.59, bf16[768,3072]{1,0:T(8,128)(2,1)} %copy-done.6), kind=kOutput, calls=%fused_computation.79 | convolution fusion | flops 2125283328 | bytes 8552448 | tf_op jit(solution)/shard_map/dot_general | solution.py:85
  131.1 1.9 slice_bitcast_fusion.3
  133.0 1.3 slice_bitcast_fusion.4
  134.3 8.6 %while.24 = (s32[]{:T(128)}, f32[3,768,128]{1,2,0:T(8,128)}, f32[3,768]{1,0:T(4,128)S(1)}, bf16[3,768,128]{1,2,0:T(8,128)(2,1)S(1)}, bf16[3,768,128]{1,2,0:T(8,1...) while((s32[]{:T(128)}, f32[3,768,128]{1,2,0:T(8,128)}, f32[3,768]{1,0:T(4,128)S(1)}, ...), condition=%wide.region_10.11_spmd, body=%wide.region_8.10_spmd.sunk | while | flops 304348416 | bytes 5719137 | solution.py:113
  135.0 2.2 fusion.152
  137.8 2.2 fusion.152
  140.7 2.2 fusion.152
  142.9 1.4 divide_convert_fusion
  144.3 15.6 %all-gather.10.cloned.1.call-done = bf16[2048,3,128]{0,2,1:T(8,128)(2,1)} async-done(((bf16[128,3,128]{0,2,1:T(8,128)(2,1)}), bf16[2048,3,128]{0,2,1:T(8,128)(2,1)}) %all-gather.10.cloned.1.call-update) | async-done | bytes 1572880 | tf_op jit(solution)/shard_map/all_gather | solution.py:215
  159.8 45.6 %all-gather.12.cloned.1.call-done = bf16[2048,3,128]{2,0,1:T(8,128)(2,1)} async-done(((bf16[128,3,128]{2,0,1:T(8,128)(2,1)}), bf16[2048,3,128]{2,0,1:T(8,128)(2,1)}) %all-gather.12.cloned.1.call-update) | async-done | bytes 1572880 | tf_op jit(solution)/shard_map/all_gather | solution.py:216
  205.5 14.5 %while.25 = (s32[]{:T(128)}, f32[3,128,128]{1,2,0:T(8,128)}, f32[3,128]{1,0:T(4,128)}, pred[2048]{0:T(1024)(128)(4,1)}, bf16[3,128,128]{1,2,0:T(8,128)(2,1)}, /*...) while((s32[]{:T(128)}, f32[3,128,128]{1,2,0:T(8,128)}, ...), condition=%wide.region_14.15_spmd, body=%wide.region_12.14_spmd.sunk | while | flops 135266176 | bytes 2201193 | solution.py:113
  205.5 1.5 fusion.155
  207.0 2.0 fusion.156
  209.0 1.3 dynamic_update_slice.25
  210.3 1.5 fusion.155
  211.8 2.0 fusion.156
  213.9 1.3 dynamic_update_slice.25
  215.1 1.5 fusion.155
  216.6 2.1 fusion.156
  218.7 1.3 dynamic_update_slice.25
  220.0 1.0 divide_convert_fusion.1
  220.9 62.4 %all-gather.16.cloned.1.call-done = bf16[1536,3072]{0,1:T(8,128)(2,1)} async-done(((bf16[1536,192]{0,1:T(8,128)(2,1)}), bf16[1536,3072]{0,1:T(8,128)(2,1)}) %all-gather.16.cloned.1.call-update) | async-done | bytes 9437200 | tf_op jit(solution)/shard_map/all_gather | solution.py:233
  283.4 77.3 %all-gather.14.cloned.1.call-done = bf16[3072,1536]{1,0:T(8,128)(2,1)} async-done(((bf16[192,1536]{1,0:T(8,128)(2,1)}), bf16[3072,1536]{1,0:T(8,128)(2,1)}) %all-gather.14.cloned.1.call-update) | async-done | bytes 9437200 | tf_op jit(solution)/shard_map/all_gather | solution.py:227
  360.7 27.2 %fusion.47 = f32[896,3072]{1,0:T(8,128)} fusion(bf16[1536,3072]{0,1:T(8,128)(2,1)} %all-gather.16.cloned.1.call-done, bf16[3072,1536]{1,0:T(8,128)(2,1)} %all-gather.14.cloned.1.call-done, bf16[128,3072]{1,0:T(8,128)(2,1)} %fusion.59, bf16[768,3072]{1,0:T(8,128)(2,1)} %copy-done.6), kind=kOutput, calls=%fused_computation.56 | convolution fusion | flops 16934830080 | bytes 35389440 | tf_op jit(solution)/shard_map/dot_general | solution.py:231
  387.9 5.9 %add_convert_fusion = bf16[896,3072]{1,0:T(8,128)(2,1)S(1)} fusion(f32[896,3072]{1,0:T(8,128)} %fusion.47, bf16[384,3072]{1,0:T(8,128)(2,1)S(1)} %copy-done, bf16[128,384]{0,1:T(8,128)(2,1)S(1)} %bitcast.218, bf16[768,384]{0,1:T(8,128)(2,1)S(1)} %bitcast.217), kind=kOutput, calls=%fused_computation.34 | convolution fusion | flops 2120810496 | bytes 19562496 | tf_op jit(solution)/shard_map/dot_general | solution.py:237
  393.7 2.4 copy-done.1
  396.1 0.9 slice.264
  397.1 3.8 slice.262
  401.1 2.8 slice.261
  404.0 1.0 fusion.75
  407.8 17.7 %reduce-scatter.8.cloned.1.call-done = bf16[16,3072]{1,0:T(8,128)(2,1)} async-done(((bf16[128,3072]{1,0:T(8,128)(2,1)}), bf16[16,3072]{1,0:T(8,128)(2,1)}) %reduce-scatter.8.cloned.1.call-update) | async-done | bytes 98320 | tf_op jit(solution)/shard_map/reduce_scatter | solution.py:251
  425.5 1.6 fusion.74
  427.1 35.2 %reduce-scatter.6.cloned.1.call-done = bf16[64,3072]{1,0:T(8,128)(2,1)} async-done(((bf16[512,3072]{1,0:T(8,128)(2,1)}), bf16[64,3072]{1,0:T(8,128)(2,1)}) %reduce-scatter.6.cloned.1.call-update) | async-done | bytes 393232 | tf_op jit(solution)/shard_map/reduce_scatter | solution.py:248
  462.3 1.2 fusion.66
  463.5 2.0 multiply_reduce_fusion.2
  465.6 1.5 fusion.70
  467.2 5.4 %collective-permute-start.1 = (f32[1,2048]{1,0:T(1,128)S(1)}, f32[1,2048]{1,0:T(1,128)S(1)}, u32[]{:S(2)}, u32[]{:S(2)}) collective-permute-start(f32[1,2048]{1,0:T(1,128)S(1)} %slice.221), channel_id=1, source_target_pairs={{1,0},{2,1},{3,2},{4,3},{5,4},{6,5},{7,6},{9,8},{10,9},{11,10},{12... | collective-permute-start | bytes 24584 | tf_op jit(solution)/shard_map/ppermute | solution.py:25
  472.7 1.9 collective-permute-start
  474.6 21.8 %reduce-scatter.4.cloned.1.call-done = bf16[32,3072]{1,0:T(8,128)(2,1)} async-done(((bf16[256,3072]{1,0:T(8,128)(2,1)}), bf16[32,3072]{1,0:T(8,128)(2,1)}) %reduce-scatter.4.cloned.1.call-update) | async-done | bytes 196624 | tf_op jit(solution)/shard_map/reduce_scatter | solution.py:245
  496.4 1.7 fusion.71
  (142 shorter events, 19.3 us)
Async XLA Ops:
  7.2 380.7 %copy-start = (bf16[384,3072]{1,0:T(8,128)(2,1)S(1)}, bf16[384,3072]{1,0:T(8,128)(2,1)}, u32[]{:S(2)}) copy-start(bf16[384,3072]{1,0:T(8,128)(2,1)} %param.38) | copy-start | bytes 7077892
  7.2 46.8 %all-gather.18.cloned.1.call-start = ((), (), s32[]{:S(2)}) async-start(), calls=%async_computation.10 | async-start | bytes 1769472 | tf_op jit(solution)/shard_map/all_gather | solution.py:190
  7.9 59.6 %all-gather.20.cloned.1.call-start = ((), (), s32[]{:S(2)}) async-start(), calls=%async_computation.11 | async-start | bytes 3538944 | tf_op jit(solution)/shard_map/all_gather | solution.py:191
  8.7 151.2 %all-gather.10.cloned.1.call-start = ((), (), s32[]{:S(2)}) async-start(), calls=%async_computation.3 | async-start | bytes 1671168 | tf_op jit(solution)/shard_map/all_gather | solution.py:215
  23.9 4.3 copy-start.27
  23.9 4.3 copy-start.22
  23.9 4.4 copy-start.23
  28.3 4.9 copy-start.15
  33.2 18.8 %copy-start.18 = (f32[1,3,3072]{2,1,0:T(4,128)S(1)}, f32[1,3,3072]{2,1,0:T(4,128)}, u32[]{:S(2)}) copy-start(f32[1,3,3072]{2,1,0:T(4,128)} %copy.82) | copy-start | bytes 110596
  67.5 3.3 copy-start.2
  67.5 3.8 copy-start.3
  73.8 4.8 copy-start.11
  73.8 4.8 copy-start.13
  78.6 4.6 copy-start.6
  78.6 2.7 copy-start.25
  81.3 1.9 copy-start.4
  81.3 2.5 copy-start.10
  83.8 2.8 copy-start.26
  86.5 2.4 copy-start.5
  114.2 0.8 copy-start.8
  114.2 16.2 %copy-start.9 = (bf16[896,3,128]{0,2,1:T(8,128)(2,1)}, bf16[896,3,128]{0,2,1:T(8,128)(2,1)S(1)}, u32[]{:S(2)}) copy-start(bf16[896,3,128]{0,2,1:T(8,128)(2,1)S(1)} %get-tuple-element.167) | copy-start | bytes 2064388
  115.8 89.7 %all-gather.12.cloned.1.call-start = ((), (), s32[]{:S(2)}) async-start(), calls=%async_computation.4 | async-start | bytes 1671168 | tf_op jit(solution)/shard_map/all_gather | solution.py:216
  120.1 9.2 %copy-start.28 = (s32[128]{0:T(128)S(1)}, s32[128]{0:T(128)}, u32[]{:S(2)}) copy-start(s32[128]{0:T(128)} %param.30) | copy-start | bytes 1540
  126.5 0.9 copy-start.14
  128.0 155.4 %all-gather.16.cloned.1.call-start = ((), (), s32[]{:S(2)}) async-start(), calls=%async_computation.6 | async-start | bytes 10027008 | tf_op jit(solution)/shard_map/all_gather | solution.py:233
  128.6 232.1 %all-gather.14.cloned.1.call-start = ((), (), s32[]{:S(2)}) async-start(), calls=%async_computation.5 | async-start | bytes 10027008 | tf_op jit(solution)/shard_map/all_gather | solution.py:227
  129.1 296.4 %reduce-scatter.8.cloned.1.call-start = ((), (), s32[]{:S(2)}) async-start(), calls=%async_computation.9 | async-start | bytes 884736 | tf_op jit(solution)/shard_map/reduce_scatter | solution.py:251
  393.7 2.4 copy-start.1
  397.1 65.2 %reduce-scatter.6.cloned.1.call-start = ((), (), s32[]{:S(2)}) async-start(), calls=%async_computation.8 | async-start | bytes 3538944 | tf_op jit(solution)/shard_map/reduce_scatter | solution.py:248
  401.0 3.0 copy-start.19
  401.0 5.5 %copy-start.29 = (s32[128]{0:T(128)S(1)}, s32[128]{0:T(128)}, u32[]{:S(2)}) copy-start(s32[128]{0:T(128)} %param.30) | copy-start | bytes 1540
  401.0 6.7 %copy-start.24 = (f32[9,64]{1,0:T(8,128)S(1)}, f32[9,64]{1,0:T(8,128)}, u32[]{:S(2)}) copy-start(f32[9,64]{1,0:T(8,128)} %param.42) | copy-start | bytes 6916
  401.0 24.5 %copy-start.16 = (bf16[1,16,3072]{2,1,0:T(8,128)(2,1)S(1)}, bf16[1,16,3072]{2,1,0:T(8,128)(2,1)}, u32[]{:S(2)}) copy-start(bf16[1,16,3072]{2,1,0:T(8,128)(2,1)} %param.26) | copy-start | bytes 294916
  401.0 24.5 %copy-start.20 = (f32[1,3072]{1,0:T(1,128)S(1)}, f32[1,3072]{1,0:T(1,128)}, u32[]{:S(2)}) copy-start(f32[1,3072]{1,0:T(1,128)} %get-tuple-element.172) | copy-start | bytes 36868
  401.0 61.3 %copy-start.7 = (bf16[1,64,3072]{2,1,0:T(8,128)(2,1)S(1)}, bf16[1,64,3072]{2,1,0:T(8,128)(2,1)}, u32[]{:S(2)}) copy-start(bf16[1,64,3072]{2,1,0:T(8,128)(2,1)} %param.25) | copy-start | bytes 1179652
  401.0 61.2 %copy-start.17 = (f32[1,3072]{1,0:T(1,128)S(1)}, f32[1,3072]{1,0:T(1,128)}, u32[]{:S(2)}) copy-start(f32[1,3072]{1,0:T(1,128)} %get-tuple-element.175) | copy-start | bytes 36868
  401.1 95.4 %reduce-scatter.4.cloned.1.call-start = ((), (), s32[]{:S(2)}) async-start(), calls=%async_computation.7 | async-start | bytes 1769472 | tf_op jit(solution)/shard_map/reduce_scatter | solution.py:245
  403.9 92.5 %copy-start.12 = (bf16[1,32,3072]{2,1,0:T(8,128)(2,1)S(1)}, bf16[1,32,3072]{2,1,0:T(8,128)(2,1)}, u32[]{:S(2)}) copy-start(bf16[1,32,3072]{2,1,0:T(8,128)(2,1)} %param.24) | copy-start | bytes 589828
  463.5 36.7 %copy-start.21 = (f32[1,2,2048]{2,1,0:T(2,128)S(1)}, f32[1,2,2048]{2,1,0:T(2,128)}, u32[]{:S(2)}) copy-start(f32[1,2,2048]{2,1,0:T(2,128)} %param.43) | copy-start | bytes 49156
  467.2 30.9 %collective-permute-start.1 = (f32[1,2048]{1,0:T(1,128)S(1)}, f32[1,2048]{1,0:T(1,128)S(1)}, u32[]{:S(2)}, u32[]{:S(2)}) collective-permute-start(f32[1,2048]{1,0:T(1,128)S(1)} %slice.221), channel_id=1, source_target_pairs={{1,0},{2,1},{3,2},{4,3},{5,4},{6,5},{7,6},{9,8},{10,9},{11,10},{12... | collective-permute-start | bytes 24584 | tf_op jit(solution)/shard_map/ppermute | solution.py:25
  472.7 26.6 %collective-permute-start = (f32[1,2048]{1,0:T(1,128)S(1)}, f32[1,2048]{1,0:T(1,128)S(1)}, u32[]{:S(2)}, u32[]{:S(2)}) collective-permute-start(f32[1,2048]{1,0:T(1,128)S(1)} %slice.219), channel_id=1, source_target_pairs={{0,1},{1,2},{2,3},{3,4},{4,5},{5,6},{6,7},{8,9},{9,10},{10,11},{11... | collective-permute-start | bytes 24584 | tf_op jit(solution)/shard_map/ppermute | solution.py:23
Sparse Core Ops, SparseCore 0:
  9.7 28.0 all-gather.17
  39.5 27.9 all-gather.19
  115.9 43.9 all-gather.9
  161.8 43.6 all-gather.11
  207.5 75.8 all-gather.15
  285.4 75.2 all-gather.13
  397.2 28.2 reduce-scatter.7
  428.0 34.1 reduce-scatter.5
  464.8 31.5 reduce-scatter.3
where the time goes:
time: 511 us; the launch traced here: 507 us
  waiting for transfers between devices  292 us (57%)
  matrix products  69.9 us (14%)
  local copies, waits for them, and re-layouts  68.9 us (13%)
  other arithmetic  38.1 us (7%)
  between operations  16 us (3%)
  blocking collectives  15.1 us (3%)
  starting transfers between devices  7.7 us (2%)
    all_gather x1, waiting for transfers between devices, per_device(): lax.all_gather(mlp_in_weight, 'wide', axis=0, tiled=True)  77.3 us
    all_gather x1, waiting for transfers between devices, per_device(): lax.all_gather(mlp_out_weight, 'wide', axis=1, tiled=True)  62.4 us
    all_gather x1, waiting for transfers between devices, per_device(): lax.all_gather(value_rows[request_count:], 'wide', axis=0, tiled=True)  45.6 us
    reduce_scatter x1, waiting for transfers between devices, per_device(): lax.psum_scatter(image_part.astype(jnp.bfloat16), 'narrow', scatter_dimen...  35.2 us
    dot_general x1, matrix products, per_device(): jnp.dot(mlp_act, lax.all_gather(mlp_out_weight, 'wide', axis=1, tiled=Tru...  27.2 us
    concatenate x2, local copies, waits for them, and re-layouts, rotate(): partner = jnp.concatenate(pieces, axis=-1)  21.9 us
    reduce_scatter x1, waiting for transfers between devices, per_device(): lax.psum_scatter(text_part.astype(jnp.bfloat16), 'narrow', scatter_dimens...  21.8 us
    dot_general x4, local copies, waits for them, and re-layouts, project_heads(): jnp.dot(modulated, qkv_parts[which], preferred_element_type=jnp.float32)  19.2 us
  transfers between devices with their start and end apart: 11, of which 8 were waited for; matrix products, arithmetic and copies ran while one was open for 18% of the time, Pallas kernels for 0%

commit v1 on v0

v1 whole, which is shorter than its diff:
```python
import functools
import math

import jax
import jax.numpy as jnp
from jax import lax
from jax.experimental import pallas as pl
from jax.experimental.pallas import tpu as pltpu
from jax.sharding import PartitionSpec as P

STEPS = 4
EPSILON = 1e-06
ROPE_BASE = 10000.0
MIB = 1 << 20
F32 = jnp.float32
BF16 = jnp.bfloat16
NT = (((1,), (1,)), ((), ()))

VMEM = pl.BlockSpec(memory_space=pltpu.VMEM)
SMEM = pl.BlockSpec(memory_space=pltpu.SMEM)
ANY = pl.BlockSpec(memory_space=pl.ANY)


def section_widths(head_dim):
    return (head_dim // 8, 7 * head_dim // 16, 7 * head_dim // 16)


def layer_norm(values):
    centre = jnp.mean(values, axis=-1, keepdims=True)
    centred = values - centre
    spread = jnp.mean(centred * centred, axis=-1, keepdims=True)
    return centred * lax.rsqrt(spread + EPSILON)


def cost(flops, moved, exps=0):
    return pl.CostEstimate(flops=int(flops), bytes_accessed=int(moved), transcendentals=int(exps))


def wide_shift(dz, dy):
    return [(z * 4 + y, ((z + dz) % 4) * 4 + (y + dy) % 4) for z in range(4) for y in range(4)]


def chip_shift(step):
    return [(x * 2 + c, ((x + step) % 4) * 2 + c) for x in range(4) for c in range(2)]


CORE_SWAP = [(i, i ^ 1) for i in range(8)]
RING_ORDER = (0, -1, 1, 2)


def ring(block, shift, first, last):
    before = lax.ppermute(block, "wide", shift(1))
    after = lax.ppermute(block, "wide", shift(-1))
    far_first = lax.ppermute(first(before), "wide", shift(1))
    far_last = lax.ppermute(last(after), "wide", shift(-1))
    return before, after, far_first, far_last


def along_y(step):
    return wide_shift(0, step)


def along_z(step):
    return wide_shift(step, 0)


def collect(block, shift_one, shift_two):
    half = block.shape[0] // 2
    before, after, far_first, far_last = ring(
        block, shift_one, lambda b: b[:half], lambda b: b[half:]
    )
    quad = jnp.concatenate([block, before, after, far_first, far_last], axis=0)
    two = 2 * block.shape[0]
    return (quad,) + ring(quad, shift_two, lambda b: b[:two], lambda b: b[two:])


def gather_rows(own):
    half = own.shape[0] // 2
    swap = functools.partial(lax.ppermute, axis_name="narrow", perm=CORE_SWAP)
    nxt = lax.ppermute(own, "narrow", chip_shift(-1))
    prv = lax.ppermute(own, "narrow", chip_shift(1))
    far_a = lax.ppermute(nxt[:half], "narrow", chip_shift(-1))
    far_b = lax.ppermute(prv[half:], "narrow", chip_shift(1))
    return jnp.concatenate(
        [own, nxt, far_a, far_b, prv, swap(own), swap(nxt), swap(far_a), swap(far_b), swap(prv)], axis=0
    )


def scatter_sum(partial):
    rows, columns = partial.shape[0] // 8, partial.shape[1]
    half = columns // 2
    other = lax.ppermute(partial[4 * rows :], "narrow", CORE_SWAP).astype(F32)
    pair = partial[: 4 * rows].astype(F32) + other
    far = pair[2 * rows : 3 * rows].astype(BF16)
    from_prv = lax.ppermute(far[:, :half], "narrow", chip_shift(1)).astype(F32)
    from_nxt = lax.ppermute(far[:, half:], "narrow", chip_shift(-1)).astype(F32)
    to_nxt = pair[rows : 2 * rows]
    to_prv = pair[3 * rows :]
    to_nxt = jnp.concatenate([to_nxt[:, :half] + from_prv, to_nxt[:, half:]], axis=1).astype(BF16)
    to_prv = jnp.concatenate([to_prv[:, :half], to_prv[:, half:] + from_nxt], axis=1).astype(BF16)
    one = lax.ppermute(to_nxt, "narrow", chip_shift(1))
    two = lax.ppermute(to_prv, "narrow", chip_shift(-1))
    return pair[:rows], one, two


def modulate_kernel(steps, text, image, extra, mod_table, out):
    here, there = steps[0], steps[1]
    shift, scale = mod_table[here, 0:1, :], mod_table[here, 1:2, :]
    row = 0
    for ref in (text, image):
        rows = ref.shape[0]
        out[row : row + rows, :] = (layer_norm(ref[...].astype(F32)) * (1.0 + scale) + shift).astype(BF16)
        row += rows
    shift, scale = mod_table[there, 0:1, :], mod_table[there, 1:2, :]
    rows = extra.shape[0]
    out[row : row + rows, :] = (layer_norm(extra[...].astype(F32)) * (1.0 + scale) + shift).astype(BF16)


def modulate(steps, text, image, extra, mod_table):
    rows = text.shape[0] + image.shape[0] + extra.shape[0]
    return pl.pallas_call(
        modulate_kernel,
        out_shape=jax.ShapeDtypeStruct((rows, text.shape[1]), BF16),
        in_specs=[SMEM, VMEM, VMEM, VMEM, VMEM],
        out_specs=VMEM,
        compiler_params=pltpu.CompilerParams(vmem_limit_bytes=8 * MIB),
        cost_estimate=cost(1e6, 2 * MIB),
    )(steps, text, image, extra, mod_table)


def partner_of(values):
    lane = lax.broadcasted_iota(jnp.int32, values.shape, 1)
    width = values.shape[1]
    result = None
    offset = 0
    rolled = {}
    for section in section_widths(width):
        half = section // 2
        for amount, start in ((width - half, offset), (half, offset + half)):
            if amount not in rolled:
                rolled[amount] = pltpu.roll(values, amount, 1)
            result = rolled[amount] if result is None else jnp.where(lane >= start, rolled[amount], result)
        offset += section
    return result


def heads_kernel(blocks, own, x, weight, gains, cosine, sine, request, extra):
    which = pl.program_id(0)
    total = x.shape[0]
    rows = total // blocks
    taken = rows - own
    step = 2 * rows
    heads = weight.shape[2] // 128

    def tile(index, carry):
        start = pl.multiple_of(index * step, 32)
        acc = jnp.dot(x[pl.ds(start, step), :], weight[0], preferred_element_type=F32)

        def put(head, values):
            for part in range(2):
                first = part * rows
                block = 2 * index + part
                request[0, head, pl.ds(pl.multiple_of(block * taken, 32), taken), :] = values[first : first + taken]
                extra[0, head, pl.ds(pl.multiple_of(block * own, 16), own), :] = values[first + taken : first + rows]

        @pl.when(which < 2)
        def _():
            gain = gains[pl.ds(which, 1), :]
            cos = cosine[pl.ds(start, step), :]
            sin = sine[pl.ds(start, step), :]
            for head in range(heads):
                part = acc[:, head * 128 : (head + 1) * 128]
                square = jnp.mean(part * part, axis=1, keepdims=True)
                part = part * lax.rsqrt(square + EPSILON) * gain
                put(head, (part * cos + partner_of(part) * sin).astype(BF16))

        @pl.when(which == 2)
        def _():
            for head in range(heads):
                put(head, acc[:, head * 128 : (head + 1) * 128].astype(BF16))

        return carry

    lax.fori_loop(0, total // step, tile, 0)


def project_heads(x, weight, gains, cosine, sine, blocks, own):
    total, width = x.shape
    heads = weight.shape[2] // 128
    extra = blocks * own
    request = total - extra
    return pl.pallas_call(
        functools.partial(heads_kernel, blocks, own),
        grid=(3,),
        out_shape=(
            jax.ShapeDtypeStruct((3, heads, request, 128), BF16),
            jax.ShapeDtypeStruct((3, heads, extra, 128), BF16),
        ),
        in_specs=[
            VMEM,
            pl.BlockSpec((1, width, weight.shape[2]), lambda i: (i, 0, 0)),
            VMEM,
            VMEM,
            VMEM,
        ],
        out_specs=(
            pl.BlockSpec((1, heads, request, 128), lambda i: (i, 0, 0, 0)),
            pl.BlockSpec((1, heads, extra, 128), lambda i: (i, 0, 0, 0)),
        ),
        compiler_params=pltpu.CompilerParams(vmem_limit_bytes=28 * MIB),
        cost_estimate=cost(6 * total * width * weight.shape[2], 16 * MIB),
    )(x, weight, gains, cosine, sine)


def weigh(query, keys, values, live):
    scores = lax.dot_general(query, keys, NT, preferred_element_type=F32)
    weights = jnp.exp(scores * (1.0 / math.sqrt(query.shape[1])))
    if live is not None:
        weights = jnp.where(live, weights, 0.0)
    running = jnp.sum(weights, axis=1, keepdims=True)
    total = jnp.dot(weights.astype(BF16), values, preferred_element_type=F32)
    return (total / running).astype(BF16)


def request_kernel(query, keys, values, out):
    step = 256
    for start in range(0, query.shape[2], step):
        out[start : start + step, :] = weigh(query[0, 0, start : start + step, :], keys[0, 0], values[0, 0], None)


def attend_request(heads):
    count, rows = heads.shape[1], heads.shape[2]

    def block(which):
        return pl.BlockSpec((1, 1, rows, 128), lambda h: (which, h, 0, 0))

    return pl.pallas_call(
        request_kernel,
        grid=(count,),
        out_shape=jax.ShapeDtypeStruct((rows, count * 128), BF16),
        in_specs=[block(0), block(1), block(2)],
        out_specs=pl.BlockSpec((rows, 128), lambda h: (0, h)),
        compiler_params=pltpu.CompilerParams(vmem_limit_bytes=16 * MIB),
        cost_estimate=cost(4 * count * rows * rows * 128, 5 * MIB, count * rows * rows),
    )(heads, heads, heads)


def extra_kernel(blocks, query, live, done, *refs):
    keys, values, out = refs[:5], refs[5:10], refs[10]
    every_key = jnp.concatenate([ref[i, 0] for ref in keys for i in range(ref.shape[0])], axis=0)
    every_value = jnp.concatenate([ref[i, 0] for ref in values for i in range(ref.shape[0])], axis=0)
    attended = weigh(query[0, 0], every_key, every_value, live[...] > 0)
    taken, own = done.shape[0] // blocks, attended.shape[0] // blocks
    rows = taken + own
    for block in range(blocks):
        out[block * rows : block * rows + taken, :] = done[block * taken : (block + 1) * taken, :]
        out[block * rows + taken : (block + 1) * rows, :] = attended[block * own : (block + 1) * own, :]


def attend_extra(heads, live, done, pieces, blocks):
    count, rows = heads.shape[1], heads.shape[2]

    def pair(first):
        return [
            pl.BlockSpec((piece.shape[0], 1, rows, 128), lambda h: (0, first + h, 0, 0)) for piece in pieces
        ]

    total = done.shape[0] + rows
    return pl.pallas_call(
        functools.partial(extra_kernel, blocks),
        grid=(count,),
        out_shape=jax.ShapeDtypeStruct((total, count * 128), BF16),
        in_specs=[
            pl.BlockSpec((1, 1, rows, 128), lambda h: (0, h, 0, 0)),
            pl.BlockSpec(live.shape, lambda h: (0, 0)),
            pl.BlockSpec((done.shape[0], 128), lambda h: (0, h)),
        ]
        + pair(0)
        + pair(count),
        out_specs=pl.BlockSpec((total, 128), lambda h: (0, h)),
        compiler_params=pltpu.CompilerParams(vmem_limit_bytes=16 * MIB),
        cost_estimate=cost(4 * count * rows * live.shape[1] * 128, 5 * MIB, count * rows * live.shape[1]),
    )(heads, live, done, *pieces, *pieces)


def gelu(values):
    inner = math.sqrt(2.0 / math.pi) * (values + 0.044715 * (values * values * values))
    return values * (0.5 * (1.0 + jnp.tanh(inner)))


def hidden_kernel(place, x, *refs):
    pieces, out, weight, done = refs[:10], refs[10], refs[11], refs[12]
    z, y = place[0], place[1]
    half = weight.shape[0] // 32
    copies = []

    def fetch(ref, index, dz, dy, part):
        group = lax.rem(z + dz + 4, 4) * 4 + lax.rem(y + dy + 4, 4)
        start = pl.multiple_of(group * (2 * half) + part * half, 32)
        copy = pltpu.make_async_copy(
            ref.at[pl.ds(index * half, half), :], weight.at[pl.ds(start, half), :], done.at[len(copies)]
        )
        copy.start()
        copies.append(copy)

    for part in range(2):
        quad, before, after, far_first, far_last = pieces[5 * part : 5 * part + 5]
        for outer, ref, span, base in (
            (0, quad, range(4), 0),
            (-1, before, range(4), 0),
            (1, after, range(4), 0),
            (2, far_first, range(2), 0),
            (2, far_last, range(2, 4), 2),
        ):
            for index in span:
                inner = RING_ORDER[index]
                dz, dy = (outer, inner) if part == 0 else (inner, outer)
                fetch(ref, index - base, dz, dy, part)
    for copy in copies:
        copy.wait()
    step = 256

    def tile(index, carry):
        columns = pl.ds(pl.multiple_of(index * step, step), step)
        acc = jnp.dot(x[...], weight[:, columns], preferred_element_type=F32)
        out[:, columns] = gelu(acc).astype(BF16)
        return carry

    lax.fori_loop(0, out.shape[1] // step, tile, 0)


def hidden_units(place, x, pieces):
    rows, width = x.shape
    units = pieces[0].shape[1]
    return pl.pallas_call(
        hidden_kernel,
        out_shape=jax.ShapeDtypeStruct((rows, units), BF16),
        in_specs=[SMEM, VMEM] + [ANY] * 10,
        out_specs=VMEM,
        scratch_shapes=[pltpu.VMEM((width, units), BF16), pltpu.SemaphoreType.DMA((32,))],
        compiler_params=pltpu.CompilerParams(vmem_limit_bytes=26 * MIB),
        cost_estimate=cost(2 * rows * width * units, 18 * MIB, rows * units),
    )(place, x, *pieces)


def output_kernel(act, weight, attended, attn_weight, out):
    acc = lax.dot_general(act[...], weight[...], NT, preferred_element_type=F32)
    acc = acc + jnp.dot(attended[...], attn_weight[...], preferred_element_type=F32)
    out[...] = acc.astype(BF16)


def output_part(act, weight, attended, attn_weight, first, columns, step=256):
    rows, units = act.shape
    base = first // step
    return pl.pallas_call(
        output_kernel,
        grid=(columns // step,),
        out_shape=jax.ShapeDtypeStruct((rows, columns), BF16),
        in_specs=[
            pl.BlockSpec((rows, units), lambda i: (0, 0)),
            pl.BlockSpec((step, units), lambda i: (base + i, 0)),
            pl.BlockSpec((rows, attended.shape[1]), lambda i: (0, 0)),
            pl.BlockSpec((attn_weight.shape[0], step), lambda i: (0, base + i)),
        ],
        out_specs=pl.BlockSpec((rows, step), lambda i: (0, i)),
        compiler_params=pltpu.CompilerParams(vmem_limit_bytes=20 * MIB),
        cost_estimate=cost(2 * rows * columns * (units + attended.shape[1]), 8 * MIB),
    )(act, weight, attended, attn_weight)


def finish_kernel(chunks, scalars, text, image, extra, mod_table, final_table, proj, *refs):
    sums, (text_out, image_out, extra_out, velocity, hidden) = refs[: 3 * chunks], refs[3 * chunks :]
    here, there, count = scalars[0], scalars[1], scalars[2]
    width = text.shape[1] // chunks
    rows_text, rows_image = text.shape[0], image.shape[0]
    for chunk in range(chunks):
        own, one, two = sums[3 * chunk : 3 * chunk + 3]
        total = own[...] + one[...].astype(F32) + two[...].astype(F32)
        columns = slice(chunk * width, (chunk + 1) * width)
        gate = mod_table[here, 2:3, columns]
        text_out[:, columns] = (text[:, columns].astype(F32) + gate * total[:rows_text]).astype(BF16)
        states = image[:, columns].astype(F32) + gate * total[rows_text : rows_text + rows_image]
        hidden[:, columns] = states
        image_out[:, columns] = states.astype(BF16)
        gate = mod_table[there, 2:3, columns]
        slots = extra[:, columns].astype(F32) + gate * total[rows_text + rows_image :]
        live = lax.broadcasted_iota(jnp.int32, slots.shape, 0) < count
        extra_out[:, columns] = jnp.where(live, slots, 0.0).astype(BF16)
    shift, scale = final_table[here, 0:1, :], final_table[here, 1:2, :]
    normed = (layer_norm(hidden[...]) * (1.0 + scale) + shift).astype(BF16)
    velocity[...] = lax.dot_general(normed, proj[...], NT, preferred_element_type=F32)


def finish(scalars, text, image, extra, mod_table, final_table, proj, sums):
    width = text.shape[1]
    flat = [part for chunk in sums for part in chunk]
    return pl.pallas_call(
        functools.partial(finish_kernel, len(sums)),
        out_shape=(
            jax.ShapeDtypeStruct(text.shape, BF16),
            jax.ShapeDtypeStruct(image.shape, BF16),
            jax.ShapeDtypeStruct(extra.shape, BF16),
            jax.ShapeDtypeStruct((image.shape[0], proj.shape[0]), F32),
        ),
        in_specs=[SMEM] + [VMEM] * (6 + len(flat)),
        out_specs=(VMEM,) * 4,
        scratch_shapes=[pltpu.VMEM((image.shape[0], width), F32)],
        compiler_params=pltpu.CompilerParams(vmem_limit_bytes=16 * MIB),
        cost_estimate=cost(1e7, 5 * MIB),
    )(scalars, text, image, extra, mod_table, final_table, proj, *flat)


def smooth_kernel(columns, delta, above, middle, below, stencil, latent, out):
    rows = middle.shape[0]
    cells = jnp.concatenate([above[...], middle[...], below[...]], axis=0)
    column = lax.rem(lax.broadcasted_iota(jnp.int32, middle.shape, 0), columns)
    total = jnp.zeros(middle.shape, F32)
    for row_tap in range(3):
        band = cells[row_tap * columns : row_tap * columns + rows]
        for col_tap in range(3):
            moved = band if col_tap == 1 else pltpu.roll(band, (1 - col_tap) % rows, 0)
            place = column + (col_tap - 1)
            moved = jnp.where((place >= 0) & (place < columns), moved, 0.0)
            tap = 3 * row_tap + col_tap
            total = total + stencil[tap : tap + 1, :] * moved
    out[...] = latent[...] + delta[0] * total


def smooth(delta, above, middle, below, stencil, latent, columns):
    return pl.pallas_call(
        functools.partial(smooth_kernel, columns),
        out_shape=jax.ShapeDtypeStruct(middle.shape, F32),
        in_specs=[SMEM] + [VMEM] * 5,
        out_specs=VMEM,
        cost_estimate=cost(1e5, 1e5),
    )(delta, above, middle, below, stencil, latent)


def rope_tables(positions, head_dim):
    angle_list, signs = [], []
    for axis_id, section in enumerate(section_widths(head_dim)):
        half_width = section // 2
        exponent = -2.0 * jnp.arange(half_width, dtype=F32) / section
        frequency = jnp.power(F32(ROPE_BASE), exponent)
        angles = positions[axis_id].astype(F32)[:, None] * frequency[None, :]
        angle_list += [angles, angles]
        signs += [-1.0] * half_width + [1.0] * half_width
    angles = jnp.concatenate(angle_list, axis=1)
    return jnp.cos(angles), jnp.sin(angles) * jnp.array(signs, F32)[None, :]


def noise_level(step_value):
    level = 1.0 - step_value.astype(F32) / STEPS
    return 3.0 * level / (1.0 + 2.0 * level)


def per_device(
    text_tokens,
    image_tokens,
    extra_tokens,
    text_pos,
    image_pos,
    extra_pos,
    extra_counts,
    request_group,
    step_index,
    mod_table,
    final_table,
    qkv_weight,
    q_scale,
    k_scale,
    attn_out_weight,
    mlp_in_weight,
    mlp_out_weight,
    proj_weight,
    stencil,
    latent,
):
    group = lax.axis_index("wide")
    member = lax.axis_index("narrow")
    z, y = group // 4, group % 4
    chip, core = member // 2, member % 2
    step_here = step_index[request_group[group]]
    step_extra = step_index[step_index.shape[0] - 1]
    own_count = extra_counts[group * 8 + member]
    scalars = jnp.stack([step_here, step_extra, own_count]).astype(jnp.int32)
    text_own, image_own, extra_own = text_tokens[0], image_tokens[0], extra_tokens[0]

    out_weight = lax.all_gather(mlp_out_weight.T, "wide", axis=0, tiled=True)
    own = modulate(scalars, text_own, image_own, extra_own, mod_table)
    x = gather_rows(own)
    half = mlp_in_weight.shape[0] // 2
    pieces = collect(mlp_in_weight[:half], along_y, along_z) + collect(mlp_in_weight[half:], along_z, along_y)

    block_ids = jnp.arange(8, dtype=jnp.int32)
    sources = ((chip + block_ids % 4) % 4) * 2 + (core ^ (block_ids // 4))

    def by_block(array):
        chosen = (sources[:, None] == block_ids[None, :])[None, :, :, None]
        return jnp.sum(jnp.where(chosen, array[:, 0].reshape(3, 1, 8, -1), 0), axis=2)

    positions = jnp.concatenate([by_block(text_pos), by_block(image_pos), by_block(extra_pos)], axis=2)
    cosine, sine = rope_tables(positions.reshape(3, -1), 128)
    request_heads, extra_heads = project_heads(
        x, qkv_weight, jnp.stack([q_scale, k_scale]), cosine, sine, 8, extra_own.shape[0]
    )

    heads, slots = extra_heads.shape[1], extra_heads.shape[2]
    shared = extra_heads[1:].reshape(1, 2 * heads, slots, 128)
    before, after, far_first, far_last = ring(shared, along_y, lambda b: b[:, :heads], lambda b: b[:, heads:])
    far = jnp.concatenate([far_first, far_last], axis=1)
    quad = jnp.concatenate([shared, before, after, far], axis=0)
    key_pieces = (quad,) + ring(quad, along_z, lambda b: b[:2], lambda b: b[2:])
    attended = attend_request(request_heads)
    order = jnp.array(RING_ORDER, jnp.int32)
    groups = ((z + order) % 4)[:, None] * 4 + ((y + order) % 4)[None, :]
    owners = groups.reshape(16, 1) * 8 + sources[None, :]
    device_ids = jnp.arange(extra_counts.shape[0], dtype=jnp.int32)
    chosen = owners.reshape(-1)[:, None] == device_ids[None, :]
    counts = jnp.sum(jnp.where(chosen, extra_counts[None, :], 0), axis=1)
    slot_ids = jnp.arange(extra_own.shape[0], dtype=jnp.int32)
    live = (slot_ids[None, :] < counts[:, None]).astype(F32).reshape(1, -1)
    attended = attend_extra(extra_heads, live, attended, key_pieces, 8)

    act = hidden_units(jnp.stack([z, y]).astype(jnp.int32), x, pieces)
    chunks = 3
    columns = out_weight.shape[0] // chunks
    sums = []
    for chunk in range(chunks):
        part = output_part(act, out_weight, attended, attn_out_weight, chunk * columns, columns)
        sums.append(scatter_sum(part))
    text_out, image_out, extra_out, velocity = finish(
        scalars, text_own, image_own, extra_own, mod_table, final_table, proj_weight.T, sums
    )
    channels = proj_weight.shape[1]
    grid_width = latent.shape[2] // channels
    above = lax.ppermute(velocity[-grid_width:], "narrow", [(i, i + 1) for i in range(7)])
    below = lax.ppermute(velocity[:grid_width], "narrow", [(i + 1, i) for i in range(7)])
    delta = (noise_level(step_here + 1) - noise_level(step_here)).reshape(1)
    latent_next = smooth(
        delta, above, velocity, below, stencil, latent[0].reshape(-1, channels), grid_width
    )
    return (text_out[None], image_out[None], extra_out[None], latent_next.reshape(latent.shape))


def solution(mesh):
    return jax.shard_map(
        per_device,
        mesh=mesh,
        in_specs=(
            P("wide", "narrow", None),
            P("wide", "narrow", None),
            P("wide", "narrow", None),
            P(None, "wide", None),
            P(None, "wide", None),
            P(None, "wide", None),
            P(),
            P(),
            P(),
            P(),
            P(),
            P(None, None, "narrow"),
            P(),
            P(),
            P("narrow", None),
            P("wide", "narrow"),
            P("narrow", "wide"),
            P(),
            P(),
            P("wide", "narrow", None),
        ),
        out_specs=(
            P("wide", "narrow", None),
            P("wide", "narrow", None),
            P("wide", "narrow", None),
            P("wide", "narrow", None),
        ),
        check_vma=False,
    )
```

time: 511 us -> 283 us (0.55)
  waiting for transfers between devices: 292 us -> 93.9 us
  matrix products: 69.9 us -> 0 us
  starting transfers between devices: 7.7 us -> 64.8 us
  Pallas kernels: 0 us -> 56.5 us
  other arithmetic: 38.1 us -> 6.72 us
  local copies, waits for them, and re-layouts: 68.9 us -> 41.1 us
  blocking collectives: 15.1 us -> 0 us
    all_gather x6 -> x1, waiting for transfers between devices: 214 us -> 0.02 us  [per_device(): out_weight = lax.all_gather(mlp_out_weight.T, 'wide', axis=0, tiled=True)]
    ppermute x2 -> x50, waiting for transfers between devices: 0.01 us -> 93.2 us  [the longest x6 42.7 us: ring(): far_first = lax.ppermute(first(before), 'wide', shift(1))]
    reduce_scatter x3 -> x0, waiting for transfers between devices: 74.7 us -> none  [the longest x1 35.2 us: per_device(): lax.psum_scatter(image_part.astype(jnp.bfloat16), 'narrow', scatter_dimen...]
    dot_general x21 -> x0, matrix products: 69.9 us -> none  [the longest x1 27.2 us: per_device(): jnp.dot(mlp_act, lax.all_gather(mlp_out_weight, 'wide', axis=1, tiled=Tru...]
    ppermute x2 -> x50, starting transfers between devices: 7.34 us -> 64.8 us  [the longest x6 11.1 us: ring(): after = lax.ppermute(block, 'wide', shift(-1))]
    pallas_call x0 -> x10, Pallas kernels: none -> 56.5 us  [the longest x1 16.8 us: project_heads(): pl.pallas_call(functools.partial(heads_kernel, blocks, own), grid=(3,), o...]
    concatenate x4 -> x3, local copies, waits for them, and re-layouts: 22 us -> 1.4 us  [the longest x2 1.35 us: collect(): quad = jnp.concatenate([block, before, after, far_first, far_last], axis=0)]
    dot_general x7 -> x0, local copies, waits for them, and re-layouts: 19.9 us -> none  [the longest x4 19.2 us: project_heads(): jnp.dot(modulated, qkv_parts[which], preferred_element_type=jnp.float32)]
  transfers between devices with their start and end apart: 11 -> 51, of which waited for: 8 -> 21; matrix products, arithmetic and copies ran while one was open for 18% -> 13% of each run, Pallas kernels for 0% -> 17%
where the time goes in v1:
time: 283 us; the launch traced here: 282 us
  waiting for transfers between devices  93.9 us (33%)
  starting transfers between devices  64.8 us (23%)
  Pallas kernels  56.5 us (20%)
  local copies, waits for them, and re-layouts  41.1 us (15%)
  between operations  18.4 us (7%)
  other arithmetic  6.72 us (2%)
    ppermute x6, waiting for transfers between devices, ring(): far_first = lax.ppermute(first(before), 'wide', shift(1))  42.7 us
    ppermute x6, waiting for transfers between devices, ring(): before = lax.ppermute(block, 'wide', shift(1))  19.3 us
    unnamed x88, local copies, waits for them, and re-layouts  18.7 us
    pallas_call x1, Pallas kernels, project_heads(): pl.pallas_call(functools.partial(heads_kernel, blocks, own), grid=(3,), o...  16.8 us
    pallas_call x1, Pallas kernels, hidden_units(): pl.pallas_call(hidden_kernel, out_shape=jax.ShapeDtypeStruct((rows, units...  14.8 us
    pallas_call x3, Pallas kernels, output_part(): pl.pallas_call(output_kernel, grid=(columns // step,), out_shape=jax.Shap...  14.3 us
    ppermute x6, starting transfers between devices, ring(): after = lax.ppermute(block, 'wide', shift(-1))  11.1 us
    ppermute x6, starting transfers between devices, ring(): far_last = lax.ppermute(last(after), 'wide', shift(-1))  8.65 us
  transfers between devices with their start and end apart: 51, of which 21 were waited for; matrix products, arithmetic and copies ran while one was open for 13% of the time, Pallas kernels for 17%

profile of v1, /device:TPU:1, one launch (start us, length us, event | category | flops | bytes accessed | tf_op | source)
XLA Modules:
  0.0 281.5 jit_solution(9359700574816064225)
XLA Ops:
  7.9 1.2 dynamic_slice.9
  12.2 1.2 dynamic_slice.11
  13.4 1.3 fusion.23
  14.8 2.0 pad_add_fusion.1.steps.scalars
  20.7 3.4 %collective-permute-start = (bf16[112,3072]{1,0:T(8,128)(2,1)S(1)}, bf16[112,3072]{1,0:T(8,128)(2,1)}, u32[]{:S(2)}, u32[]{:S(2)}) collective-permute-start(bf16[112,3072]{1,0:T(8,128)(2,1)S(1)} %shard_map.237), channel_id=1, source_target_pairs={{0,6},{1,7},{2,0},{3,1},{4,2},{5,3},{6,4},{7,5},{8,14},{9,15},{10,... | collective-permute-start | bytes 2064392 | tf_op jit(solution)/shard_map/ppermute | solution.py:80
  26.0 1.3 collective-permute-start.9
  27.3 1.4 collective-permute-start.10
  31.5 1.7 sine_multiply_fusion
  33.2 9.4 %collective-permute-done.9 = bf16[96,1536]{1,0:T(8,128)(2,1)} collective-permute-done((bf16[96,1536]{1,0:T(8,128)(2,1)}, bf16[96,1536]{1,0:T(8,128)(2,1)}, u32[]{:S(2)}, u32[]{:S(2)}) %collective-permute-start.9) | collective-permute-done | bytes 294944 | tf_op jit(solution)/shard_map/ppermute | solution.py:52
  42.6 1.8 collective-permute-start.17
  44.4 1.7 constant_dynamic-update-slice_fusion.13
  46.1 1.7 collective-permute-start.18
  47.8 1.7 constant_dynamic-update-slice_fusion.12
  51.5 1.4 collective-permute-done.17
  53.6 1.3 collective-permute-done.18
  54.9 1.3 collective-permute-start.12
  57.1 5.3 %collective-permute-done.11 = bf16[48,1536]{1,0:T(8,128)(2,1)S(1)} collective-permute-done((bf16[48,1536]{1,0:T(8,128)(2,1)S(1)}, bf16[48,1536]{1,0:T(8,128)(2,1)S(1)}, u32[]{:S(2)}, u32[]{:S(2)}) %collective-permute-start.11) | collective-permute-done | bytes 147488 | tf_op jit(solution)/shard_map/ppermute | solution.py:54
  63.1 3.1 %collective-permute-start.20 = (bf16[48,1536]{1,0:T(8,128)(2,1)S(1)}, bf16[48,1536]{1,0:T(8,128)(2,1)S(1)}, u32[]{:S(2)}, u32[]{:S(2)}) collective-permute-start(bf16[48,1536]{1,0:T(8,128)(2,1)S(1)} %slice.246), channel_id=1, source_target_pairs={{0,96},{8,104},{16,112},{24,120},{32,0},{40,8},{48,16},{56,24},{64... | collective-permute-start | bytes 442376 | tf_op jit(solution)/shard_map/ppermute | solution.py:55
  66.9 5.0 %collective-permute-done.19 = bf16[48,1536]{1,0:T(8,128)(2,1)S(1)} collective-permute-done((bf16[48,1536]{1,0:T(8,128)(2,1)S(1)}, bf16[48,1536]{1,0:T(8,128)(2,1)S(1)}, u32[]{:S(2)}, u32[]{:S(2)}) %collective-permute-start.19) | collective-permute-done | bytes 147488 | tf_op jit(solution)/shard_map/ppermute | solution.py:54
  72.5 2.7 collective-permute-start.14
  76.2 3.2 %collective-permute-start.1 = (bf16[56,3072]{1,0:T(8,128)(2,1)S(1)}, bf16[56,3072]{1,0:T(8,128)(2,1)S(1)}, u32[]{:S(2)}, u32[]{:S(2)}) collective-permute-start(bf16[56,3072]{1,0:T(8,128)(2,1)S(1)} %slice.239), channel_id=1, source_target_pairs={{0,6},{1,7},{2,0},{3,1},{4,2},{5,3},{6,4},{7,5},{8,14},{9,15},{10,... | collective-permute-start | bytes 1032200 | tf_op jit(solution)/shard_map/ppermute | solution.py:82
  79.5 1.2 constant_dynamic-update-slice_fusion.8
  80.6 3.0 %collective-permute-done.1 = bf16[56,3072]{1,0:T(8,128)(2,1)S(1)} collective-permute-done((bf16[56,3072]{1,0:T(8,128)(2,1)S(1)}, bf16[56,3072]{1,0:T(8,128)(2,1)S(1)}, u32[]{:S(2)}, u32[]{:S(2)}) %collective-permute-start.1) | collective-permute-done | bytes 344096 | tf_op jit(solution)/shard_map/ppermute | solution.py:82
  83.7 8.6 %collective-permute-done.3 = bf16[56,3072]{1,0:T(8,128)(2,1)S(1)} collective-permute-done((bf16[56,3072]{1,0:T(8,128)(2,1)S(1)}, bf16[56,3072]{1,0:T(8,128)(2,1)S(1)}, u32[]{:S(2)}, u32[]{:S(2)}) %collective-permute-start.3) | collective-permute-done | bytes 344096 | tf_op jit(solution)/shard_map/ppermute | solution.py:83
  92.3 4.3 %collective-permute-start.5 = (bf16[112,3072]{1,0:T(8,128)(2,1)}, bf16[112,3072]{1,0:T(8,128)(2,1)S(1)}, u32[]{:S(2)}, u32[]{:S(2)}) collective-permute-start(bf16[112,3072]{1,0:T(8,128)(2,1)} %collective-permute-done), channel_id=1, source_target_pairs={{0,1},{1,0},{2,3},{3,2},{4,5},{5,4},{6,7},{7,6},{8,9},{9,8},{10,11... | collective-permute-start | bytes 2064392 | tf_op jit(solution)/shard_map/ppermute | solution.py:85
  99.0 1.2 collective-permute-done.6
  100.7 1.3 collective-permute-done.7
  102.0 16.8 %shard_map.239 = (bf16[3,3,768,128]{3,2,1,0:T(8,128)(2,1)S(1)}, bf16[3,3,128,128]{3,2,1,0:T(8,128)(2,1)S(1)}) custom-call(bf16[896,3072]{1,0:T(8,128)(2,1)S(1)} %constant_dynamic-update-slice_fusion.x, bf16[3,3072,384]{2,1,0:T(8,128)(2,1)S(1)} %bitcast.22, f32[2,128]{1,0:T(2,128)S(1)} %pad_maximum_fusion.6.gains, f32[896,128]{1,0:T(8,128)S(1)} %get-tuple-element.45.cosine, ...), custom_call_target="tpu_custom_call" | custom-call | flops 6341787648 | bytes 16777216 | tf_op jit(solution)/shard_map/pallas_call | solution.py:192
  118.9 2.7 collective-permute-start.26
  122.3 4.0 %collective-permute-done.25 = bf16[1,6,128,128]{3,2,1,0:T(8,128)(2,1)S(1)} collective-permute-done((bf16[1,6,128,128]{3,2,1,0:T(8,128)(2,1)S(1)}, bf16[1,6,128,128]{3,2,1,0:T(8,128)(2,1)S(1)}, u32[]{:S(2)}, u32[]{:S(2)}) %collective-permute-start.25) | collective-permute-done | bytes 196640 | tf_op jit(solution)/shard_map/ppermute | solution.py:52
  126.3 1.5 collective-permute-start.27
  127.8 25.8 %collective-permute-done.27 = bf16[1,3,128,128]{3,2,1,0:T(8,128)(2,1)S(1)} collective-permute-done((bf16[1,3,128,128]{3,2,1,0:T(8,128)(2,1)S(1)}, bf16[1,3,128,128]{3,2,1,0:T(8,128)(2,1)S(1)}, u32[]{:S(2)}, u32[]{:S(2)}) %collective-permute-start.27) | collective-permute-done | bytes 98336 | tf_op jit(solution)/shard_map/ppermute | solution.py:54
  153.6 3.5 %collective-permute-done.28 = bf16[1,3,128,128]{3,2,1,0:T(8,128)(2,1)S(1)} collective-permute-done((bf16[1,3,128,128]{3,2,1,0:T(8,128)(2,1)S(1)}, bf16[1,3,128,128]{3,2,1,0:T(8,128)(2,1)S(1)}, u32[]{:S(2)}, u32[]{:S(2)}) %collective-permute-start.28) | collective-permute-done | bytes 98336 | tf_op jit(solution)/shard_map/ppermute | solution.py:55
  157.3 2.7 collective-permute-start.30
  160.2 1.9 slice.243
  162.1 1.9 slice.244
  164.1 2.7 collective-permute-start.16
  166.7 1.9 slice.247
  168.7 1.9 slice.248
  170.6 4.5 %collective-permute-done.29.refs_1_.refs_6_ = bf16[4,6,128,128]{3,2,1,0:T(8,128)(2,1)S(1)} collective-permute-done((bf16[4,6,128,128]{3,2,1,0:T(8,128)(2,1)S(1)}, bf16[4,6,128,128]{3,2,1,0:T(8,128)(2,1)S(1)}, u32[]{:S(2)}, u32[]{:S(2)}) %collective-permute-start.29) | collective-permute-done | bytes 786464 | tf_op jit(solution)/shard_map/ppermute | solution.py:52
  175.2 1.5 collective-permute-start.24
  177.3 2.8 %shard_map.240.done = bf16[768,384]{1,0:T(8,128)(2,1)S(1)} custom-call(bf16[3,3,768,128]{3,2,1,0:T(8,128)(2,1)S(1)} %get-tuple-element.11.query.keys.values, bf16[3,3,768,128]{3,2,1,0:T(8,128)(2,1)S(1)} %get-tuple-element.11.query.keys.values, bf16[3,3,768,128]{3,2,1,0:T(8,128)(2,1)S(1)} %get-tuple-element.11.query.keys.values), custom_call_target="tpu_custom_call" | custom-call | flops 905969664 | bytes 5242880 | tf_op jit(solution)/shard_map/pallas_call | solution.py:237
  181.3 6.6 %collective-permute-done.15.refs_3_ = bf16[192,1536]{1,0:T(8,128)(2,1)} collective-permute-done((bf16[192,1536]{1,0:T(8,128)(2,1)}, bf16[192,1536]{1,0:T(8,128)(2,1)}, u32[]{:S(2)}, u32[]{:S(2)}) %collective-permute-start.15) | collective-permute-done | bytes 589856 | tf_op jit(solution)/shard_map/ppermute | solution.py:54
  187.9 14.8 %shard_map.238.act = bf16[896,1536]{1,0:T(8,128)(2,1)S(1)} custom-call(s32[2]{0:T(128)S(1)} %pad_add_fusion.2.place, bf16[896,3072]{1,0:T(8,128)(2,1)S(1)} %copy-done.20, bf16[384,1536]{1,0:T(8,128)(2,1)} %constant_dynamic-update-slice_fusion.10.refs_0_, bf16[384,1536]{1,0:T(8,128)(2,1)} %collective-permute-done.13.refs_1_, ...), custom_call_target="tpu_custom_call" | custom-call | flops 8455716864 | bytes 18874368 | tf_op jit(solution)/shard_map/pallas_call | solution.py:335
  202.8 3.3 %shard_map.241.attended = bf16[896,384]{1,0:T(8,128)(2,1)S(1)} custom-call(bf16[3,3,128,128]{3,2,1,0:T(8,128)(2,1)S(1)} %copy-done.11, f32[1,2048]{1,0:T(1,128)S(1)} %reshape.232.live, bf16[768,384]{1,0:T(8,128)(2,1)S(1)} %shard_map.240.done, bf16[4,6,128,128]{3,2,1,0:T(8,128)(2,1)S(1)} %copy-done.3, bf16[4,6,128,128]{3,2,1,0:T(8,128)(2,1)S(1)} %copy-done.5, ...), custom_call_target="tpu_custom_call" | custom-call | flops 402653184 | bytes 5242880 | tf_op jit(solution)/shard_map/pallas_call | solution.py:269
  206.1 3.7 %copy-done = bf16[3072,1536]{1,0:T(8,128)(2,1)S(1)} copy-done((bf16[3072,1536]{1,0:T(8,128)(2,1)S(1)}, bf16[3072,1536]{1,0:T(8,128)(2,1)}, u32[]{:S(2)}) %copy-start) | copy-done | bytes 9437208
  209.7 1.7 copy-done.1
  211.4 4.8 %shard_map.244 = bf16[896,1024]{1,0:T(8,128)(2,1)S(1)} custom-call(bf16[896,1536]{1,0:T(8,128)(2,1)S(1)} %shard_map.238.act, bf16[3072,1536]{1,0:T(8,128)(2,1)S(1)} %copy-done, bf16[896,384]{1,0:T(8,128)(2,1)S(1)} %shard_map.241.attended, bf16[384,3072]{1,0:T(8,128)(2,1)S(1)} %copy-done.1), custom_call_target="tpu_custom_call" | custom-call | flops 3523215360 | bytes 8388608 | tf_op jit(solution)/shard_map/pallas_call | solution.py:355
  216.3 6.5 %collective-permute-start.43 = (bf16[448,1024]{1,0:T(8,128)(2,1)S(1)}, bf16[448,1024]{1,0:T(8,128)(2,1)S(1)}, u32[]{:S(2)}, u32[]{:S(2)}) collective-permute-start(bf16[448,1024]{1,0:T(8,128)(2,1)S(1)} %slice.275), channel_id=1, source_target_pairs={{0,1},{1,0},{2,3},{3,2},{4,5},{5,4},{6,7},{7,6},{8,9},{9,8},{10,11... | collective-permute-start | bytes 2752520 | tf_op jit(solution)/shard_map/ppermute | solution.py:92
  222.7 4.8 %shard_map.243 = bf16[896,1024]{1,0:T(8,128)(2,1)S(1)} custom-call(bf16[896,1536]{1,0:T(8,128)(2,1)S(1)} %shard_map.238.act, bf16[3072,1536]{1,0:T(8,128)(2,1)S(1)} %copy-done, bf16[896,384]{1,0:T(8,128)(2,1)S(1)} %shard_map.241.attended, bf16[384,3072]{1,0:T(8,128)(2,1)S(1)} %copy-done.1), custom_call_target="tpu_custom_call" | custom-call | flops 3523215360 | bytes 8388608 | tf_op jit(solution)/shard_map/pallas_call | solution.py:355
  227.7 4.8 %shard_map.242 = bf16[896,1024]{1,0:T(8,128)(2,1)S(1)} custom-call(bf16[896,1536]{1,0:T(8,128)(2,1)S(1)} %shard_map.238.act, bf16[3072,1536]{1,0:T(8,128)(2,1)S(1)} %copy-done, bf16[896,384]{1,0:T(8,128)(2,1)S(1)} %shard_map.241.attended, bf16[384,3072]{1,0:T(8,128)(2,1)S(1)} %copy-done.1), custom_call_target="tpu_custom_call" | custom-call | flops 3523215360 | bytes 8388608 | tf_op jit(solution)/shard_map/pallas_call | solution.py:355
  233.6 2.7 collective-permute-start.46
  236.8 2.7 collective-permute-start.41
  240.0 2.7 collective-permute-start.36
  242.9 1.5 collective-permute-start.45
  244.5 1.3 collective-permute-start.42
  246.3 2.5 collective-permute-start.37
  249.5 4.0 %collective-permute-done.42.refs_5_ = bf16[112,1024]{1,0:T(8,128)(2,1)S(1)} collective-permute-done((bf16[112,1024]{1,0:T(8,128)(2,1)S(1)}, bf16[112,1024]{1,0:T(8,128)(2,1)S(1)}, u32[]{:S(2)}, u32[]{:S(2)}) %collective-permute-start.42) | collective-permute-done | bytes 229408 | tf_op jit(solution)/shard_map/ppermute | solution.py:102
  254.7 3.8 %collective-permute-done.37.refs_2_ = bf16[112,1024]{1,0:T(8,128)(2,1)S(1)} collective-permute-done((bf16[112,1024]{1,0:T(8,128)(2,1)S(1)}, bf16[112,1024]{1,0:T(8,128)(2,1)S(1)}, u32[]{:S(2)}, u32[]{:S(2)}) %collective-permute-start.37) | collective-permute-done | bytes 229408 | tf_op jit(solution)/shard_map/ppermute | solution.py:102
  259.6 2.0 shard_map.245
  261.6 4.4 %collective-permute-start.48 = (f32[32,64]{1,0:T(8,128)S(1)}, f32[32,64]{1,0:T(8,128)S(1)}, u32[]{:S(2)}, u32[]{:S(2)}) collective-permute-start(f32[32,64]{1,0:T(8,128)S(1)} %get-tuple-element.47), channel_id=1, source_target_pairs={{0,1},{1,2},{2,3},{3,4},{4,5},{5,6},{6,7},{8,9},{9,10},{10,11},{11... | collective-permute-start | bytes 24584 | tf_op jit(solution)/shard_map/ppermute | solution.py:537
  266.1 1.9 collective-permute-start.49
  271.7 1.5 shard_map.246
  273.2 1.4 reshape.231
  (218 shorter events, 31.1 us)
Async XLA Ops:
  7.2 17.8 %copy-start.21 = (bf16[192,1536]{1,0:T(8,128)(2,1)S(1)}, bf16[192,1536]{1,0:T(8,128)(2,1)}, u32[]{:S(2)}) copy-start(bf16[192,1536]{1,0:T(8,128)(2,1)} %param.37) | copy-start | bytes 1769476
  7.2 198.9 %all-gather.2.cloned.1.call-start = ((), (), s32[]{:S(2)}) async-start(), calls=%async_computation | async-start | bytes 10027008 | tf_op jit(solution)/shard_map/all_gather | solution.py:489
  10.5 18.3 %copy-start.26 = (s32[3,1,512]{2,1,0:T(1,128)S(1)}, s32[3,1,512]{2,1,0:T(1,128)}, u32[]{:S(2)}) copy-start(s32[3,1,512]{2,1,0:T(1,128)} %param.26) | copy-start | bytes 18436
  10.5 18.4 %copy-start.27 = (s32[3,1,256]{2,1,0:T(1,128)S(1)}, s32[3,1,256]{2,1,0:T(1,128)}, u32[]{:S(2)}) copy-start(s32[3,1,256]{2,1,0:T(1,128)} %param.25) | copy-start | bytes 9220
  10.5 18.5 %copy-start.28 = (s32[3,1,128]{2,1,0:T(1,128)S(1)}, s32[3,1,128]{2,1,0:T(1,128)}, u32[]{:S(2)}) copy-start(s32[3,1,128]{2,1,0:T(1,128)} %param.27) | copy-start | bytes 4612
  11.5 18.5 %copy-start.6 = (f32[4,3,3072]{2,1,0:T(4,128)}, f32[4,3,3072]{2,1,0:T(4,128)S(1)}, u32[]{:S(2)}) copy-start(f32[4,3,3072]{2,1,0:T(4,128)S(1)} %copy.31.mod_table) | copy-start | bytes 442372
  20.7 51.9 %collective-permute-start = (bf16[112,3072]{1,0:T(8,128)(2,1)S(1)}, bf16[112,3072]{1,0:T(8,128)(2,1)}, u32[]{:S(2)}, u32[]{:S(2)}) collective-permute-start(bf16[112,3072]{1,0:T(8,128)(2,1)S(1)} %shard_map.237), channel_id=1, source_target_pairs={{0,6},{1,7},{2,0},{3,1},{4,2},{5,3},{6,4},{7,5},{8,14},{9,15},{10,... | collective-permute-start | bytes 2064392 | tf_op jit(solution)/shard_map/ppermute | solution.py:80
  24.0 52.2 %collective-permute-start.2 = (bf16[112,3072]{1,0:T(8,128)(2,1)S(1)}, bf16[112,3072]{1,0:T(8,128)(2,1)S(1)}, u32[]{:S(2)}, u32[]{:S(2)}) collective-permute-start(bf16[112,3072]{1,0:T(8,128)(2,1)S(1)} %shard_map.237), channel_id=1, source_target_pairs={{0,2},{1,3},{2,4},{3,5},{4,6},{5,7},{6,0},{7,1},{8,10},{9,11},{10,... | collective-permute-start | bytes 2064392 | tf_op jit(solution)/shard_map/ppermute | solution.py:81
  24.0 72.7 %collective-permute-start.4 = (bf16[112,3072]{1,0:T(8,128)(2,1)S(1)}, bf16[112,3072]{1,0:T(8,128)(2,1)}, u32[]{:S(2)}, u32[]{:S(2)}) collective-permute-start(bf16[112,3072]{1,0:T(8,128)(2,1)S(1)} %shard_map.237), channel_id=1, source_target_pairs={{0,1},{1,0},{2,3},{3,2},{4,5},{5,4},{6,7},{7,6},{8,9},{9,8},{10,11... | collective-permute-start | bytes 2064392 | tf_op jit(solution)/shard_map/ppermute | solution.py:85
  26.0 16.6 %collective-permute-start.9 = (bf16[96,1536]{1,0:T(8,128)(2,1)}, bf16[96,1536]{1,0:T(8,128)(2,1)}, u32[]{:S(2)}, u32[]{:S(2)}) collective-permute-start(bf16[96,1536]{1,0:T(8,128)(2,1)} %get-tuple-element.43), channel_id=1, source_target_pairs={{0,8},{8,16},{16,24},{24,0},{32,40},{40,48},{48,56},{56,32},{64,72... | collective-permute-start | bytes 884744 | tf_op jit(solution)/shard_map/ppermute | solution.py:52
  27.3 18.8 %collective-permute-start.10 = (bf16[96,1536]{1,0:T(8,128)(2,1)}, bf16[96,1536]{1,0:T(8,128)(2,1)}, u32[]{:S(2)}, u32[]{:S(2)}) collective-permute-start(bf16[96,1536]{1,0:T(8,128)(2,1)} %get-tuple-element.43), channel_id=1, source_target_pairs={{0,24},{8,0},{16,8},{24,16},{32,56},{40,32},{48,40},{56,48},{64,88... | collective-permute-start | bytes 884744 | tf_op jit(solution)/shard_map/ppermute | solution.py:53
  42.6 10.2 %collective-permute-start.17 = (bf16[96,1536]{1,0:T(8,128)(2,1)S(1)}, bf16[96,1536]{1,0:T(8,128)(2,1)S(1)}, u32[]{:S(2)}, u32[]{:S(2)}) collective-permute-start(bf16[96,1536]{1,0:T(8,128)(2,1)S(1)} %copy-done.22), channel_id=1, source_target_pairs={{0,32},{8,40},{16,48},{24,56},{32,64},{40,72},{48,80},{56,88},{64,... | collective-permute-start | bytes 884744 | tf_op jit(solution)/shard_map/ppermute | solution.py:52
  46.1 8.8 %collective-permute-start.18 = (bf16[96,1536]{1,0:T(8,128)(2,1)S(1)}, bf16[96,1536]{1,0:T(8,128)(2,1)S(1)}, u32[]{:S(2)}, u32[]{:S(2)}) collective-permute-start(bf16[96,1536]{1,0:T(8,128)(2,1)S(1)} %copy-done.22), channel_id=1, source_target_pairs={{0,96},{8,104},{16,112},{24,120},{32,0},{40,8},{48,16},{56,24},{64... | collective-permute-start | bytes 884744 | tf_op jit(solution)/shard_map/ppermute | solution.py:53
  50.4 51.7 %slice-start = ((s8[7077888]{0:T(1024)(128)(4,1)}), s8[4194304]{0:T(1024)(128)(4,1)S(1)}, s32[]{:S(2)}) async-start(s8[7077888]{0:T(1024)(128)(4,1)} %bitcast.21), calls=%async_computation.1 | async-start | bytes 8388608
  52.9 9.5 %collective-permute-start.11 = (bf16[48,1536]{1,0:T(8,128)(2,1)S(1)}, bf16[48,1536]{1,0:T(8,128)(2,1)S(1)}, u32[]{:S(2)}, u32[]{:S(2)}) collective-permute-start(bf16[48,1536]{1,0:T(8,128)(2,1)S(1)} %slice.241), channel_id=1, source_target_pairs={{0,8},{8,16},{16,24},{24,0},{32,40},{40,48},{48,56},{56,32},{64,72... | collective-permute-start | bytes 442376 | tf_op jit(solution)/shard_map/ppermute | solution.py:54
  54.9 8.1 %collective-permute-start.12 = (bf16[48,1536]{1,0:T(8,128)(2,1)S(1)}, bf16[48,1536]{1,0:T(8,128)(2,1)S(1)}, u32[]{:S(2)}, u32[]{:S(2)}) collective-permute-start(bf16[48,1536]{1,0:T(8,128)(2,1)S(1)} %slice.242), channel_id=1, source_target_pairs={{0,24},{8,0},{16,8},{24,16},{32,56},{40,32},{48,40},{56,48},{64,88... | collective-permute-start | bytes 442376 | tf_op jit(solution)/shard_map/ppermute | solution.py:55
  62.4 9.5 %collective-permute-start.19 = (bf16[48,1536]{1,0:T(8,128)(2,1)S(1)}, bf16[48,1536]{1,0:T(8,128)(2,1)S(1)}, u32[]{:S(2)}, u32[]{:S(2)}) collective-permute-start(bf16[48,1536]{1,0:T(8,128)(2,1)S(1)} %slice.245), channel_id=1, source_target_pairs={{0,32},{8,40},{16,48},{24,56},{32,64},{40,72},{48,80},{56,88},{64,... | collective-permute-start | bytes 442376 | tf_op jit(solution)/shard_map/ppermute | solution.py:54
  63.1 58.5 %collective-permute-start.20 = (bf16[48,1536]{1,0:T(8,128)(2,1)S(1)}, bf16[48,1536]{1,0:T(8,128)(2,1)S(1)}, u32[]{:S(2)}, u32[]{:S(2)}) collective-permute-start(bf16[48,1536]{1,0:T(8,128)(2,1)S(1)} %slice.246), channel_id=1, source_target_pairs={{0,96},{8,104},{16,112},{24,120},{32,0},{40,8},{48,16},{56,24},{64... | collective-permute-start | bytes 442376 | tf_op jit(solution)/shard_map/ppermute | solution.py:55
  71.9 85.5 %collective-permute-start.13 = (bf16[384,1536]{1,0:T(8,128)(2,1)}, bf16[384,1536]{1,0:T(8,128)(2,1)}, u32[]{:S(2)}, u32[]{:S(2)}) collective-permute-start(bf16[384,1536]{1,0:T(8,128)(2,1)} %constant_dynamic-update-slice_fusion.10.refs_0_), channel_id=1, source_target_pairs={{0,32},{8,40},{16,48},{24,56},{32,64},{40,72},{48,80},{56,88},{64,... | collective-permute-start | bytes 3538952 | tf_op jit(solution)/shard_map/ppermute | solution.py:52
  72.5 89.6 %collective-permute-start.14 = (bf16[384,1536]{1,0:T(8,128)(2,1)}, bf16[384,1536]{1,0:T(8,128)(2,1)}, u32[]{:S(2)}, u32[]{:S(2)}) collective-permute-start(bf16[384,1536]{1,0:T(8,128)(2,1)} %constant_dynamic-update-slice_fusion.10.refs_0_), channel_id=1, source_target_pairs={{0,96},{8,104},{16,112},{24,120},{32,0},{40,8},{48,16},{56,24},{64... | collective-permute-start | bytes 3538952 | tf_op jit(solution)/shard_map/ppermute | solution.py:53
  76.2 7.4 %collective-permute-start.1 = (bf16[56,3072]{1,0:T(8,128)(2,1)S(1)}, bf16[56,3072]{1,0:T(8,128)(2,1)S(1)}, u32[]{:S(2)}, u32[]{:S(2)}) collective-permute-start(bf16[56,3072]{1,0:T(8,128)(2,1)S(1)} %slice.239), channel_id=1, source_target_pairs={{0,6},{1,7},{2,0},{3,1},{4,2},{5,3},{6,4},{7,5},{8,14},{9,15},{10,... | collective-permute-start | bytes 1032200 | tf_op jit(solution)/shard_map/ppermute | solution.py:82
  83.6 8.7 %collective-permute-start.3 = (bf16[56,3072]{1,0:T(8,128)(2,1)S(1)}, bf16[56,3072]{1,0:T(8,128)(2,1)S(1)}, u32[]{:S(2)}, u32[]{:S(2)}) collective-permute-start(bf16[56,3072]{1,0:T(8,128)(2,1)S(1)} %slice.240), channel_id=1, source_target_pairs={{0,2},{1,3},{2,4},{3,5},{4,6},{5,7},{6,0},{7,1},{8,10},{9,11},{10,... | collective-permute-start | bytes 1032200 | tf_op jit(solution)/shard_map/ppermute | solution.py:83
  83.7 18.4 %slice-start.1 = ((s8[7077888]{0:T(1024)(128)(4,1)}), s8[2883584]{0:T(1024)(128)(4,1)S(1)}, s32[]{:S(2)}) async-start(s8[7077888]{0:T(1024)(128)(4,1)} %bitcast.21), calls=%async_computation.2 | async-start | bytes 5767168
  92.3 6.3 %collective-permute-start.5 = (bf16[112,3072]{1,0:T(8,128)(2,1)}, bf16[112,3072]{1,0:T(8,128)(2,1)S(1)}, u32[]{:S(2)}, u32[]{:S(2)}) collective-permute-start(bf16[112,3072]{1,0:T(8,128)(2,1)} %collective-permute-done), channel_id=1, source_target_pairs={{0,1},{1,0},{2,3},{3,2},{4,5},{5,4},{6,7},{7,6},{8,9},{9,8},{10,11... | collective-permute-start | bytes 2064392 | tf_op jit(solution)/shard_map/ppermute | solution.py:85
  96.7 5.2 %collective-permute-start.8 = (bf16[112,3072]{1,0:T(8,128)(2,1)S(1)}, bf16[112,3072]{1,0:T(8,128)(2,1)S(1)}, u32[]{:S(2)}, u32[]{:S(2)}) collective-permute-start(bf16[112,3072]{1,0:T(8,128)(2,1)S(1)} %collective-permute-done.2), channel_id=1, source_target_pairs={{0,1},{1,0},{2,3},{3,2},{4,5},{5,4},{6,7},{7,6},{8,9},{9,8},{10,11... | collective-permute-start | bytes 2064392 | tf_op jit(solution)/shard_map/ppermute | solution.py:85
  98.6 1.7 collective-permute-start.6
  100.3 1.7 collective-permute-start.7
  102.0 16.8 %copy-start.19 = (bf16[896,3072]{1,0:T(8,128)(2,1)}, bf16[896,3072]{1,0:T(8,128)(2,1)S(1)}, u32[]{:S(2)}) copy-start(bf16[896,3072]{1,0:T(8,128)(2,1)S(1)} %constant_dynamic-update-slice_fusion.x) | copy-start | bytes 16515076
  118.8 38.3 %copy-start.10 = (bf16[3,3,128,128]{3,2,1,0:T(8,128)(2,1)}, bf16[3,3,128,128]{3,2,1,0:T(8,128)(2,1)S(1)}, u32[]{:S(2)}) copy-start(bf16[3,3,128,128]{3,2,1,0:T(8,128)(2,1)S(1)} %get-tuple-element.10.query) | copy-start | bytes 884740
  118.8 38.5 %copy-start.30 = (s32[4]{0:T(128)S(1)}, s32[4]{0:T(128)}, u32[]{:S(2)}) copy-start(s32[4]{0:T(128)} %constant.148.clone) | copy-start | bytes 52
  118.9 7.4 %collective-permute-start.25 = (bf16[1,6,128,128]{3,2,1,0:T(8,128)(2,1)S(1)}, bf16[1,6,128,128]{3,2,1,0:T(8,128)(2,1)S(1)}, u32[]{:S(2)}, u32[]{:S(2)}) collective-permute-start(bf16[1,6,128,128]{3,2,1,0:T(8,128)(2,1)S(1)} %bitcast.23), channel_id=1, source_target_pairs={{0,8},{8,16},{16,24},{24,0},{32,40},{40,48},{48,56},{56,32},{64,72... | collective-permute-start | bytes 589832 | tf_op jit(solution)/shard_map/ppermute | solution.py:52
  118.9 7.3 %collective-permute-start.26 = (bf16[1,6,128,128]{3,2,1,0:T(8,128)(2,1)S(1)}, bf16[1,6,128,128]{3,2,1,0:T(8,128)(2,1)S(1)}, u32[]{:S(2)}, u32[]{:S(2)}) collective-permute-start(bf16[1,6,128,128]{3,2,1,0:T(8,128)(2,1)S(1)} %bitcast.24), channel_id=1, source_target_pairs={{0,24},{8,0},{16,8},{24,16},{32,56},{40,32},{48,40},{56,48},{64,88... | collective-permute-start | bytes 589832 | tf_op jit(solution)/shard_map/ppermute | solution.py:53
  122.3 41.8 %collective-permute-start.21 = (bf16[384,1536]{1,0:T(8,128)(2,1)}, bf16[384,1536]{1,0:T(8,128)(2,1)}, u32[]{:S(2)}, u32[]{:S(2)}) collective-permute-start(bf16[384,1536]{1,0:T(8,128)(2,1)} %constant_dynamic-update-slice_fusion.15.refs_5_), channel_id=1, source_target_pairs={{0,8},{8,16},{16,24},{24,0},{32,40},{40,48},{48,56},{56,32},{64,72... | collective-permute-start | bytes 3538952 | tf_op jit(solution)/shard_map/ppermute | solution.py:52
  126.3 42.4 %collective-permute-start.22 = (bf16[384,1536]{1,0:T(8,128)(2,1)}, bf16[384,1536]{1,0:T(8,128)(2,1)}, u32[]{:S(2)}, u32[]{:S(2)}) collective-permute-start(bf16[384,1536]{1,0:T(8,128)(2,1)} %constant_dynamic-update-slice_fusion.15.refs_5_), channel_id=1, source_target_pairs={{0,24},{8,0},{16,8},{24,16},{32,56},{40,32},{48,40},{56,48},{64,88... | collective-permute-start | bytes 3538952 | tf_op jit(solution)/shard_map/ppermute | solution.py:53
  126.3 27.4 %collective-permute-start.27 = (bf16[1,3,128,128]{3,2,1,0:T(8,128)(2,1)S(1)}, bf16[1,3,128,128]{3,2,1,0:T(8,128)(2,1)S(1)}, u32[]{:S(2)}, u32[]{:S(2)}) collective-permute-start(bf16[1,3,128,128]{3,2,1,0:T(8,128)(2,1)S(1)} %slice.252), channel_id=1, source_target_pairs={{0,8},{8,16},{16,24},{24,0},{32,40},{40,48},{48,56},{56,32},{64,72... | collective-permute-start | bytes 294920 | tf_op jit(solution)/shard_map/ppermute | solution.py:54
  153.6 3.5 %collective-permute-start.28 = (bf16[1,3,128,128]{3,2,1,0:T(8,128)(2,1)S(1)}, bf16[1,3,128,128]{3,2,1,0:T(8,128)(2,1)S(1)}, u32[]{:S(2)}, u32[]{:S(2)}) collective-permute-start(bf16[1,3,128,128]{3,2,1,0:T(8,128)(2,1)S(1)} %slice.253), channel_id=1, source_target_pairs={{0,24},{8,0},{16,8},{24,16},{32,56},{40,32},{48,40},{56,48},{64,88... | collective-permute-start | bytes 294920 | tf_op jit(solution)/shard_map/ppermute | solution.py:55
  157.2 18.0 %collective-permute-start.29 = (bf16[4,6,128,128]{3,2,1,0:T(8,128)(2,1)S(1)}, bf16[4,6,128,128]{3,2,1,0:T(8,128)(2,1)S(1)}, u32[]{:S(2)}, u32[]{:S(2)}) collective-permute-start(bf16[4,6,128,128]{3,2,1,0:T(8,128)(2,1)S(1)} %maximum_maximum_fusion.refs_0_.refs_5_), channel_id=1, source_target_pairs={{0,32},{8,40},{16,48},{24,56},{32,64},{40,72},{48,80},{56,88},{64,... | collective-permute-start | bytes 2359304 | tf_op jit(solution)/shard_map/ppermute | solution.py:52
  157.3 22.8 %collective-permute-start.30 = (bf16[4,6,128,128]{3,2,1,0:T(8,128)(2,1)S(1)}, bf16[4,6,128,128]{3,2,1,0:T(8,128)(2,1)}, u32[]{:S(2)}, u32[]{:S(2)}) collective-permute-start(bf16[4,6,128,128]{3,2,1,0:T(8,128)(2,1)S(1)} %maximum_maximum_fusion.refs_0_.refs_5_), channel_id=1, source_target_pairs={{0,96},{8,104},{16,112},{24,120},{32,0},{40,8},{48,16},{56,24},{64... | collective-permute-start | bytes 2359304 | tf_op jit(solution)/shard_map/ppermute | solution.py:53
  162.1 25.8 %collective-permute-start.15 = (bf16[192,1536]{1,0:T(8,128)(2,1)}, bf16[192,1536]{1,0:T(8,128)(2,1)}, u32[]{:S(2)}, u32[]{:S(2)}) collective-permute-start(bf16[192,1536]{1,0:T(8,128)(2,1)} %slice.243), channel_id=1, source_target_pairs={{0,32},{8,40},{16,48},{24,56},{32,64},{40,72},{48,80},{56,88},{64,... | collective-permute-start | bytes 1769480 | tf_op jit(solution)/shard_map/ppermute | solution.py:54
  164.1 23.8 %collective-permute-start.16 = (bf16[192,1536]{1,0:T(8,128)(2,1)}, bf16[192,1536]{1,0:T(8,128)(2,1)}, u32[]{:S(2)}, u32[]{:S(2)}) collective-permute-start(bf16[192,1536]{1,0:T(8,128)(2,1)} %slice.244), channel_id=1, source_target_pairs={{0,96},{8,104},{16,112},{24,120},{32,0},{40,8},{48,16},{56,24},{64... | collective-permute-start | bytes 1769480 | tf_op jit(solution)/shard_map/ppermute | solution.py:55
  168.7 19.2 %collective-permute-start.23 = (bf16[192,1536]{1,0:T(8,128)(2,1)}, bf16[192,1536]{1,0:T(8,128)(2,1)}, u32[]{:S(2)}, u32[]{:S(2)}) collective-permute-start(bf16[192,1536]{1,0:T(8,128)(2,1)} %slice.247), channel_id=1, source_target_pairs={{0,8},{8,16},{16,24},{24,0},{32,40},{40,48},{48,56},{56,32},{64,72... | collective-permute-start | bytes 1769480 | tf_op jit(solution)/shard_map/ppermute | solution.py:54
  175.2 12.8 %collective-permute-start.24 = (bf16[192,1536]{1,0:T(8,128)(2,1)}, bf16[192,1536]{1,0:T(8,128)(2,1)}, u32[]{:S(2)}, u32[]{:S(2)}) collective-permute-start(bf16[192,1536]{1,0:T(8,128)(2,1)} %slice.248), channel_id=1, source_target_pairs={{0,24},{8,0},{16,8},{24,16},{32,56},{40,32},{48,40},{56,48},{64,88... | collective-permute-start | bytes 1769480 | tf_op jit(solution)/shard_map/ppermute | solution.py:55
  180.2 22.6 %collective-permute-start.31 = (bf16[2,6,128,128]{3,2,1,0:T(8,128)(2,1)S(1)}, bf16[2,6,128,128]{3,2,1,0:T(8,128)(2,1)S(1)}, u32[]{:S(2)}, u32[]{:S(2)}) collective-permute-start(bf16[2,6,128,128]{3,2,1,0:T(8,128)(2,1)S(1)} %slice.254), channel_id=1, source_target_pairs={{0,32},{8,40},{16,48},{24,56},{32,64},{40,72},{48,80},{56,88},{64,... | collective-permute-start | bytes 1179656 | tf_op jit(solution)/shard_map/ppermute | solution.py:54
  181.3 21.5 %copy-start.3 = (bf16[4,6,128,128]{3,2,1,0:T(8,128)(2,1)S(1)}, bf16[4,6,128,128]{3,2,1,0:T(8,128)(2,1)}, u32[]{:S(2)}) copy-start(bf16[4,6,128,128]{3,2,1,0:T(8,128)(2,1)} %copy-done.2) | copy-start | bytes 2359300
  181.3 21.5 %copy-start.5 = (bf16[4,6,128,128]{3,2,1,0:T(8,128)(2,1)S(1)}, bf16[4,6,128,128]{3,2,1,0:T(8,128)(2,1)}, u32[]{:S(2)}) copy-start(bf16[4,6,128,128]{3,2,1,0:T(8,128)(2,1)} %copy-done.4) | copy-start | bytes 2359300
  181.3 21.5 %copy-start.11 = (bf16[3,3,128,128]{3,2,1,0:T(8,128)(2,1)S(1)}, bf16[3,3,128,128]{3,2,1,0:T(8,128)(2,1)}, u32[]{:S(2)}) copy-start(bf16[3,3,128,128]{3,2,1,0:T(8,128)(2,1)} %copy-done.10) | copy-start | bytes 884740
  187.9 14.8 %collective-permute-start.32 = (bf16[2,6,128,128]{3,2,1,0:T(8,128)(2,1)S(1)}, bf16[2,6,128,128]{3,2,1,0:T(8,128)(2,1)S(1)}, u32[]{:S(2)}, u32[]{:S(2)}) collective-permute-start(bf16[2,6,128,128]{3,2,1,0:T(8,128)(2,1)S(1)} %slice.255), channel_id=1, source_target_pairs={{0,96},{8,104},{16,112},{24,120},{32,0},{40,8},{48,16},{56,24},{64... | collective-permute-start | bytes 1179656 | tf_op jit(solution)/shard_map/ppermute | solution.py:55
  216.3 16.9 %collective-permute-start.43 = (bf16[448,1024]{1,0:T(8,128)(2,1)S(1)}, bf16[448,1024]{1,0:T(8,128)(2,1)S(1)}, u32[]{:S(2)}, u32[]{:S(2)}) collective-permute-start(bf16[448,1024]{1,0:T(8,128)(2,1)S(1)} %slice.275), channel_id=1, source_target_pairs={{0,1},{1,0},{2,3},{3,2},{4,5},{5,4},{6,7},{7,6},{8,9},{9,8},{10,11... | collective-permute-start | bytes 2752520 | tf_op jit(solution)/shard_map/ppermute | solution.py:92
  227.6 8.7 %collective-permute-start.38 = (bf16[448,1024]{1,0:T(8,128)(2,1)S(1)}, bf16[448,1024]{1,0:T(8,128)(2,1)S(1)}, u32[]{:S(2)}, u32[]{:S(2)}) collective-permute-start(bf16[448,1024]{1,0:T(8,128)(2,1)S(1)} %slice.266), channel_id=1, source_target_pairs={{0,1},{1,0},{2,3},{3,2},{4,5},{5,4},{6,7},{7,6},{8,9},{9,8},{10,11... | collective-permute-start | bytes 2752520 | tf_op jit(solution)/shard_map/ppermute | solution.py:92
  232.6 6.9 %collective-permute-start.33 = (bf16[448,1024]{1,0:T(8,128)(2,1)S(1)}, bf16[448,1024]{1,0:T(8,128)(2,1)S(1)}, u32[]{:S(2)}, u32[]{:S(2)}) collective-permute-start(bf16[448,1024]{1,0:T(8,128)(2,1)S(1)} %slice.257), channel_id=1, source_target_pairs={{0,1},{1,0},{2,3},{3,2},{4,5},{5,4},{6,7},{7,6},{8,9},{9,8},{10,11... | collective-permute-start | bytes 2752520 | tf_op jit(solution)/shard_map/ppermute | solution.py:92
  233.6 6.4 %collective-permute-start.44 = (bf16[112,512]{1,0:T(8,128)(2,1)S(1)}, bf16[112,512]{1,0:T(8,128)(2,1)S(1)}, u32[]{:S(2)}, u32[]{:S(2)}) collective-permute-start(bf16[112,512]{1,0:T(8,128)(2,1)S(1)} %get-tuple-element.31), channel_id=1, source_target_pairs={{0,2},{1,3},{2,4},{3,5},{4,6},{5,7},{6,0},{7,1},{8,10},{9,11},{10,... | collective-permute-start | bytes 344072 | tf_op jit(solution)/shard_map/ppermute | solution.py:95
  233.6 9.0 %collective-permute-start.46 = (bf16[112,512]{1,0:T(8,128)(2,1)S(1)}, bf16[112,512]{1,0:T(8,128)(2,1)S(1)}, u32[]{:S(2)}, u32[]{:S(2)}) collective-permute-start(bf16[112,512]{1,0:T(8,128)(2,1)S(1)} %get-tuple-element.29), channel_id=1, source_target_pairs={{0,6},{1,7},{2,0},{3,1},{4,2},{5,3},{6,4},{7,5},{8,14},{9,15},{10,... | collective-permute-start | bytes 344072 | tf_op jit(solution)/shard_map/ppermute | solution.py:96
  236.7 6.1 %collective-permute-start.39 = (bf16[112,512]{1,0:T(8,128)(2,1)S(1)}, bf16[112,512]{1,0:T(8,128)(2,1)S(1)}, u32[]{:S(2)}, u32[]{:S(2)}) collective-permute-start(bf16[112,512]{1,0:T(8,128)(2,1)S(1)} %get-tuple-element.35), channel_id=1, source_target_pairs={{0,2},{1,3},{2,4},{3,5},{4,6},{5,7},{6,0},{7,1},{8,10},{9,11},{10,... | collective-permute-start | bytes 344072 | tf_op jit(solution)/shard_map/ppermute | solution.py:95
  236.8 7.6 %collective-permute-start.41 = (bf16[112,512]{1,0:T(8,128)(2,1)S(1)}, bf16[112,512]{1,0:T(8,128)(2,1)S(1)}, u32[]{:S(2)}, u32[]{:S(2)}) collective-permute-start(bf16[112,512]{1,0:T(8,128)(2,1)S(1)} %get-tuple-element.33), channel_id=1, source_target_pairs={{0,6},{1,7},{2,0},{3,1},{4,2},{5,3},{6,4},{7,5},{8,14},{9,15},{10,... | collective-permute-start | bytes 344072 | tf_op jit(solution)/shard_map/ppermute | solution.py:96
  239.9 5.9 %collective-permute-start.34 = (bf16[112,512]{1,0:T(8,128)(2,1)S(1)}, bf16[112,512]{1,0:T(8,128)(2,1)S(1)}, u32[]{:S(2)}, u32[]{:S(2)}) collective-permute-start(bf16[112,512]{1,0:T(8,128)(2,1)S(1)} %get-tuple-element.39), channel_id=1, source_target_pairs={{0,2},{1,3},{2,4},{3,5},{4,6},{5,7},{6,0},{7,1},{8,10},{9,11},{10,... | collective-permute-start | bytes 344072 | tf_op jit(solution)/shard_map/ppermute | solution.py:95
  240.0 6.1 %collective-permute-start.36 = (bf16[112,512]{1,0:T(8,128)(2,1)S(1)}, bf16[112,512]{1,0:T(8,128)(2,1)S(1)}, u32[]{:S(2)}, u32[]{:S(2)}) collective-permute-start(bf16[112,512]{1,0:T(8,128)(2,1)S(1)} %get-tuple-element.37), channel_id=1, source_target_pairs={{0,6},{1,7},{2,0},{3,1},{4,2},{5,3},{6,4},{7,5},{8,14},{9,15},{10,... | collective-permute-start | bytes 344072 | tf_op jit(solution)/shard_map/ppermute | solution.py:96
  242.7 6.1 %collective-permute-start.47 = (bf16[112,1024]{1,0:T(8,128)(2,1)S(1)}, bf16[112,1024]{1,0:T(8,128)(2,1)S(1)}, u32[]{:S(2)}, u32[]{:S(2)}) collective-permute-start(bf16[112,1024]{1,0:T(8,128)(2,1)S(1)} %pad_maximum_fusion.5), channel_id=1, source_target_pairs={{0,6},{1,7},{2,0},{3,1},{4,2},{5,3},{6,4},{7,5},{8,14},{9,15},{10,... | collective-permute-start | bytes 688136 | tf_op jit(solution)/shard_map/ppermute | solution.py:102
  242.9 6.7 %collective-permute-start.45 = (bf16[112,1024]{1,0:T(8,128)(2,1)S(1)}, bf16[112,1024]{1,0:T(8,128)(2,1)S(1)}, u32[]{:S(2)}, u32[]{:S(2)}) collective-permute-start(bf16[112,1024]{1,0:T(8,128)(2,1)S(1)} %pad_maximum_fusion.4), channel_id=1, source_target_pairs={{0,2},{1,3},{2,4},{3,5},{4,6},{5,7},{6,0},{7,1},{8,10},{9,11},{10,... | collective-permute-start | bytes 688136 | tf_op jit(solution)/shard_map/ppermute | solution.py:101
  244.5 9.0 %collective-permute-start.42 = (bf16[112,1024]{1,0:T(8,128)(2,1)S(1)}, bf16[112,1024]{1,0:T(8,128)(2,1)S(1)}, u32[]{:S(2)}, u32[]{:S(2)}) collective-permute-start(bf16[112,1024]{1,0:T(8,128)(2,1)S(1)} %pad_maximum_fusion.3), channel_id=1, source_target_pairs={{0,6},{1,7},{2,0},{3,1},{4,2},{5,3},{6,4},{7,5},{8,14},{9,15},{10,... | collective-permute-start | bytes 688136 | tf_op jit(solution)/shard_map/ppermute | solution.py:102
  245.8 8.9 %collective-permute-start.40 = (bf16[112,1024]{1,0:T(8,128)(2,1)S(1)}, bf16[112,1024]{1,0:T(8,128)(2,1)S(1)}, u32[]{:S(2)}, u32[]{:S(2)}) collective-permute-start(bf16[112,1024]{1,0:T(8,128)(2,1)S(1)} %pad_maximum_fusion.2), channel_id=1, source_target_pairs={{0,2},{1,3},{2,4},{3,5},{4,6},{5,7},{6,0},{7,1},{8,10},{9,11},{10,... | collective-permute-start | bytes 688136 | tf_op jit(solution)/shard_map/ppermute | solution.py:101
  246.3 12.1 %collective-permute-start.37 = (bf16[112,1024]{1,0:T(8,128)(2,1)S(1)}, bf16[112,1024]{1,0:T(8,128)(2,1)S(1)}, u32[]{:S(2)}, u32[]{:S(2)}) collective-permute-start(bf16[112,1024]{1,0:T(8,128)(2,1)S(1)} %pad_maximum_fusion.1), channel_id=1, source_target_pairs={{0,6},{1,7},{2,0},{3,1},{4,2},{5,3},{6,4},{7,5},{8,14},{9,15},{10,... | collective-permute-start | bytes 688136 | tf_op jit(solution)/shard_map/ppermute | solution.py:102
  248.8 10.8 %collective-permute-start.35 = (bf16[112,1024]{1,0:T(8,128)(2,1)S(1)}, bf16[112,1024]{1,0:T(8,128)(2,1)S(1)}, u32[]{:S(2)}, u32[]{:S(2)}) collective-permute-start(bf16[112,1024]{1,0:T(8,128)(2,1)S(1)} %pad_maximum_fusion), channel_id=1, source_target_pairs={{0,2},{1,3},{2,4},{3,5},{4,6},{5,7},{6,0},{7,1},{8,10},{9,11},{10,... | collective-permute-start | bytes 688136 | tf_op jit(solution)/shard_map/ppermute | solution.py:101
  261.6 8.5 %collective-permute-start.48 = (f32[32,64]{1,0:T(8,128)S(1)}, f32[32,64]{1,0:T(8,128)S(1)}, u32[]{:S(2)}, u32[]{:S(2)}) collective-permute-start(f32[32,64]{1,0:T(8,128)S(1)} %get-tuple-element.47), channel_id=1, source_target_pairs={{0,1},{1,2},{2,3},{3,4},{4,5},{5,6},{6,7},{8,9},{9,10},{10,11},{11... | collective-permute-start | bytes 24584 | tf_op jit(solution)/shard_map/ppermute | solution.py:537
  266.1 5.1 %collective-permute-start.49 = (f32[32,64]{1,0:T(8,128)S(1)}, f32[32,64]{1,0:T(8,128)S(1)}, u32[]{:S(2)}, u32[]{:S(2)}) collective-permute-start(f32[32,64]{1,0:T(8,128)S(1)} %get-tuple-element.46), channel_id=1, source_target_pairs={{1,0},{2,1},{3,2},{4,3},{5,4},{6,5},{7,6},{9,8},{10,9},{11,10},{12... | collective-permute-start | bytes 24584 | tf_op jit(solution)/shard_map/ppermute | solution.py:538
  (23 other events, 168.9 us)
Sparse Core Ops, SparseCore 0:
  10.1 106.1 all-gather.1

commit v2 on v1

--- a/solution.py
+++ b/solution.py
@@ -48,14 +48,6 @@
 RING_ORDER = (0, -1, 1, 2)
 
 
-def ring(block, shift, first, last):
-    before = lax.ppermute(block, "wide", shift(1))
-    after = lax.ppermute(block, "wide", shift(-1))
-    far_first = lax.ppermute(first(before), "wide", shift(1))
-    far_last = lax.ppermute(last(after), "wide", shift(-1))
-    return before, after, far_first, far_last
-
-
 def along_y(step):
     return wide_shift(0, step)
 
@@ -64,26 +56,22 @@
     return wide_shift(step, 0)
 
 
-def collect(block, shift_one, shift_two):
-    half = block.shape[0] // 2
-    before, after, far_first, far_last = ring(
-        block, shift_one, lambda b: b[:half], lambda b: b[half:]
-    )
-    quad = jnp.concatenate([block, before, after, far_first, far_last], axis=0)
-    two = 2 * block.shape[0]
-    return (quad,) + ring(quad, shift_two, lambda b: b[:two], lambda b: b[two:])
-
-
-def gather_rows(own):
-    half = own.shape[0] // 2
-    swap = functools.partial(lax.ppermute, axis_name="narrow", perm=CORE_SWAP)
-    nxt = lax.ppermute(own, "narrow", chip_shift(-1))
-    prv = lax.ppermute(own, "narrow", chip_shift(1))
-    far_a = lax.ppermute(nxt[:half], "narrow", chip_shift(-1))
-    far_b = lax.ppermute(prv[half:], "narrow", chip_shift(1))
-    return jnp.concatenate(
-        [own, nxt, far_a, far_b, prv, swap(own), swap(nxt), swap(far_a), swap(far_b), swap(prv)], axis=0
-    )
+def wide(block, pairs):
+    return lax.ppermute(block, "wide", pairs)
+
+
+def output_layout():
+    def places(part, *pairs):
+        found = [(outer, inner) for outer, some in pairs for inner in some]
+        return [(part, outer, inner) if part == 0 else (part, inner, outer) for outer, inner in found]
+
+    low, high = RING_ORDER[:2], RING_ORDER[2:]
+    first = [place for part in range(2) for place in places(part, (0, RING_ORDER))]
+    first += [place for part in range(2) for place in places(part, (-1, low), (1, high))]
+    return [first] + [places(part, (-1, high), (2, low), (1, low), (2, high)) for part in (1, 0)]
+
+
+LAYOUT = output_layout()
 
 
 def scatter_sum(partial):
@@ -103,8 +91,12 @@
     return pair[:rows], one, two
 
 
-def modulate_kernel(steps, text, image, extra, mod_table, out):
-    here, there = steps[0], steps[1]
+def steps_of(ids, request_group, step_index):
+    return step_index[request_group[ids[0]]], step_index[step_index.shape[0] - 1]
+
+
+def modulate_kernel(ids, request_group, step_index, text, image, extra, mod_table, out):
+    here, there = steps_of(ids, request_group, step_index)
     shift, scale = mod_table[here, 0:1, :], mod_table[here, 1:2, :]
     row = 0
     for ref in (text, image):
@@ -116,16 +108,16 @@
     out[row : row + rows, :] = (layer_norm(extra[...].astype(F32)) * (1.0 + scale) + shift).astype(BF16)
 
 
-def modulate(steps, text, image, extra, mod_table):
+def modulate(scalars, text, image, extra, mod_table):
     rows = text.shape[0] + image.shape[0] + extra.shape[0]
     return pl.pallas_call(
         modulate_kernel,
         out_shape=jax.ShapeDtypeStruct((rows, text.shape[1]), BF16),
-        in_specs=[SMEM, VMEM, VMEM, VMEM, VMEM],
+        in_specs=[SMEM] * 3 + [VMEM] * 4,
         out_specs=VMEM,
         compiler_params=pltpu.CompilerParams(vmem_limit_bytes=8 * MIB),
         cost_estimate=cost(1e6, 2 * MIB),
-    )(steps, text, image, extra, mod_table)
+    )(*scalars, text, image, extra, mod_table)
 
 
 def partner_of(values):
@@ -149,7 +141,7 @@
     total = x.shape[0]
     rows = total // blocks
     taken = rows - own
-    step = 2 * rows
+    step = 4 * rows
     heads = weight.shape[2] // 128
 
     def tile(index, carry):
@@ -157,9 +149,9 @@
         acc = jnp.dot(x[pl.ds(start, step), :], weight[0], preferred_element_type=F32)
 
         def put(head, values):
-            for part in range(2):
+            for part in range(4):
                 first = part * rows
-                block = 2 * index + part
+                block = 4 * index + part
                 request[0, head, pl.ds(pl.multiple_of(block * taken, 32), taken), :] = values[first : first + taken]
                 extra[0, head, pl.ds(pl.multiple_of(block * own, 16), own), :] = values[first + taken : first + rows]
 
@@ -207,7 +199,7 @@
             pl.BlockSpec((1, heads, request, 128), lambda i: (i, 0, 0, 0)),
             pl.BlockSpec((1, heads, extra, 128), lambda i: (i, 0, 0, 0)),
         ),
-        compiler_params=pltpu.CompilerParams(vmem_limit_bytes=28 * MIB),
+        compiler_params=pltpu.CompilerParams(vmem_limit_bytes=32 * MIB),
         cost_estimate=cost(6 * total * width * weight.shape[2], 16 * MIB),
     )(x, weight, gains, cosine, sine)
 
@@ -288,95 +280,107 @@
     return values * (0.5 * (1.0 + jnp.tanh(inner)))
 
 
-def hidden_kernel(place, x, *refs):
-    pieces, out, weight, done = refs[:10], refs[10], refs[11], refs[12]
-    z, y = place[0], place[1]
-    half = weight.shape[0] // 32
-    copies = []
-
-    def fetch(ref, index, dz, dy, part):
-        group = lax.rem(z + dz + 4, 4) * 4 + lax.rem(y + dy + 4, 4)
+def hidden_kernel(x, weight, out):
+    out[...] = gelu(jnp.dot(x[...], weight[...], preferred_element_type=F32)).astype(BF16)
+
+
+def hidden_units(x, weight, step=256):
+    rows, width = x.shape
+    units = weight.shape[1]
+    return pl.pallas_call(
+        hidden_kernel,
+        grid=(units // step,),
+        out_shape=jax.ShapeDtypeStruct((rows, units), BF16),
+        in_specs=[pl.BlockSpec((rows, width), lambda i: (0, 0)), pl.BlockSpec((width, step), lambda i: (0, i))],
+        out_specs=pl.BlockSpec((rows, step), lambda i: (0, i)),
+        compiler_params=pltpu.CompilerParams(vmem_limit_bytes=40 * MIB),
+        cost_estimate=cost(2 * rows * width * units, 18 * MIB, rows * units),
+    )(x, weight)
+
+
+def output_kernel(chunk, ids, act, attended, attn_weight, *refs):
+    pieces, out, weight, attn_part = refs[:-3], refs[-3], refs[-2], refs[-1]
+    z, y = ids[0] // 4, ids[0] % 4
+    row = 0
+    for piece in pieces:
+        rows = piece.shape[0]
+        weight[row : row + rows, :] = piece[...]
+        row += rows
+    half = row // len(LAYOUT[chunk])
+    for index, (part, dz, dy) in enumerate(LAYOUT[chunk]):
+        group = lax.rem(z + (dz + 4), 4) * 4 + lax.rem(y + (dy + 4), 4)
         start = pl.multiple_of(group * (2 * half) + part * half, 32)
-        copy = pltpu.make_async_copy(
-            ref.at[pl.ds(index * half, half), :], weight.at[pl.ds(start, half), :], done.at[len(copies)]
-        )
-        copy.start()
-        copies.append(copy)
-
-    for part in range(2):
-        quad, before, after, far_first, far_last = pieces[5 * part : 5 * part + 5]
-        for outer, ref, span, base in (
-            (0, quad, range(4), 0),
-            (-1, before, range(4), 0),
-            (1, after, range(4), 0),
-            (2, far_first, range(2), 0),
-            (2, far_last, range(2, 4), 2),
-        ):
-            for index in span:
-                inner = RING_ORDER[index]
-                dz, dy = (outer, inner) if part == 0 else (inner, outer)
-                fetch(ref, index - base, dz, dy, part)
-    for copy in copies:
-        copy.wait()
+        attn_part[index * half : (index + 1) * half, :] = attn_weight[pl.ds(start, half), :]
     step = 256
 
     def tile(index, carry):
         columns = pl.ds(pl.multiple_of(index * step, step), step)
-        acc = jnp.dot(x[...], weight[:, columns], preferred_element_type=F32)
-        out[:, columns] = gelu(acc).astype(BF16)
+        acc = lax.dot_general(act[...], weight[columns, :], NT, preferred_element_type=F32)
+        acc = acc + lax.dot_general(attended[...], attn_part[columns, :], NT, preferred_element_type=F32)
+        out[:, columns] = acc.astype(BF16)
         return carry
 
-    lax.fori_loop(0, out.shape[1] // step, tile, 0)
-
-
-def hidden_units(place, x, pieces):
-    rows, width = x.shape
-    units = pieces[0].shape[1]
-    return pl.pallas_call(
-        hidden_kernel,
-        out_shape=jax.ShapeDtypeStruct((rows, units), BF16),
-        in_specs=[SMEM, VMEM] + [ANY] * 10,
+    lax.fori_loop(0, row // step, tile, 0)
+
+
+def output_part(chunk, ids, act, attended, attn_weight, pieces):
+    rows, units = act.shape
+    columns = sum(piece.shape[0] for piece in pieces)
+    return pl.pallas_call(
+        functools.partial(output_kernel, chunk),
+        out_shape=jax.ShapeDtypeStruct((rows, columns), BF16),
+        in_specs=[SMEM] + [VMEM] * (3 + len(pieces)),
         out_specs=VMEM,
-        scratch_shapes=[pltpu.VMEM((width, units), BF16), pltpu.SemaphoreType.DMA((32,))],
-        compiler_params=pltpu.CompilerParams(vmem_limit_bytes=26 * MIB),
-        cost_estimate=cost(2 * rows * width * units, 18 * MIB, rows * units),
-    )(place, x, *pieces)
-
-
-def output_kernel(act, weight, attended, attn_weight, out):
-    acc = lax.dot_general(act[...], weight[...], NT, preferred_element_type=F32)
-    acc = acc + jnp.dot(attended[...], attn_weight[...], preferred_element_type=F32)
-    out[...] = acc.astype(BF16)
-
-
-def output_part(act, weight, attended, attn_weight, first, columns, step=256):
-    rows, units = act.shape
-    base = first // step
-    return pl.pallas_call(
-        output_kernel,
-        grid=(columns // step,),
-        out_shape=jax.ShapeDtypeStruct((rows, columns), BF16),
-        in_specs=[
-            pl.BlockSpec((rows, units), lambda i: (0, 0)),
-            pl.BlockSpec((step, units), lambda i: (base + i, 0)),
-            pl.BlockSpec((rows, attended.shape[1]), lambda i: (0, 0)),
-            pl.BlockSpec((attn_weight.shape[0], step), lambda i: (0, base + i)),
-        ],
-        out_specs=pl.BlockSpec((rows, step), lambda i: (0, i)),
-        compiler_params=pltpu.CompilerParams(vmem_limit_bytes=20 * MIB),
+        scratch_shapes=[pltpu.VMEM((columns, units), BF16), pltpu.VMEM((columns, attended.shape[1]), BF16)],
+        compiler_params=pltpu.CompilerParams(vmem_limit_bytes=24 * MIB),
         cost_estimate=cost(2 * rows * columns * (units + attended.shape[1]), 8 * MIB),
-    )(act, weight, attended, attn_weight)
-
-
-def finish_kernel(chunks, scalars, text, image, extra, mod_table, final_table, proj, *refs):
-    sums, (text_out, image_out, extra_out, velocity, hidden) = refs[: 3 * chunks], refs[3 * chunks :]
-    here, there, count = scalars[0], scalars[1], scalars[2]
-    width = text.shape[1] // chunks
+    )(ids, act, attended, attn_weight, *pieces)
+
+
+def split_three(first, second, third):
+    lane = lax.broadcasted_iota(jnp.int32, first.shape, 1)
+    return (
+        first,
+        jnp.where(lane < 32, pltpu.roll(first, 32, 1), pltpu.roll(second, 32, 1)),
+        jnp.where(lane < 64, pltpu.roll(second, 64, 1), pltpu.roll(third, 64, 1)),
+        pltpu.roll(third, 96, 1),
+    )
+
+
+def join_four(one, two, three, four):
+    lane = lax.broadcasted_iota(jnp.int32, one.shape, 1)
+    two, three, four = pltpu.roll(two, 96, 1), pltpu.roll(three, 64, 1), pltpu.roll(four, 32, 1)
+    return jnp.concatenate(
+        [jnp.where(lane < 96, one, two), jnp.where(lane < 64, two, three), jnp.where(lane < 32, three, four)], axis=1
+    )
+
+
+def finish_kernel(
+    chunks, ids, request_group, step_index, counts, slot_of, text, image, extra, mod_table, final_table, proj, *refs
+):
+    sums, (text_out, image_out, extra_out, velocity, hidden, parts) = refs[: 3 * chunks], refs[3 * chunks :]
+    here, there = steps_of(ids, request_group, step_index)
+    count = counts[ids[0] * 8 + ids[1]]
+    z, y = ids[0] // 4, ids[0] % 4
     rows_text, rows_image = text.shape[0], image.shape[0]
+    filled = 0
     for chunk in range(chunks):
         own, one, two = sums[3 * chunk : 3 * chunk + 3]
         total = own[...] + one[...].astype(F32) + two[...].astype(F32)
-        columns = slice(chunk * width, (chunk + 1) * width)
+        for half in range(total.shape[1] // 384):
+            tiles = [total[:, (3 * half + i) * 128 : (3 * half + i + 1) * 128] for i in range(3)]
+            for index, part in enumerate(split_three(*tiles)):
+                parts[filled + 4 * half + index] = part
+        filled += 4 * (total.shape[1] // 384)
+    width = 384
+    for pair in range(8):
+        found = []
+        for group in (2 * pair, 2 * pair + 1):
+            dz = lax.rem(group // 4 - z + 4, 4)
+            dy = lax.rem(group % 4 - y + 4, 4)
+            found += [parts[slot_of[part * 16 + dz * 4 + dy]] for part in range(2)]
+        total = join_four(*found)
+        columns = slice(pair * width, (pair + 1) * width)
         gate = mod_table[here, 2:3, columns]
         text_out[:, columns] = (text[:, columns].astype(F32) + gate * total[:rows_text]).astype(BF16)
         states = image[:, columns].astype(F32) + gate * total[rows_text : rows_text + rows_image]
@@ -394,6 +398,10 @@
 def finish(scalars, text, image, extra, mod_table, final_table, proj, sums):
     width = text.shape[1]
     flat = [part for chunk in sums for part in chunk]
+    slot_of = [0] * 32
+    for index, (part, dz, dy) in enumerate(place for chunk in LAYOUT for place in chunk):
+        slot_of[part * 16 + (dz % 4) * 4 + dy % 4] = index
+    rows = flat[0].shape[0]
     return pl.pallas_call(
         functools.partial(finish_kernel, len(sums)),
         out_shape=(
@@ -402,12 +410,12 @@
             jax.ShapeDtypeStruct(extra.shape, BF16),
             jax.ShapeDtypeStruct((image.shape[0], proj.shape[0]), F32),
         ),
-        in_specs=[SMEM] + [VMEM] * (6 + len(flat)),
+        in_specs=[SMEM] * 5 + [VMEM] * (6 + len(flat)),
         out_specs=(VMEM,) * 4,
-        scratch_shapes=[pltpu.VMEM((image.shape[0], width), F32)],
-        compiler_params=pltpu.CompilerParams(vmem_limit_bytes=16 * MIB),
+        scratch_shapes=[pltpu.VMEM((image.shape[0], width), F32), pltpu.VMEM((32, rows, 128), F32)],
+        compiler_params=pltpu.CompilerParams(vmem_limit_bytes=20 * MIB),
         cost_estimate=cost(1e7, 5 * MIB),
-    )(scalars, text, image, extra, mod_table, final_table, proj, *flat)
+    )(*scalars, jnp.array(slot_of, jnp.int32), text, image, extra, mod_table, final_table, proj, *flat)
 
 
 def smooth_kernel(columns, delta, above, middle, below, stencil, latent, out):
@@ -480,17 +488,44 @@
     member = lax.axis_index("narrow")
     z, y = group // 4, group % 4
     chip, core = member // 2, member % 2
-    step_here = step_index[request_group[group]]
-    step_extra = step_index[step_index.shape[0] - 1]
-    own_count = extra_counts[group * 8 + member]
-    scalars = jnp.stack([step_here, step_extra, own_count]).astype(jnp.int32)
+    ids = jnp.stack([group, member]).astype(jnp.int32)
+    scalars = (ids, request_group, step_index)
     text_own, image_own, extra_own = text_tokens[0], image_tokens[0], extra_tokens[0]
 
-    out_weight = lax.all_gather(mlp_out_weight.T, "wide", axis=0, tiled=True)
+    hidden_weight = lax.all_gather(mlp_in_weight, "wide", axis=0, tiled=True)
     own = modulate(scalars, text_own, image_own, extra_own, mod_table)
-    x = gather_rows(own)
-    half = mlp_in_weight.shape[0] // 2
-    pieces = collect(mlp_in_weight[:half], along_y, along_z) + collect(mlp_in_weight[half:], along_z, along_y)
+
+    together = lax.optimization_barrier
+    out_weight = mlp_out_weight.T
+    size = out_weight.shape[0] // 2
+    routes = ((along_y, along_z), (along_z, along_y))
+    mine = [out_weight[:size], out_weight[size:]]
+    near = [wide(mine[i], routes[i][0](step)) for i in range(2) for step in (1, -1)]
+    *near, own = together((*near, own))
+
+    def swap(block):
+        return lax.ppermute(block, "narrow", CORE_SWAP)
+
+    nxt = lax.ppermute(own, "narrow", chip_shift(-1))
+    prv = lax.ppermute(own, "narrow", chip_shift(1))
+    own_swapped = swap(own)
+    far = [wide(near[2 * i], routes[i][0](1)) for i in range(2)]
+    *far, nxt, prv, own_swapped = together((*far, nxt, prv, own_swapped))
+
+    cut = own.shape[0] // 2
+    far_a = lax.ppermute(nxt[:cut], "narrow", chip_shift(-1))
+    far_b = lax.ppermute(prv[cut:], "narrow", chip_shift(1))
+    near_swapped = swap(jnp.concatenate([nxt, prv], axis=0))
+    low = [jnp.concatenate([mine[i], near[2 * i]], axis=0) for i in range(2)]
+    high = [jnp.concatenate([near[2 * i + 1], far[i]], axis=0) for i in range(2)]
+    early = [wide(low[0], routes[0][1](1)), wide(high[0], routes[0][1](-1))]
+    far_a, far_b, near_swapped, low[1], high[1] = together((far_a, far_b, near_swapped, low[1], high[1]))
+    across = jnp.concatenate([far_a, far_b], axis=0)
+    early += [wide(low[1], routes[1][1](1)), wide(high[1], routes[1][1](-1))]
+    rows = own.shape[0]
+    x = jnp.concatenate(
+        [own, nxt, across, prv, own_swapped, near_swapped[:rows], swap(across), near_swapped[rows:]], axis=0
+    )
 
     block_ids = jnp.arange(8, dtype=jnp.int32)
     sources = ((chip + block_ids % 4) % 4) * 2 + (core ^ (block_ids // 4))
@@ -506,12 +541,29 @@
     )
 
     heads, slots = extra_heads.shape[1], extra_heads.shape[2]
+    extra_heads, *early = together((extra_heads, *early))
     shared = extra_heads[1:].reshape(1, 2 * heads, slots, 128)
-    before, after, far_first, far_last = ring(shared, along_y, lambda b: b[:, :heads], lambda b: b[:, heads:])
-    far = jnp.concatenate([far_first, far_last], axis=1)
-    quad = jnp.concatenate([shared, before, after, far], axis=0)
-    key_pieces = (quad,) + ring(quad, along_z, lambda b: b[:2], lambda b: b[2:])
+    before, after = wide(shared, along_y(1)), wide(shared, along_y(-1))
+
+    def rest(i):
+        ahead = jnp.concatenate([high[i], early[2 * i]], axis=0)
+        back = jnp.concatenate([low[i], early[2 * i + 1]], axis=0)
+        return ahead, back
+
+    ahead, back = rest(1)
+    before, after, ahead, back = together((before, after, ahead, back))
+    first, second = wide(before[:, :heads], along_y(1)), wide(after[:, heads:], along_y(-1))
+    late = [[wide(ahead, routes[1][1](1)), wide(back, routes[1][1](-1))]]
     attended = attend_request(request_heads)
+    key_quad = jnp.concatenate([shared, before, after, jnp.concatenate([first, second], axis=1)], axis=0)
+    above, below = wide(key_quad, along_z(1)), wide(key_quad, along_z(-1))
+    ahead, back = rest(0)
+    above, below, ahead, back, x, attended = together((above, below, ahead, back, x, attended))
+    first, second = wide(above[:2], along_z(1)), wide(below[2:], along_z(-1))
+    late.append([wide(ahead, routes[0][1](1)), wide(back, routes[0][1](-1))])
+    act = hidden_units(x, hidden_weight)
+    act, first, second = together((act, first, second))
+    key_pieces = (key_quad, above, below, first, second)
     order = jnp.array(RING_ORDER, jnp.int32)
     groups = ((z + order) % 4)[:, None] * 4 + ((y + order) % 4)[None, :]
     owners = groups.reshape(16, 1) * 8 + sources[None, :]
@@ -522,20 +574,17 @@
     live = (slot_ids[None, :] < counts[:, None]).astype(F32).reshape(1, -1)
     attended = attend_extra(extra_heads, live, attended, key_pieces, 8)
 
-    act = hidden_units(jnp.stack([z, y]).astype(jnp.int32), x, pieces)
-    chunks = 3
-    columns = out_weight.shape[0] // chunks
-    sums = []
-    for chunk in range(chunks):
-        part = output_part(act, out_weight, attended, attn_out_weight, chunk * columns, columns)
-        sums.append(scatter_sum(part))
+    attn_weight = attn_out_weight.T
+    chunks = [low[:1] + high[:1] + low[1:] + high[1:] + early] + late
+    sums = [scatter_sum(output_part(i, ids, act, attended, attn_weight, pieces)) for i, pieces in enumerate(chunks)]
     text_out, image_out, extra_out, velocity = finish(
-        scalars, text_own, image_own, extra_own, mod_table, final_table, proj_weight.T, sums
+        (*scalars, extra_counts), text_own, image_own, extra_own, mod_table, final_table, proj_weight.T, sums
     )
     channels = proj_weight.shape[1]
     grid_width = latent.shape[2] // channels
     above = lax.ppermute(velocity[-grid_width:], "narrow", [(i, i + 1) for i in range(7)])
     below = lax.ppermute(velocity[:grid_width], "narrow", [(i + 1, i) for i in range(7)])
+    step_here = step_index[request_group[group]]
     delta = (noise_level(step_here + 1) - noise_level(step_here)).reshape(1)
     latent_next = smooth(
         delta, above, velocity, below, stencil, latent[0].reshape(-1, channels), grid_width

time: 283 us -> 245 us (0.87)
  waiting for transfers between devices: 93.9 us -> 69.2 us
  local copies, waits for them, and re-layouts: 41.1 us -> 22.6 us
  other arithmetic: 6.72 us -> 12 us
    ppermute x33 -> x29, waiting for transfers between devices: 81.6 us -> 54.3 us  [the longest x22 49.8 us: wide(): return lax.ppermute(block, 'wide', pairs)]
    slice x15 -> x7, local copies, waits for them, and re-layouts: 12.9 us -> 3.69 us  [the longest x1 1.84 us: per_device(): mine = [out_weight[:size], out_weight[size:]]]
    concatenate x1 -> x8, other arithmetic: 0.08 us -> 7.79 us  [the longest x2 4.15 us: rest(): ahead = jnp.concatenate([high[i], early[2 * i]], axis=0)]
    unnamed x88 -> x131, local copies, waits for them, and re-layouts: 18.7 us -> 12.9 us
    ppermute x3, waiting for transfers between devices: 0.01 us -> 5.86 us  [scatter_sum(): from_prv = lax.ppermute(far[:, :half], 'narrow', chip_shift(1)).astype(F32)]
    ppermute x33 -> x29, starting transfers between devices: 37.3 us -> 38.3 us  [the longest x22 29.6 us: wide(): return lax.ppermute(block, 'wide', pairs)]
  transfers between devices with their start and end apart: 51 -> 47, of which waited for: 21 -> 12; matrix products, arithmetic and copies ran while one was open for 13% -> 10% of each run, Pallas kernels for 17% -> 21%
where the time goes in v2:
time: 245 us; the launch traced here: 244 us
  waiting for transfers between devices  69.2 us (28%)
  starting transfers between devices  65.6 us (27%)
  Pallas kernels  55.9 us (23%)
  local copies, waits for them, and re-layouts  22.6 us (9%)
  between operations  18.6 us (8%)
  other arithmetic  12 us (5%)
    ppermute x22, waiting for transfers between devices, wide(): return lax.ppermute(block, 'wide', pairs)  49.8 us
    ppermute x22, starting transfers between devices, wide(): return lax.ppermute(block, 'wide', pairs)  29.6 us
    pallas_call x3, Pallas kernels, output_part(): pl.pallas_call(functools.partial(output_kernel, chunk), out_shape=jax.Sha...  18.5 us
    pallas_call x1, Pallas kernels, project_heads(): pl.pallas_call(functools.partial(heads_kernel, blocks, own), grid=(3,), o...  14 us
    unnamed x131, local copies, waits for them, and re-layouts  12.9 us
    pallas_call x1, Pallas kernels, hidden_units(): pl.pallas_call(hidden_kernel, grid=(units // step,), out_shape=jax.ShapeD...  11.9 us
    ppermute x3, waiting for transfers between devices, scatter_sum(): two = lax.ppermute(to_prv, 'narrow', chip_shift(-1))  7.41 us
    ppermute x3, starting transfers between devices, scatter_sum(): from_nxt = lax.ppermute(far[:, half:], 'narrow', chip_shift(-1)).astype(F32)  7.21 us
  transfers between devices with their start and end apart: 47, of which 12 were waited for; matrix products, arithmetic and copies ran while one was open for 10% of the time, Pallas kernels for 21%

profile of v2, /device:TPU:1, one launch (start us, length us, event | category | flops | bytes accessed | tf_op | source)
XLA Modules:
  0.0 243.9 jit_solution(4085693376764750102)
XLA Ops:
  7.9 1.8 fusion.21
  9.8 2.1 collective-permute-start
  11.9 1.4 collective-permute-start.1
  13.4 1.6 collective-permute-start.2
  15.0 2.1 collective-permute-start.3
  19.4 1.0 concatenate.78
  20.6 1.1 shard_map.246
  21.7 1.9 collective-permute-done.2
  23.6 2.5 %collective-permute-start.6 = (bf16[112,3072]{1,0:T(8,128)(2,1)S(1)}, bf16[112,3072]{1,0:T(8,128)(2,1)S(1)}, u32[]{:S(2)}, u32[]{:S(2)}) collective-permute-start(bf16[112,3072]{1,0:T(8,128)(2,1)S(1)} %shard_map.246), channel_id=1, source_target_pairs={{0,6},{1,7},{2,0},{3,1},{4,2},{5,3},{6,4},{7,5},{8,14},{9,15},{10,... | collective-permute-start | bytes 2064392 | tf_op jit(solution)/shard_map/ppermute | solution.py:509
  26.1 2.1 collective-permute-start.8
  28.2 1.6 sine_multiply_fusion
  29.9 1.0 collective-permute-start.5
  30.9 1.1 pad_maximum_fusion.6.refs_2_
  32.1 1.2 pad_maximum_fusion.8.refs_0_
  33.3 11.9 %collective-permute-done.4 = bf16[96,1536]{1,0:T(8,128)(2,1)S(1)} collective-permute-done((bf16[96,1536]{1,0:T(8,128)(2,1)}, bf16[96,1536]{1,0:T(8,128)(2,1)S(1)}, u32[]{:S(2)}, u32[]{:S(2)}) %collective-permute-start.4) | collective-permute-done | bytes 294944 | tf_op jit(solution)/shard_map/ppermute | solution.py:60
  46.3 1.2 collective-permute-start.10
  47.5 1.6 collective-permute-start.9
  49.1 2.6 %collective-permute-start.14 = (bf16[192,1536]{1,0:T(8,128)(2,1)S(1)}, bf16[192,1536]{1,0:T(8,128)(2,1)S(1)}, u32[]{:S(2)}, u32[]{:S(2)}) collective-permute-start(bf16[192,1536]{1,0:T(8,128)(2,1)S(1)} %constant_dynamic-update-slice_fusion.7.refs_1_), channel_id=1, source_target_pairs={{0,96},{8,104},{16,112},{24,120},{32,0},{40,8},{48,16},{56,24},{64... | collective-permute-start | bytes 1769480 | tf_op jit(solution)/shard_map/ppermute | solution.py:60
  51.7 1.1 pad_maximum_fusion.7.refs_3_
  52.9 4.5 %collective-permute-done.10 = bf16[56,3072]{1,0:T(8,128)(2,1)S(1)} collective-permute-done((bf16[56,3072]{1,0:T(8,128)(2,1)S(1)}, bf16[56,3072]{1,0:T(8,128)(2,1)S(1)}, u32[]{:S(2)}, u32[]{:S(2)}) %collective-permute-start.10) | collective-permute-done | bytes 344096 | tf_op jit(solution)/shard_map/ppermute | solution.py:517
  58.6 2.3 collective-permute-start.16
  61.3 2.8 %slice-done.1 = s8[2883584]{0:T(1024)(128)(4,1)S(1)} async-done(((s8[7077888]{0:T(1024)(128)(4,1)}), s8[2883584]{0:T(1024)(128)(4,1)S(1)}, s32[]{:S(2)}) %slice-start.1) | async-done | bytes 2883608
  64.1 14.0 %shard_map.247 = (bf16[3,3,768,128]{3,2,1,0:T(8,128)(2,1)S(1)}, bf16[3,3,128,128]{3,2,1,0:T(8,128)(2,1)S(1)}) custom-call(bf16[896,3072]{1,0:T(8,128)(2,1)S(1)} %slice_dynamic-update-slice_fusion.x, bf16[3,3072,384]{2,1,0:T(8,128)(2,1)S(1)} %bitcast.26, f32[2,128]{1,0:T(2,128)S(1)} %pad_maximum_fusion.15.gains, f32[896,128]{1,0:T(8,128)S(1)} %get-tuple-element.109.cosine, ...), custom_call_target="tpu_custom_call" | custom-call | flops 6341787648 | bytes 16777216 | tf_op jit(solution)/shard_map/pallas_call | solution.py:184
  78.1 9.2 %collective-permute-done.15.refs_6_ = bf16[192,1536]{1,0:T(8,128)(2,1)S(1)} collective-permute-done((bf16[192,1536]{1,0:T(8,128)(2,1)S(1)}, bf16[192,1536]{1,0:T(8,128)(2,1)S(1)}, u32[]{:S(2)}, u32[]{:S(2)}) %collective-permute-start.15) | collective-permute-done | bytes 589856 | tf_op jit(solution)/shard_map/ppermute | solution.py:60
  87.6 2.7 %collective-permute-start.18 = (bf16[1,6,128,128]{3,2,1,0:T(8,128)(2,1)S(1)}, bf16[1,6,128,128]{3,2,1,0:T(8,128)(2,1)S(1)}, u32[]{:S(2)}, u32[]{:S(2)}) collective-permute-start(bf16[1,6,128,128]{3,2,1,0:T(8,128)(2,1)S(1)} %bitcast.28), channel_id=1, source_target_pairs={{0,24},{8,0},{16,8},{24,16},{32,56},{40,32},{48,40},{56,48},{64,88... | collective-permute-start | bytes 589832 | tf_op jit(solution)/shard_map/ppermute | solution.py:60
  90.3 1.6 pad_maximum_fusion.1
  91.9 7.7 %collective-permute-done.17 = bf16[1,6,128,128]{3,2,1,0:T(8,128)(2,1)S(1)} collective-permute-done((bf16[1,6,128,128]{3,2,1,0:T(8,128)(2,1)S(1)}, bf16[1,6,128,128]{3,2,1,0:T(8,128)(2,1)S(1)}, u32[]{:S(2)}, u32[]{:S(2)}) %collective-permute-start.17) | collective-permute-done | bytes 196640 | tf_op jit(solution)/shard_map/ppermute | solution.py:60
  100.4 2.1 collective-permute-start.20
  102.4 4.8 %collective-permute-done.19 = bf16[1,3,128,128]{3,2,1,0:T(8,128)(2,1)S(1)} collective-permute-done((bf16[1,3,128,128]{3,2,1,0:T(8,128)(2,1)S(1)}, bf16[1,3,128,128]{3,2,1,0:T(8,128)(2,1)S(1)}, u32[]{:S(2)}, u32[]{:S(2)}) %collective-permute-start.19) | collective-permute-done | bytes 98336 | tf_op jit(solution)/shard_map/ppermute | solution.py:60
  107.3 0.9 collective-permute-start.21
  108.3 1.8 collective-permute-start.22
  110.8 2.9 %shard_map.248.done = bf16[768,384]{1,0:T(8,128)(2,1)S(1)} custom-call(bf16[3,3,768,128]{3,2,1,0:T(8,128)(2,1)S(1)} %get-tuple-element.66.query.keys.values, bf16[3,3,768,128]{3,2,1,0:T(8,128)(2,1)S(1)} %get-tuple-element.66.query.keys.values, bf16[3,3,768,128]{3,2,1,0:T(8,128)(2,1)S(1)} %get-tuple-element.66.query.keys.values), custom_call_target="tpu_custom_call" | custom-call | flops 905969664 | bytes 5242880 | tf_op jit(solution)/shard_map/pallas_call | solution.py:229
  113.6 0.8 copy-done
  114.5 2.6 %pad_maximum_fusion.3 = (bf16[384,1536]{1,0:T(8,128)(2,1)}, bf16[384,1536]{1,0:T(8,128)(2,1)}) fusion(bf16[192,1536]{1,0:T(8,128)(2,1)S(1)} %copy-done.14, bf16[96,1536]{1,0:T(8,128)(2,1)S(1)} %copy-done.43, bf16[96,1536]{1,0:T(8,128)(2,1)S(1)} %copy-done.41, bf16[192,1536]{1,0:T(8,128)(2,1)S(1)} %copy-done.17, bf16[96,1536]{1,0:T(8,128)(2,1)} %collective-permute-done, ...), kind=kLoop, calls=%fused_computation.6 | loop fusion | flops 7077888 | bytes 4718592 | tf_op jit(solution)/shard_map/concatenate | solution.py:549
  117.1 8.2 %collective-permute-done.21.refs_1_.refs_6_ = bf16[4,6,128,128]{3,2,1,0:T(8,128)(2,1)S(1)} collective-permute-done((bf16[4,6,128,128]{3,2,1,0:T(8,128)(2,1)S(1)}, bf16[4,6,128,128]{3,2,1,0:T(8,128)(2,1)S(1)}, u32[]{:S(2)}, u32[]{:S(2)}) %collective-permute-start.21) | collective-permute-done | bytes 786464 | tf_op jit(solution)/shard_map/ppermute | solution.py:60
  126.2 1.3 collective-permute-start.37
  127.5 1.4 collective-permute-start.38
  129.3 2.7 %collective-permute-start.31 = (bf16[384,1536]{1,0:T(8,128)(2,1)}, bf16[384,1536]{1,0:T(8,128)(2,1)}, u32[]{:S(2)}, u32[]{:S(2)}) collective-permute-start(bf16[384,1536]{1,0:T(8,128)(2,1)} %get-tuple-element.75), channel_id=1, source_target_pairs={{0,24},{8,0},{16,8},{24,16},{32,56},{40,32},{48,40},{56,48},{64,88... | collective-permute-start | bytes 3538952 | tf_op jit(solution)/shard_map/ppermute | solution.py:60
  132.1 4.3 %copy.34 = bf16[384,3072]{0,1:T(8,128)(2,1)} copy(bf16[384,3072]{1,0:T(8,128)(2,1)} %param.37) | data formatting | bytes 4718592 | tf_op args[14]
  136.4 1.8 slice.181
  138.2 1.1 collective-permute-start.24
  139.3 2.6 %copy-done.33 = bf16[896,3072]{1,0:T(8,128)(2,1)S(1)} copy-done((bf16[896,3072]{1,0:T(8,128)(2,1)S(1)}, bf16[896,3072]{1,0:T(8,128)(2,1)}, u32[]{:S(2)}) %copy-start.33) | copy-done | bytes 5505048
  141.9 11.9 %shard_map.249.act = bf16[896,1536]{1,0:T(8,128)(2,1)S(1)} custom-call(bf16[896,3072]{1,0:T(8,128)(2,1)S(1)} %copy-done.33, bf16[3072,1536]{1,0:T(8,128)(2,1)} %all-gather.2.cloned.1.call-done.weight), custom_call_target="tpu_custom_call" | custom-call | flops 8455716864 | bytes 18874368 | tf_op jit(solution)/shard_map/pallas_call | solution.py:290
  153.8 5.9 %collective-permute-done.24.refs_4_.refs_9_ = bf16[2,6,128,128]{3,2,1,0:T(8,128)(2,1)S(1)} collective-permute-done((bf16[2,6,128,128]{3,2,1,0:T(8,128)(2,1)}, bf16[2,6,128,128]{3,2,1,0:T(8,128)(2,1)S(1)}, u32[]{:S(2)}, u32[]{:S(2)}) %collective-permute-start.24) | collective-permute-done | bytes 393248 | tf_op jit(solution)/shard_map/ppermute | solution.py:60
  159.6 3.2 %shard_map.250.attended = bf16[896,384]{1,0:T(8,128)(2,1)S(1)} custom-call(bf16[3,3,128,128]{3,2,1,0:T(8,128)(2,1)S(1)} %copy-done.10, f32[1,2048]{1,0:T(1,128)S(1)} %reshape.232.live, bf16[768,384]{1,0:T(8,128)(2,1)S(1)} %copy-done.1, bf16[4,6,128,128]{3,2,1,0:T(8,128)(2,1)S(1)} %maximum_maximum_fusion.refs_0_.refs_5_, ...), custom_call_target="tpu_custom_call" | custom-call | flops 402653184 | bytes 5242880 | tf_op jit(solution)/shard_map/pallas_call | solution.py:261
  162.9 5.3 %shard_map.253 = bf16[896,768]{1,0:T(8,128)(2,1)S(1)} custom-call(s32[2]{0:T(128)S(1)} %pad_add_fusion.1.ids, bf16[896,1536]{1,0:T(8,128)(2,1)S(1)} %shard_map.249.act, bf16[896,384]{1,0:T(8,128)(2,1)S(1)} %shard_map.250.attended, bf16[3072,384]{1,0:T(8,128)(2,1)S(1)} %bitcast.15, bf16[384,1536]{1,0:T(8,128)(2,1)} %collective-permute-done.37.refs_0_, ...), custom_call_target="tpu_custom_call" | custom-call | flops 2642411520 | bytes 8388608 | tf_op jit(solution)/shard_map/pallas_call | solution.py:329
  168.4 4.9 %collective-permute-start.39 = (bf16[448,768]{1,0:T(8,128)(2,1)S(1)}, bf16[448,768]{1,0:T(8,128)(2,1)S(1)}, u32[]{:S(2)}, u32[]{:S(2)}) collective-permute-start(bf16[448,768]{1,0:T(8,128)(2,1)S(1)} %slice.235), channel_id=1, source_target_pairs={{0,1},{1,0},{2,3},{3,2},{4,5},{5,4},{6,7},{7,6},{8,9},{9,8},{10,11... | collective-permute-start | bytes 2064392 | tf_op jit(solution)/shard_map/ppermute | solution.py:80
  173.3 5.3 %shard_map.252 = bf16[896,768]{1,0:T(8,128)(2,1)S(1)} custom-call(s32[2]{0:T(128)S(1)} %pad_add_fusion.1.ids, bf16[896,1536]{1,0:T(8,128)(2,1)S(1)} %shard_map.249.act, bf16[896,384]{1,0:T(8,128)(2,1)S(1)} %shard_map.250.attended, bf16[3072,384]{1,0:T(8,128)(2,1)S(1)} %bitcast.16, bf16[384,1536]{1,0:T(8,128)(2,1)} %collective-permute-done.30.refs_0_, ...), custom_call_target="tpu_custom_call" | custom-call | flops 2642411520 | bytes 8388608 | tf_op jit(solution)/shard_map/pallas_call | solution.py:329
  179.2 7.9 %shard_map.251 = bf16[896,1536]{1,0:T(8,128)(2,1)S(1)} custom-call(s32[2]{0:T(128)S(1)} %pad_add_fusion.1.ids, bf16[896,1536]{1,0:T(8,128)(2,1)S(1)} %shard_map.249.act, bf16[896,384]{1,0:T(8,128)(2,1)S(1)} %shard_map.250.attended, bf16[3072,384]{1,0:T(8,128)(2,1)S(1)} %bitcast.17, bf16[192,1536]{1,0:T(8,128)(2,1)S(1)} %copy-done.24, ...), custom_call_target="tpu_custom_call" | custom-call | flops 5284823040 | bytes 8388608 | tf_op jit(solution)/shard_map/pallas_call | solution.py:329
  187.8 1.0 collective-permute-start.40
  188.8 1.8 collective-permute-start.42
  191.0 2.7 %collective-permute-start.35 = (bf16[112,384]{1,0:T(8,128)(2,1)S(1)}, bf16[112,384]{1,0:T(8,128)(2,1)S(1)}, u32[]{:S(2)}, u32[]{:S(2)}) collective-permute-start(bf16[112,384]{1,0:T(8,128)(2,1)S(1)} %get-tuple-element.103), channel_id=1, source_target_pairs={{0,6},{1,7},{2,0},{3,1},{4,2},{5,3},{6,4},{7,5},{8,14},{9,15},{10,... | collective-permute-start | bytes 258056 | tf_op jit(solution)/shard_map/ppermute | solution.py:84
  193.7 2.0 collective-permute-start.43
  196.5 2.7 %collective-permute-start.28 = (bf16[112,768]{1,0:T(8,128)(2,1)S(1)}, bf16[112,768]{1,0:T(8,128)(2,1)S(1)}, u32[]{:S(2)}, u32[]{:S(2)}) collective-permute-start(bf16[112,768]{1,0:T(8,128)(2,1)S(1)} %get-tuple-element.95), channel_id=1, source_target_pairs={{0,6},{1,7},{2,0},{3,1},{4,2},{5,3},{6,4},{7,5},{8,14},{9,15},{10,... | collective-permute-start | bytes 516104 | tf_op jit(solution)/shard_map/ppermute | solution.py:84
  199.2 5.8 %collective-permute-done.26 = bf16[112,768]{1,0:T(8,128)(2,1)S(1)} collective-permute-done((bf16[112,768]{1,0:T(8,128)(2,1)S(1)}, bf16[112,768]{1,0:T(8,128)(2,1)S(1)}, u32[]{:S(2)}, u32[]{:S(2)}) %collective-permute-start.26) | collective-permute-done | bytes 172064 | tf_op jit(solution)/shard_map/ppermute | solution.py:83
  205.3 1.5 collective-permute-start.27
  206.9 1.3 collective-permute-start.36
  208.7 7.4 %collective-permute-done.36.refs_5_ = bf16[112,768]{1,0:T(8,128)(2,1)S(1)} collective-permute-done((bf16[112,768]{1,0:T(8,128)(2,1)S(1)}, bf16[112,768]{1,0:T(8,128)(2,1)S(1)}, u32[]{:S(2)}, u32[]{:S(2)}) %collective-permute-start.36) | collective-permute-done | bytes 172064 | tf_op jit(solution)/shard_map/ppermute | solution.py:90
  216.1 0.9 collective-permute-done.34.refs_4_
  217.1 2.9 %shard_map.254 = (bf16[32,3072]{1,0:T(8,128)(2,1)}, bf16[64,3072]{1,0:T(8,128)(2,1)}, bf16[16,3072]{1,0:T(8,128)(2,1)}, f32[64,64]{1,0:T(8,128)S(1)}) custom-call(s32[2]{0:T(128)S(1)} %pad_add_fusion.1.ids, s32[16]{0:T(128)S(1)} %copy-done.34, s32[17]{0:T(128)S(1)} %copy-done.35, s32[128]{0:T(128)S(1)} %copy-done.36, s32[32]{0:T(128)S(1)} %copy-done.37, ...), custom_call_target="tpu_custom_call" | custom-call | flops 10000000 | bytes 5242880 | tf_op jit(solution)/shard_map/pallas_call | solution.py:405
  220.0 5.8 %collective-permute-start.44 = (f32[32,64]{1,0:T(8,128)S(1)}, f32[32,64]{1,0:T(8,128)S(1)}, u32[]{:S(2)}, u32[]{:S(2)}) collective-permute-start(f32[32,64]{1,0:T(8,128)S(1)} %get-tuple-element.111), channel_id=1, source_target_pairs={{0,1},{1,2},{2,3},{3,4},{4,5},{5,6},{6,7},{8,9},{9,10},{10,11},{11... | collective-permute-start | bytes 24584 | tf_op jit(solution)/shard_map/ppermute | solution.py:585
  225.7 1.9 collective-permute-start.45
  234.1 1.5 shard_map.255
  235.6 1.4 reshape.231
  (249 shorter events, 15.2 us)
Async XLA Ops:
  7.2 132.1 %all-gather.2.cloned.1.call-start = ((), (), s32[]{:S(2)}) async-start(), calls=%async_computation | async-start | bytes 10027008 | tf_op jit(solution)/shard_map/all_gather | solution.py:495
  9.8 22.3 %copy-start.38 = (bf16[96,1536]{1,0:T(8,128)(2,1)}, bf16[96,1536]{1,0:T(8,128)(2,1)S(1)}, u32[]{:S(2)}) copy-start(bf16[96,1536]{1,0:T(8,128)(2,1)S(1)} %get-tuple-element.107) | copy-start | bytes 884740
  9.8 11.9 %collective-permute-start = (bf16[96,1536]{1,0:T(8,128)(2,1)S(1)}, bf16[96,1536]{1,0:T(8,128)(2,1)}, u32[]{:S(2)}, u32[]{:S(2)}) collective-permute-start(bf16[96,1536]{1,0:T(8,128)(2,1)S(1)} %get-tuple-element.107), channel_id=1, source_target_pairs={{0,8},{8,16},{16,24},{24,0},{32,40},{40,48},{48,56},{56,32},{64,72... | collective-permute-start | bytes 884744 | tf_op jit(solution)/shard_map/ppermute | solution.py:60
  11.9 9.8 %collective-permute-start.1 = (bf16[96,1536]{1,0:T(8,128)(2,1)S(1)}, bf16[96,1536]{1,0:T(8,128)(2,1)S(1)}, u32[]{:S(2)}, u32[]{:S(2)}) collective-permute-start(bf16[96,1536]{1,0:T(8,128)(2,1)S(1)} %get-tuple-element.107), channel_id=1, source_target_pairs={{0,24},{8,0},{16,8},{24,16},{32,56},{40,32},{48,40},{56,48},{64,88... | collective-permute-start | bytes 884744 | tf_op jit(solution)/shard_map/ppermute | solution.py:60
  13.4 10.2 %collective-permute-start.2 = (bf16[96,1536]{1,0:T(8,128)(2,1)}, bf16[96,1536]{1,0:T(8,128)(2,1)}, u32[]{:S(2)}, u32[]{:S(2)}) collective-permute-start(bf16[96,1536]{1,0:T(8,128)(2,1)} %get-tuple-element.106), channel_id=1, source_target_pairs={{0,32},{8,40},{16,48},{24,56},{32,64},{40,72},{48,80},{56,88},{64,... | collective-permute-start | bytes 884744 | tf_op jit(solution)/shard_map/ppermute | solution.py:60
  15.0 8.6 %collective-permute-start.3 = (bf16[96,1536]{1,0:T(8,128)(2,1)}, bf16[96,1536]{1,0:T(8,128)(2,1)}, u32[]{:S(2)}, u32[]{:S(2)}) collective-permute-start(bf16[96,1536]{1,0:T(8,128)(2,1)} %get-tuple-element.106), channel_id=1, source_target_pairs={{0,96},{8,104},{16,112},{24,120},{32,0},{40,8},{48,16},{56,24},{64... | collective-permute-start | bytes 884744 | tf_op jit(solution)/shard_map/ppermute | solution.py:60
  21.7 24.5 %copy-start.40 = (bf16[96,1536]{1,0:T(8,128)(2,1)}, bf16[96,1536]{1,0:T(8,128)(2,1)S(1)}, u32[]{:S(2)}) copy-start(bf16[96,1536]{1,0:T(8,128)(2,1)S(1)} %collective-permute-done.1) | copy-start | bytes 884740
  23.6 21.8 %collective-permute-start.6 = (bf16[112,3072]{1,0:T(8,128)(2,1)S(1)}, bf16[112,3072]{1,0:T(8,128)(2,1)S(1)}, u32[]{:S(2)}, u32[]{:S(2)}) collective-permute-start(bf16[112,3072]{1,0:T(8,128)(2,1)S(1)} %shard_map.246), channel_id=1, source_target_pairs={{0,6},{1,7},{2,0},{3,1},{4,2},{5,3},{6,4},{7,5},{8,14},{9,15},{10,... | collective-permute-start | bytes 2064392 | tf_op jit(solution)/shard_map/ppermute | solution.py:509
  26.1 19.3 %collective-permute-start.7 = (bf16[112,3072]{1,0:T(8,128)(2,1)S(1)}, bf16[112,3072]{1,0:T(8,128)(2,1)S(1)}, u32[]{:S(2)}, u32[]{:S(2)}) collective-permute-start(bf16[112,3072]{1,0:T(8,128)(2,1)S(1)} %shard_map.246), channel_id=1, source_target_pairs={{0,2},{1,3},{2,4},{3,5},{4,6},{5,7},{6,0},{7,1},{8,10},{9,11},{10,... | collective-permute-start | bytes 2064392 | tf_op jit(solution)/shard_map/ppermute | solution.py:510
  26.1 19.3 %collective-permute-start.8 = (bf16[112,3072]{1,0:T(8,128)(2,1)S(1)}, bf16[112,3072]{1,0:T(8,128)(2,1)S(1)}, u32[]{:S(2)}, u32[]{:S(2)}) collective-permute-start(bf16[112,3072]{1,0:T(8,128)(2,1)S(1)} %shard_map.246), channel_id=1, source_target_pairs={{0,1},{1,0},{2,3},{3,2},{4,5},{5,4},{6,7},{7,6},{8,9},{9,8},{10,11... | collective-permute-start | bytes 2064392 | tf_op jit(solution)/shard_map/ppermute | solution.py:507
  29.8 15.3 %collective-permute-start.4 = (bf16[96,1536]{1,0:T(8,128)(2,1)}, bf16[96,1536]{1,0:T(8,128)(2,1)S(1)}, u32[]{:S(2)}, u32[]{:S(2)}) collective-permute-start(bf16[96,1536]{1,0:T(8,128)(2,1)} %collective-permute-done), channel_id=1, source_target_pairs={{0,8},{8,16},{16,24},{24,0},{32,40},{40,48},{48,56},{56,32},{64,72... | collective-permute-start | bytes 884744 | tf_op jit(solution)/shard_map/ppermute | solution.py:60
  29.9 15.5 %collective-permute-start.5 = (bf16[96,1536]{1,0:T(8,128)(2,1)}, bf16[96,1536]{1,0:T(8,128)(2,1)S(1)}, u32[]{:S(2)}, u32[]{:S(2)}) collective-permute-start(bf16[96,1536]{1,0:T(8,128)(2,1)} %collective-permute-done.2), channel_id=1, source_target_pairs={{0,32},{8,40},{16,48},{24,56},{32,64},{40,72},{48,80},{56,88},{64,... | collective-permute-start | bytes 884744 | tf_op jit(solution)/shard_map/ppermute | solution.py:60
  32.0 58.2 %copy-start.2 = (bf16[192,1536]{1,0:T(8,128)(2,1)}, bf16[192,1536]{1,0:T(8,128)(2,1)S(1)}, u32[]{:S(2)}) copy-start(bf16[192,1536]{1,0:T(8,128)(2,1)S(1)} %pad_maximum_fusion.6.refs_2_) | copy-start | bytes 1769476
  45.1 33.0 %collective-permute-start.13 = (bf16[192,1536]{1,0:T(8,128)(2,1)S(1)}, bf16[192,1536]{1,0:T(8,128)(2,1)S(1)}, u32[]{:S(2)}, u32[]{:S(2)}) collective-permute-start(bf16[192,1536]{1,0:T(8,128)(2,1)S(1)} %pad_maximum_fusion.8.refs_0_), channel_id=1, source_target_pairs={{0,32},{8,40},{16,48},{24,56},{32,64},{40,72},{48,80},{56,88},{64,... | collective-permute-start | bytes 1769480 | tf_op jit(solution)/shard_map/ppermute | solution.py:60
  45.5 11.9 %collective-permute-start.11 = (bf16[224,3072]{1,0:T(8,128)(2,1)S(1)}, bf16[224,3072]{1,0:T(8,128)(2,1)S(1)}, u32[]{:S(2)}, u32[]{:S(2)}) collective-permute-start(bf16[224,3072]{1,0:T(8,128)(2,1)S(1)} %pad_maximum_fusion), channel_id=1, source_target_pairs={{0,1},{1,0},{2,3},{3,2},{4,5},{5,4},{6,7},{7,6},{8,9},{9,8},{10,11... | collective-permute-start | bytes 4128776 | tf_op jit(solution)/shard_map/ppermute | solution.py:507
  46.2 15.0 %slice-start = ((s8[7077888]{0:T(1024)(128)(4,1)}), s8[4194304]{0:T(1024)(128)(4,1)S(1)}, s32[]{:S(2)}) async-start(s8[7077888]{0:T(1024)(128)(4,1)} %bitcast.25), calls=%async_computation.1 | async-start | bytes 8388608
  46.3 11.1 %collective-permute-start.10 = (bf16[56,3072]{1,0:T(8,128)(2,1)S(1)}, bf16[56,3072]{1,0:T(8,128)(2,1)S(1)}, u32[]{:S(2)}, u32[]{:S(2)}) collective-permute-start(bf16[56,3072]{1,0:T(8,128)(2,1)S(1)} %slice.171), channel_id=1, source_target_pairs={{0,2},{1,3},{2,4},{3,5},{4,6},{5,7},{6,0},{7,1},{8,10},{9,11},{10,... | collective-permute-start | bytes 1032200 | tf_op jit(solution)/shard_map/ppermute | solution.py:517
  47.5 9.9 %collective-permute-start.9 = (bf16[56,3072]{1,0:T(8,128)(2,1)S(1)}, bf16[56,3072]{1,0:T(8,128)(2,1)S(1)}, u32[]{:S(2)}, u32[]{:S(2)}) collective-permute-start(bf16[56,3072]{1,0:T(8,128)(2,1)S(1)} %slice.170), channel_id=1, source_target_pairs={{0,6},{1,7},{2,0},{3,1},{4,2},{5,3},{6,4},{7,5},{8,14},{9,15},{10,... | collective-permute-start | bytes 1032200 | tf_op jit(solution)/shard_map/ppermute | solution.py:516
  49.1 29.0 %collective-permute-start.14 = (bf16[192,1536]{1,0:T(8,128)(2,1)S(1)}, bf16[192,1536]{1,0:T(8,128)(2,1)S(1)}, u32[]{:S(2)}, u32[]{:S(2)}) collective-permute-start(bf16[192,1536]{1,0:T(8,128)(2,1)S(1)} %constant_dynamic-update-slice_fusion.7.refs_1_), channel_id=1, source_target_pairs={{0,96},{8,104},{16,112},{24,120},{32,0},{40,8},{48,16},{56,24},{64... | collective-permute-start | bytes 1769480 | tf_op jit(solution)/shard_map/ppermute | solution.py:60
  52.8 37.5 %copy-start.4 = (bf16[192,1536]{1,0:T(8,128)(2,1)}, bf16[192,1536]{1,0:T(8,128)(2,1)S(1)}, u32[]{:S(2)}) copy-start(bf16[192,1536]{1,0:T(8,128)(2,1)S(1)} %pad_maximum_fusion.7.refs_3_) | copy-start | bytes 1769476
  57.4 3.7 %collective-permute-start.12 = (bf16[112,3072]{1,0:T(8,128)(2,1)S(1)}, bf16[112,3072]{1,0:T(8,128)(2,1)S(1)}, u32[]{:S(2)}, u32[]{:S(2)}) collective-permute-start(bf16[112,3072]{1,0:T(8,128)(2,1)S(1)} %pad_maximum_fusion.5), channel_id=1, source_target_pairs={{0,1},{1,0},{2,3},{3,2},{4,5},{5,4},{6,7},{7,6},{8,9},{9,8},{10,11... | collective-permute-start | bytes 2064392 | tf_op jit(solution)/shard_map/ppermute | solution.py:507
  58.2 29.1 %collective-permute-start.15 = (bf16[192,1536]{1,0:T(8,128)(2,1)S(1)}, bf16[192,1536]{1,0:T(8,128)(2,1)S(1)}, u32[]{:S(2)}, u32[]{:S(2)}) collective-permute-start(bf16[192,1536]{1,0:T(8,128)(2,1)S(1)} %pad_maximum_fusion.6.refs_2_), channel_id=1, source_target_pairs={{0,8},{8,16},{16,24},{24,0},{32,40},{40,48},{48,56},{56,32},{64,72... | collective-permute-start | bytes 1769480 | tf_op jit(solution)/shard_map/ppermute | solution.py:60
  58.6 28.8 %collective-permute-start.16 = (bf16[192,1536]{1,0:T(8,128)(2,1)S(1)}, bf16[192,1536]{1,0:T(8,128)(2,1)S(1)}, u32[]{:S(2)}, u32[]{:S(2)}) collective-permute-start(bf16[192,1536]{1,0:T(8,128)(2,1)S(1)} %pad_maximum_fusion.7.refs_3_), channel_id=1, source_target_pairs={{0,24},{8,0},{16,8},{24,16},{32,56},{40,32},{48,40},{56,48},{64,88... | collective-permute-start | bytes 1769480 | tf_op jit(solution)/shard_map/ppermute | solution.py:60
  61.3 16.8 %copy-start.32 = (bf16[896,3072]{1,0:T(8,128)(2,1)}, bf16[896,3072]{1,0:T(8,128)(2,1)S(1)}, u32[]{:S(2)}) copy-start(bf16[896,3072]{1,0:T(8,128)(2,1)S(1)} %slice_dynamic-update-slice_fusion.x) | copy-start | bytes 16515076
  78.1 13.8 %copy-start.9 = (bf16[3,3,128,128]{3,2,1,0:T(8,128)(2,1)}, bf16[3,3,128,128]{3,2,1,0:T(8,128)(2,1)S(1)}, u32[]{:S(2)}) copy-start(bf16[3,3,128,128]{3,2,1,0:T(8,128)(2,1)S(1)} %get-tuple-element.59.query) | copy-start | bytes 884740
  78.1 13.7 %copy-start.13 = (bf16[192,1536]{1,0:T(8,128)(2,1)}, bf16[192,1536]{1,0:T(8,128)(2,1)S(1)}, u32[]{:S(2)}) copy-start(bf16[192,1536]{1,0:T(8,128)(2,1)S(1)} %collective-permute-done.13.refs_4_) | copy-start | bytes 1769476
  78.1 13.7 %copy-start.16 = (bf16[192,1536]{1,0:T(8,128)(2,1)}, bf16[192,1536]{1,0:T(8,128)(2,1)S(1)}, u32[]{:S(2)}) copy-start(bf16[192,1536]{1,0:T(8,128)(2,1)S(1)} %collective-permute-done.14.refs_5_) | copy-start | bytes 1769476
  87.4 12.2 %collective-permute-start.17 = (bf16[1,6,128,128]{3,2,1,0:T(8,128)(2,1)S(1)}, bf16[1,6,128,128]{3,2,1,0:T(8,128)(2,1)S(1)}, u32[]{:S(2)}, u32[]{:S(2)}) collective-permute-start(bf16[1,6,128,128]{3,2,1,0:T(8,128)(2,1)S(1)} %bitcast.27), channel_id=1, source_target_pairs={{0,8},{8,16},{16,24},{24,0},{32,40},{40,48},{48,56},{56,32},{64,72... | collective-permute-start | bytes 589832 | tf_op jit(solution)/shard_map/ppermute | solution.py:60
  87.6 12.0 %collective-permute-start.18 = (bf16[1,6,128,128]{3,2,1,0:T(8,128)(2,1)S(1)}, bf16[1,6,128,128]{3,2,1,0:T(8,128)(2,1)S(1)}, u32[]{:S(2)}, u32[]{:S(2)}) collective-permute-start(bf16[1,6,128,128]{3,2,1,0:T(8,128)(2,1)S(1)} %bitcast.28), channel_id=1, source_target_pairs={{0,24},{8,0},{16,8},{24,16},{32,56},{40,32},{48,40},{56,48},{64,88... | collective-permute-start | bytes 589832 | tf_op jit(solution)/shard_map/ppermute | solution.py:60
  91.9 18.2 %copy-start.53 = (s32[4]{0:T(128)S(1)}, s32[4]{0:T(128)}, u32[]{:S(2)}) copy-start(s32[4]{0:T(128)} %constant.147.clone) | copy-start | bytes 52
  99.6 7.6 %collective-permute-start.19 = (bf16[1,3,128,128]{3,2,1,0:T(8,128)(2,1)S(1)}, bf16[1,3,128,128]{3,2,1,0:T(8,128)(2,1)S(1)}, u32[]{:S(2)}, u32[]{:S(2)}) collective-permute-start(bf16[1,3,128,128]{3,2,1,0:T(8,128)(2,1)S(1)} %slice.178), channel_id=1, source_target_pairs={{0,8},{8,16},{16,24},{24,0},{32,40},{40,48},{48,56},{56,32},{64,72... | collective-permute-start | bytes 294920 | tf_op jit(solution)/shard_map/ppermute | solution.py:60
  100.4 6.9 %collective-permute-start.20 = (bf16[1,3,128,128]{3,2,1,0:T(8,128)(2,1)S(1)}, bf16[1,3,128,128]{3,2,1,0:T(8,128)(2,1)S(1)}, u32[]{:S(2)}, u32[]{:S(2)}) collective-permute-start(bf16[1,3,128,128]{3,2,1,0:T(8,128)(2,1)S(1)} %slice.179), channel_id=1, source_target_pairs={{0,24},{8,0},{16,8},{24,16},{32,56},{40,32},{48,40},{56,48},{64,88... | collective-permute-start | bytes 294920 | tf_op jit(solution)/shard_map/ppermute | solution.py:60
  107.3 18.0 %collective-permute-start.21 = (bf16[4,6,128,128]{3,2,1,0:T(8,128)(2,1)S(1)}, bf16[4,6,128,128]{3,2,1,0:T(8,128)(2,1)S(1)}, u32[]{:S(2)}, u32[]{:S(2)}) collective-permute-start(bf16[4,6,128,128]{3,2,1,0:T(8,128)(2,1)S(1)} %maximum_maximum_fusion.refs_0_.refs_5_), channel_id=1, source_target_pairs={{0,32},{8,40},{16,48},{24,56},{32,64},{40,72},{48,80},{56,88},{64,... | collective-permute-start | bytes 2359304 | tf_op jit(solution)/shard_map/ppermute | solution.py:60
  108.3 17.1 %collective-permute-start.22 = (bf16[4,6,128,128]{3,2,1,0:T(8,128)(2,1)S(1)}, bf16[4,6,128,128]{3,2,1,0:T(8,128)(2,1)}, u32[]{:S(2)}, u32[]{:S(2)}) collective-permute-start(bf16[4,6,128,128]{3,2,1,0:T(8,128)(2,1)S(1)} %maximum_maximum_fusion.refs_0_.refs_5_), channel_id=1, source_target_pairs={{0,96},{8,104},{16,112},{24,120},{32,0},{40,8},{48,16},{56,24},{64... | collective-permute-start | bytes 2359304 | tf_op jit(solution)/shard_map/ppermute | solution.py:60
  114.5 14.4 %copy-start.50 = (s32[16]{0:T(128)S(1)}, s32[16]{0:T(128)}, u32[]{:S(2)}) copy-start(s32[16]{0:T(128)} %mul.109) | copy-start | bytes 196
  114.5 14.4 %copy-start.55 = (s32[8]{0:T(128)S(1)}, s32[8]{0:T(128)}, u32[]{:S(2)}) copy-start(s32[8]{0:T(128)} %copy-done.54) | copy-start | bytes 100
  114.5 14.5 %copy-start.36 = (s32[128]{0:T(128)S(1)}, s32[128]{0:T(128)}, u32[]{:S(2)}) copy-start(s32[128]{0:T(128)} %counts.1) | copy-start | bytes 1540
  125.4 12.8 %collective-permute-start.23 = (bf16[2,6,128,128]{3,2,1,0:T(8,128)(2,1)S(1)}, bf16[2,6,128,128]{3,2,1,0:T(8,128)(2,1)S(1)}, u32[]{:S(2)}, u32[]{:S(2)}) collective-permute-start(bf16[2,6,128,128]{3,2,1,0:T(8,128)(2,1)S(1)} %slice.180), channel_id=1, source_target_pairs={{0,32},{8,40},{16,48},{24,56},{32,64},{40,72},{48,80},{56,88},{64,... | collective-permute-start | bytes 1179656 | tf_op jit(solution)/shard_map/ppermute | solution.py:60
  126.2 36.7 %collective-permute-start.37 = (bf16[384,1536]{1,0:T(8,128)(2,1)}, bf16[384,1536]{1,0:T(8,128)(2,1)}, u32[]{:S(2)}, u32[]{:S(2)}) collective-permute-start(bf16[384,1536]{1,0:T(8,128)(2,1)} %get-tuple-element.76), channel_id=1, source_target_pairs={{0,32},{8,40},{16,48},{24,56},{32,64},{40,72},{48,80},{56,88},{64,... | collective-permute-start | bytes 3538952 | tf_op jit(solution)/shard_map/ppermute | solution.py:60
  127.5 35.4 %collective-permute-start.38 = (bf16[384,1536]{1,0:T(8,128)(2,1)}, bf16[384,1536]{1,0:T(8,128)(2,1)}, u32[]{:S(2)}, u32[]{:S(2)}) collective-permute-start(bf16[384,1536]{1,0:T(8,128)(2,1)} %get-tuple-element.77), channel_id=1, source_target_pairs={{0,96},{8,104},{16,112},{24,120},{32,0},{40,8},{48,16},{56,24},{64... | collective-permute-start | bytes 3538952 | tf_op jit(solution)/shard_map/ppermute | solution.py:60
  129.2 44.1 %collective-permute-start.30 = (bf16[384,1536]{1,0:T(8,128)(2,1)}, bf16[384,1536]{1,0:T(8,128)(2,1)}, u32[]{:S(2)}, u32[]{:S(2)}) collective-permute-start(bf16[384,1536]{1,0:T(8,128)(2,1)} %get-tuple-element.74), channel_id=1, source_target_pairs={{0,8},{8,16},{16,24},{24,0},{32,40},{40,48},{48,56},{56,32},{64,72... | collective-permute-start | bytes 3538952 | tf_op jit(solution)/shard_map/ppermute | solution.py:60
  129.3 44.0 %collective-permute-start.31 = (bf16[384,1536]{1,0:T(8,128)(2,1)}, bf16[384,1536]{1,0:T(8,128)(2,1)}, u32[]{:S(2)}, u32[]{:S(2)}) collective-permute-start(bf16[384,1536]{1,0:T(8,128)(2,1)} %get-tuple-element.75), channel_id=1, source_target_pairs={{0,24},{8,0},{16,8},{24,16},{32,56},{40,32},{48,40},{56,48},{64,88... | collective-permute-start | bytes 3538952 | tf_op jit(solution)/shard_map/ppermute | solution.py:60
  138.2 21.5 %copy-start.1 = (bf16[768,384]{1,0:T(8,128)(2,1)S(1)}, bf16[768,384]{1,0:T(8,128)(2,1)}, u32[]{:S(2)}) copy-start(bf16[768,384]{1,0:T(8,128)(2,1)} %copy-done) | copy-start | bytes 1769476
  138.2 21.5 %copy-start.10 = (bf16[3,3,128,128]{3,2,1,0:T(8,128)(2,1)S(1)}, bf16[3,3,128,128]{3,2,1,0:T(8,128)(2,1)}, u32[]{:S(2)}) copy-start(bf16[3,3,128,128]{3,2,1,0:T(8,128)(2,1)} %copy-done.9) | copy-start | bytes 884740
  138.2 21.5 %collective-permute-start.24 = (bf16[2,6,128,128]{3,2,1,0:T(8,128)(2,1)}, bf16[2,6,128,128]{3,2,1,0:T(8,128)(2,1)S(1)}, u32[]{:S(2)}, u32[]{:S(2)}) collective-permute-start(bf16[2,6,128,128]{3,2,1,0:T(8,128)(2,1)} %slice.181), channel_id=1, source_target_pairs={{0,96},{8,104},{16,112},{24,120},{32,0},{40,8},{48,16},{56,24},{64... | collective-permute-start | bytes 1179656 | tf_op jit(solution)/shard_map/ppermute | solution.py:60
  168.4 19.3 %collective-permute-start.39 = (bf16[448,768]{1,0:T(8,128)(2,1)S(1)}, bf16[448,768]{1,0:T(8,128)(2,1)S(1)}, u32[]{:S(2)}, u32[]{:S(2)}) collective-permute-start(bf16[448,768]{1,0:T(8,128)(2,1)S(1)} %slice.235), channel_id=1, source_target_pairs={{0,1},{1,0},{2,3},{3,2},{4,5},{5,4},{6,7},{7,6},{8,9},{9,8},{10,11... | collective-permute-start | bytes 2064392 | tf_op jit(solution)/shard_map/ppermute | solution.py:80
  178.7 12.0 %collective-permute-start.32 = (bf16[448,768]{1,0:T(8,128)(2,1)S(1)}, bf16[448,768]{1,0:T(8,128)(2,1)S(1)}, u32[]{:S(2)}, u32[]{:S(2)}) collective-permute-start(bf16[448,768]{1,0:T(8,128)(2,1)S(1)} %slice.226), channel_id=1, source_target_pairs={{0,1},{1,0},{2,3},{3,2},{4,5},{5,4},{6,7},{7,6},{8,9},{9,8},{10,11... | collective-permute-start | bytes 2064392 | tf_op jit(solution)/shard_map/ppermute | solution.py:80
  187.2 8.6 %collective-permute-start.25 = (bf16[448,1536]{1,0:T(8,128)(2,1)S(1)}, bf16[448,1536]{1,0:T(8,128)(2,1)S(1)}, u32[]{:S(2)}, u32[]{:S(2)}) collective-permute-start(bf16[448,1536]{1,0:T(8,128)(2,1)S(1)} %slice.217), channel_id=1, source_target_pairs={{0,1},{1,0},{2,3},{3,2},{4,5},{5,4},{6,7},{7,6},{8,9},{9,8},{10,11... | collective-permute-start | bytes 4128776 | tf_op jit(solution)/shard_map/ppermute | solution.py:80
  187.8 5.8 %collective-permute-start.40 = (bf16[112,384]{1,0:T(8,128)(2,1)S(1)}, bf16[112,384]{1,0:T(8,128)(2,1)S(1)}, u32[]{:S(2)}, u32[]{:S(2)}) collective-permute-start(bf16[112,384]{1,0:T(8,128)(2,1)S(1)} %get-tuple-element.101), channel_id=1, source_target_pairs={{0,2},{1,3},{2,4},{3,5},{4,6},{5,7},{6,0},{7,1},{8,10},{9,11},{10,... | collective-permute-start | bytes 258056 | tf_op jit(solution)/shard_map/ppermute | solution.py:83
  188.8 4.8 %collective-permute-start.42 = (bf16[112,384]{1,0:T(8,128)(2,1)S(1)}, bf16[112,384]{1,0:T(8,128)(2,1)S(1)}, u32[]{:S(2)}, u32[]{:S(2)}) collective-permute-start(bf16[112,384]{1,0:T(8,128)(2,1)S(1)} %get-tuple-element.99), channel_id=1, source_target_pairs={{0,6},{1,7},{2,0},{3,1},{4,2},{5,3},{6,4},{7,5},{8,14},{9,15},{10,... | collective-permute-start | bytes 258056 | tf_op jit(solution)/shard_map/ppermute | solution.py:84
  190.9 5.6 %collective-permute-start.33 = (bf16[112,384]{1,0:T(8,128)(2,1)S(1)}, bf16[112,384]{1,0:T(8,128)(2,1)S(1)}, u32[]{:S(2)}, u32[]{:S(2)}) collective-permute-start(bf16[112,384]{1,0:T(8,128)(2,1)S(1)} %get-tuple-element.105), channel_id=1, source_target_pairs={{0,2},{1,3},{2,4},{3,5},{4,6},{5,7},{6,0},{7,1},{8,10},{9,11},{10,... | collective-permute-start | bytes 258056 | tf_op jit(solution)/shard_map/ppermute | solution.py:83
  191.0 8.2 %collective-permute-start.35 = (bf16[112,384]{1,0:T(8,128)(2,1)S(1)}, bf16[112,384]{1,0:T(8,128)(2,1)S(1)}, u32[]{:S(2)}, u32[]{:S(2)}) collective-permute-start(bf16[112,384]{1,0:T(8,128)(2,1)S(1)} %get-tuple-element.103), channel_id=1, source_target_pairs={{0,6},{1,7},{2,0},{3,1},{4,2},{5,3},{6,4},{7,5},{8,14},{9,15},{10,... | collective-permute-start | bytes 258056 | tf_op jit(solution)/shard_map/ppermute | solution.py:84
  193.7 14.5 %collective-permute-start.43 = (bf16[112,768]{1,0:T(8,128)(2,1)S(1)}, bf16[112,768]{1,0:T(8,128)(2,1)S(1)}, u32[]{:S(2)}, u32[]{:S(2)}) collective-permute-start(bf16[112,768]{1,0:T(8,128)(2,1)S(1)} %pad_maximum_fusion.14), channel_id=1, source_target_pairs={{0,6},{1,7},{2,0},{3,1},{4,2},{5,3},{6,4},{7,5},{8,14},{9,15},{10,... | collective-permute-start | bytes 516104 | tf_op jit(solution)/shard_map/ppermute | solution.py:90
  195.8 12.9 %collective-permute-start.41 = (bf16[112,768]{1,0:T(8,128)(2,1)S(1)}, bf16[112,768]{1,0:T(8,128)(2,1)S(1)}, u32[]{:S(2)}, u32[]{:S(2)}) collective-permute-start(bf16[112,768]{1,0:T(8,128)(2,1)S(1)} %pad_maximum_fusion.13), channel_id=1, source_target_pairs={{0,2},{1,3},{2,4},{3,5},{4,6},{5,7},{6,0},{7,1},{8,10},{9,11},{10,... | collective-permute-start | bytes 516104 | tf_op jit(solution)/shard_map/ppermute | solution.py:89
  196.4 8.7 %collective-permute-start.26 = (bf16[112,768]{1,0:T(8,128)(2,1)S(1)}, bf16[112,768]{1,0:T(8,128)(2,1)S(1)}, u32[]{:S(2)}, u32[]{:S(2)}) collective-permute-start(bf16[112,768]{1,0:T(8,128)(2,1)S(1)} %get-tuple-element.97), channel_id=1, source_target_pairs={{0,2},{1,3},{2,4},{3,5},{4,6},{5,7},{6,0},{7,1},{8,10},{9,11},{10,... | collective-permute-start | bytes 516104 | tf_op jit(solution)/shard_map/ppermute | solution.py:83
  196.5 8.6 %collective-permute-start.28 = (bf16[112,768]{1,0:T(8,128)(2,1)S(1)}, bf16[112,768]{1,0:T(8,128)(2,1)S(1)}, u32[]{:S(2)}, u32[]{:S(2)}) collective-permute-start(bf16[112,768]{1,0:T(8,128)(2,1)S(1)} %get-tuple-element.95), channel_id=1, source_target_pairs={{0,6},{1,7},{2,0},{3,1},{4,2},{5,3},{6,4},{7,5},{8,14},{9,15},{10,... | collective-permute-start | bytes 516104 | tf_op jit(solution)/shard_map/ppermute | solution.py:84
  205.2 11.8 %collective-permute-start.29 = (bf16[112,1536]{1,0:T(8,128)(2,1)S(1)}, bf16[112,1536]{1,0:T(8,128)(2,1)S(1)}, u32[]{:S(2)}, u32[]{:S(2)}) collective-permute-start(bf16[112,1536]{1,0:T(8,128)(2,1)S(1)} %pad_maximum_fusion.10), channel_id=1, source_target_pairs={{0,6},{1,7},{2,0},{3,1},{4,2},{5,3},{6,4},{7,5},{8,14},{9,15},{10,... | collective-permute-start | bytes 1032200 | tf_op jit(solution)/shard_map/ppermute | solution.py:90
  205.3 11.7 %collective-permute-start.27 = (bf16[112,1536]{1,0:T(8,128)(2,1)S(1)}, bf16[112,1536]{1,0:T(8,128)(2,1)S(1)}, u32[]{:S(2)}, u32[]{:S(2)}) collective-permute-start(bf16[112,1536]{1,0:T(8,128)(2,1)S(1)} %pad_maximum_fusion.9), channel_id=1, source_target_pairs={{0,2},{1,3},{2,4},{3,5},{4,6},{5,7},{6,0},{7,1},{8,10},{9,11},{10,... | collective-permute-start | bytes 1032200 | tf_op jit(solution)/shard_map/ppermute | solution.py:89
  206.9 9.2 %collective-permute-start.36 = (bf16[112,768]{1,0:T(8,128)(2,1)S(1)}, bf16[112,768]{1,0:T(8,128)(2,1)S(1)}, u32[]{:S(2)}, u32[]{:S(2)}) collective-permute-start(bf16[112,768]{1,0:T(8,128)(2,1)S(1)} %pad_maximum_fusion.12), channel_id=1, source_target_pairs={{0,6},{1,7},{2,0},{3,1},{4,2},{5,3},{6,4},{7,5},{8,14},{9,15},{10,... | collective-permute-start | bytes 516104 | tf_op jit(solution)/shard_map/ppermute | solution.py:90
  208.3 8.8 %collective-permute-start.34 = (bf16[112,768]{1,0:T(8,128)(2,1)S(1)}, bf16[112,768]{1,0:T(8,128)(2,1)S(1)}, u32[]{:S(2)}, u32[]{:S(2)}) collective-permute-start(bf16[112,768]{1,0:T(8,128)(2,1)S(1)} %pad_maximum_fusion.11), channel_id=1, source_target_pairs={{0,2},{1,3},{2,4},{3,5},{4,6},{5,7},{6,0},{7,1},{8,10},{9,11},{10,... | collective-permute-start | bytes 516104 | tf_op jit(solution)/shard_map/ppermute | solution.py:89
  217.1 15.0 %copy-start.45 = (f32[1,2,2048]{2,1,0:T(2,128)S(1)}, f32[1,2,2048]{2,1,0:T(2,128)}, u32[]{:S(2)}) copy-start(f32[1,2,2048]{2,1,0:T(2,128)} %param.42) | copy-start | bytes 49156
  220.0 13.0 %copy-start.30 = (f32[64,64]{1,0:T(8,128)}, f32[64,64]{1,0:T(8,128)S(1)}, u32[]{:S(2)}) copy-start(f32[64,64]{1,0:T(8,128)S(1)} %get-tuple-element.81.middle) | copy-start | bytes 49156
  220.0 12.9 %collective-permute-start.44 = (f32[32,64]{1,0:T(8,128)S(1)}, f32[32,64]{1,0:T(8,128)S(1)}, u32[]{:S(2)}, u32[]{:S(2)}) collective-permute-start(f32[32,64]{1,0:T(8,128)S(1)} %get-tuple-element.111), channel_id=1, source_target_pairs={{0,1},{1,2},{2,3},{3,4},{4,5},{5,6},{6,7},{8,9},{9,10},{10,11},{11... | collective-permute-start | bytes 24584 | tf_op jit(solution)/shard_map/ppermute | solution.py:585
  225.7 7.2 %collective-permute-start.45 = (f32[32,64]{1,0:T(8,128)S(1)}, f32[32,64]{1,0:T(8,128)S(1)}, u32[]{:S(2)}, u32[]{:S(2)}) collective-permute-start(f32[32,64]{1,0:T(8,128)S(1)} %get-tuple-element.110), channel_id=1, source_target_pairs={{1,0},{2,1},{3,2},{4,3},{5,4},{6,5},{7,6},{9,8},{10,9},{11,10},{12... | collective-permute-start | bytes 24584 | tf_op jit(solution)/shard_map/ppermute | solution.py:586
  (43 other events, 267.2 us)
Sparse Core Ops, SparseCore 0:
  10.2 101.5 all-gather.1

commit v3 on v2

--- a/solution.py
+++ b/solution.py
@@ -74,18 +74,24 @@
 LAYOUT = output_layout()
 
 
-def scatter_sum(partial):
-    rows, columns = partial.shape[0] // 8, partial.shape[1]
-    half = columns // 2
-    other = lax.ppermute(partial[4 * rows :], "narrow", CORE_SWAP).astype(F32)
-    pair = partial[: 4 * rows].astype(F32) + other
+def to_core(partial):
+    return lax.ppermute(partial[partial.shape[0] // 2 :], "narrow", CORE_SWAP)
+
+
+def to_far(partial, other):
+    rows, half = partial.shape[0] // 8, partial.shape[1] // 2
+    pair = partial[: 4 * rows].astype(F32) + other.astype(F32)
     far = pair[2 * rows : 3 * rows].astype(BF16)
-    from_prv = lax.ppermute(far[:, :half], "narrow", chip_shift(1)).astype(F32)
-    from_nxt = lax.ppermute(far[:, half:], "narrow", chip_shift(-1)).astype(F32)
-    to_nxt = pair[rows : 2 * rows]
-    to_prv = pair[3 * rows :]
-    to_nxt = jnp.concatenate([to_nxt[:, :half] + from_prv, to_nxt[:, half:]], axis=1).astype(BF16)
-    to_prv = jnp.concatenate([to_prv[:, :half], to_prv[:, half:] + from_nxt], axis=1).astype(BF16)
+    from_prv = lax.ppermute(far[:, :half], "narrow", chip_shift(1))
+    from_nxt = lax.ppermute(far[:, half:], "narrow", chip_shift(-1))
+    return pair, from_prv, from_nxt
+
+
+def to_near(pair, from_prv, from_nxt):
+    rows, half = pair.shape[0] // 4, pair.shape[1] // 2
+    to_nxt, to_prv = pair[rows : 2 * rows], pair[3 * rows :]
+    to_nxt = jnp.concatenate([to_nxt[:, :half] + from_prv.astype(F32), to_nxt[:, half:]], axis=1).astype(BF16)
+    to_prv = jnp.concatenate([to_prv[:, :half], to_prv[:, half:] + from_nxt.astype(F32)], axis=1).astype(BF16)
     one = lax.ppermute(to_nxt, "narrow", chip_shift(1))
     two = lax.ppermute(to_prv, "narrow", chip_shift(-1))
     return pair[:rows], one, two
@@ -144,36 +150,21 @@
     step = 4 * rows
     heads = weight.shape[2] // 128
 
-    def tile(index, carry):
-        start = pl.multiple_of(index * step, 32)
-        acc = jnp.dot(x[pl.ds(start, step), :], weight[0], preferred_element_type=F32)
-
-        def put(head, values):
-            for part in range(4):
-                first = part * rows
-                block = 4 * index + part
-                request[0, head, pl.ds(pl.multiple_of(block * taken, 32), taken), :] = values[first : first + taken]
-                extra[0, head, pl.ds(pl.multiple_of(block * own, 16), own), :] = values[first + taken : first + rows]
-
-        @pl.when(which < 2)
-        def _():
-            gain = gains[pl.ds(which, 1), :]
-            cos = cosine[pl.ds(start, step), :]
-            sin = sine[pl.ds(start, step), :]
-            for head in range(heads):
-                part = acc[:, head * 128 : (head + 1) * 128]
-                square = jnp.mean(part * part, axis=1, keepdims=True)
-                part = part * lax.rsqrt(square + EPSILON) * gain
-                put(head, (part * cos + partner_of(part) * sin).astype(BF16))
-
-        @pl.when(which == 2)
-        def _():
-            for head in range(heads):
-                put(head, acc[:, head * 128 : (head + 1) * 128].astype(BF16))
-
-        return carry
-
-    lax.fori_loop(0, total // step, tile, 0)
+    plain = which == 2
+    gain = gains[pl.ds(jnp.minimum(which, 1), 1), :]
+    for start in range(0, total, step):
+        acc = jnp.dot(x[start : start + step, :], weight[0], preferred_element_type=F32)
+        cos = cosine[start : start + step, :]
+        sin = sine[start : start + step, :]
+        for head in range(heads):
+            part = acc[:, head * 128 : (head + 1) * 128]
+            square = jnp.mean(part * part, axis=1, keepdims=True)
+            normed = part * lax.rsqrt(square + EPSILON) * gain
+            values = jnp.where(plain, part, normed * cos + partner_of(normed) * sin).astype(BF16)
+            for index in range(step // rows):
+                first, block = index * rows, start // rows + index
+                request[0, head, block * taken : (block + 1) * taken, :] = values[first : first + taken]
+                extra[0, head, block * own : (block + 1) * own, :] = values[first + taken : first + rows]
 
 
 def project_heads(x, weight, gains, cosine, sine, blocks, own):
@@ -276,12 +267,16 @@
 
 
 def gelu(values):
-    inner = math.sqrt(2.0 / math.pi) * (values + 0.044715 * (values * values * values))
-    return values * (0.5 * (1.0 + jnp.tanh(inner)))
+    root = math.sqrt(2.0 / math.pi)
+    half = 0.5 * values
+    return half + half * jnp.tanh(values * (root + (root * 0.044715) * (values * values)))
 
 
 def hidden_kernel(x, weight, out):
-    out[...] = gelu(jnp.dot(x[...], weight[...], preferred_element_type=F32)).astype(BF16)
+    rows = x.shape[0] // 2
+    for start in (0, rows):
+        acc = jnp.dot(x[start : start + rows, :], weight[...], preferred_element_type=F32)
+        out[start : start + rows, :] = gelu(acc).astype(BF16)
 
 
 def hidden_units(x, weight, step=256):
@@ -492,6 +487,8 @@
     scalars = (ids, request_group, step_index)
     text_own, image_own, extra_own = text_tokens[0], image_tokens[0], extra_tokens[0]
 
+    channels = proj_weight.shape[1]
+    latent_rows = latent[0].reshape(-1, channels)
     hidden_weight = lax.all_gather(mlp_in_weight, "wide", axis=0, tiled=True)
     own = modulate(scalars, text_own, image_own, extra_own, mod_table)
 
@@ -510,7 +507,9 @@
     prv = lax.ppermute(own, "narrow", chip_shift(1))
     own_swapped = swap(own)
     far = [wide(near[2 * i], routes[i][0](1)) for i in range(2)]
-    *far, nxt, prv, own_swapped = together((*far, nxt, prv, own_swapped))
+    *far, nxt, prv, own_swapped, attn_weight, late_latent = together(
+        (*far, nxt, prv, own_swapped, attn_out_weight.T, latent_rows)
+    )
 
     cut = own.shape[0] // 2
     far_a = lax.ppermute(nxt[:cut], "narrow", chip_shift(-1))
@@ -574,20 +573,36 @@
     live = (slot_ids[None, :] < counts[:, None]).astype(F32).reshape(1, -1)
     attended = attend_extra(extra_heads, live, attended, key_pieces, 8)
 
-    attn_weight = attn_out_weight.T
     chunks = [low[:1] + high[:1] + low[1:] + high[1:] + early] + late
-    sums = [scatter_sum(output_part(i, ids, act, attended, attn_weight, pieces)) for i, pieces in enumerate(chunks)]
+
+    def output(i, act):
+        return output_part(i, ids, act, attended, attn_weight, chunks[i])
+
+    part0 = output(1, act)
+    other0 = to_core(part0)
+    part1 = output(2, act)
+    other0, part1, act = together((other0, part1, act))
+    far0 = to_far(part0, other0)
+    other1 = to_core(part1)
+    part2 = output(0, act)
+    *far0, other1, part2 = together((*far0, other1, part2))
+    sum0 = to_near(*far0)
+    far1 = to_far(part1, other1)
+    other2 = to_core(part2)
+    *far1, other2 = together((*far1, other2))
+    sum1 = to_near(*far1)
+    far2 = to_far(part2, other2)
+    sums = [to_near(*far2), sum0, sum1]
     text_out, image_out, extra_out, velocity = finish(
         (*scalars, extra_counts), text_own, image_own, extra_own, mod_table, final_table, proj_weight.T, sums
     )
-    channels = proj_weight.shape[1]
     grid_width = latent.shape[2] // channels
     above = lax.ppermute(velocity[-grid_width:], "narrow", [(i, i + 1) for i in range(7)])
     below = lax.ppermute(velocity[:grid_width], "narrow", [(i + 1, i) for i in range(7)])
     step_here = step_index[request_group[group]]
     delta = (noise_level(step_here + 1) - noise_level(step_here)).reshape(1)
     latent_next = smooth(
-        delta, above, velocity, below, stencil, latent[0].reshape(-1, channels), grid_width
+        delta, above, velocity, below, stencil, late_latent, grid_width
     )
     return (text_out[None], image_out[None], extra_out[None], latent_next.reshape(latent.shape))
 

time: 245 us -> 242 us (0.988)
  waiting for transfers between devices: 69.2 us -> 65.4 us
    ppermute x22, waiting for transfers between devices: 49.8 us -> 45.1 us  [wide(): return lax.ppermute(block, 'wide', pairs)]
    ppermute x22, starting transfers between devices: 29.6 us -> 26.4 us  [wide(): return lax.ppermute(block, 'wide', pairs)]
    unnamed x131 -> x137, local copies, waits for them, and re-layouts: 12.9 us -> 13.6 us
  transfers between devices with their start and end apart: 47 -> 47, of which waited for: 12 -> 13; matrix products, arithmetic and copies ran while one was open for 10% -> 11% of each run, Pallas kernels for 21% -> 21%
where the time goes in v3:
time: 242 us; the launch traced here: 241 us
  waiting for transfers between devices  65.4 us (27%)
  starting transfers between devices  65 us (27%)
  Pallas kernels  54.5 us (23%)
  local copies, waits for them, and re-layouts  24.1 us (10%)
  between operations  18.7 us (8%)
  other arithmetic  13.2 us (5%)
    ppermute x22, waiting for transfers between devices, wide(): return lax.ppermute(block, 'wide', pairs)  45.1 us
    ppermute x22, starting transfers between devices, wide(): return lax.ppermute(block, 'wide', pairs)  26.4 us
    pallas_call x3, Pallas kernels, output_part(): pl.pallas_call(functools.partial(output_kernel, chunk), out_shape=jax.Sha...  18.2 us
    unnamed x137, local copies, waits for them, and re-layouts  13.6 us
    pallas_call x1, Pallas kernels, project_heads(): pl.pallas_call(functools.partial(heads_kernel, blocks, own), grid=(3,), o...  12.7 us
    pallas_call x1, Pallas kernels, hidden_units(): pl.pallas_call(hidden_kernel, grid=(units // step,), out_shape=jax.ShapeD...  12 us
    ppermute x3, starting transfers between devices, to_far(): from_nxt = lax.ppermute(far[:, half:], 'narrow', chip_shift(-1))  7.99 us
    ppermute x3, waiting for transfers between devices, to_near(): two = lax.ppermute(to_prv, 'narrow', chip_shift(-1))  7.66 us
  transfers between devices with their start and end apart: 47, of which 13 were waited for; matrix products, arithmetic and copies ran while one was open for 11% of the time, Pallas kernels for 21%

profile of v3, /device:TPU:1, one launch (start us, length us, event | category | flops | bytes accessed | tf_op | source)
XLA Modules:
  0.0 240.9 jit_solution(6411616341115563078)
XLA Ops:
  7.9 1.8 fusion.19
  9.8 2.1 collective-permute-start
  11.9 1.4 collective-permute-start.1
  13.3 1.6 collective-permute-start.2
  15.0 2.1 collective-permute-start.3
  19.4 4.3 %copy.34 = bf16[384,3072]{0,1:T(8,128)(2,1)} copy(bf16[384,3072]{1,0:T(8,128)(2,1)} %param.37) | data formatting | bytes 4718592 | tf_op args[14]
  24.4 1.0 concatenate.78
  25.6 1.1 shard_map.246
  26.7 2.5 %collective-permute-start.6 = (bf16[112,3072]{1,0:T(8,128)(2,1)S(1)}, bf16[112,3072]{1,0:T(8,128)(2,1)S(1)}, u32[]{:S(2)}, u32[]{:S(2)}) collective-permute-start(bf16[112,3072]{1,0:T(8,128)(2,1)S(1)} %shard_map.246), channel_id=1, source_target_pairs={{0,6},{1,7},{2,0},{3,1},{4,2},{5,3},{6,4},{7,5},{8,14},{9,15},{10,... | collective-permute-start | bytes 2064392 | tf_op jit(solution)/shard_map/ppermute | solution.py:506
  29.2 1.8 collective-permute-start.8
  31.0 1.6 sine_multiply_fusion
  32.8 1.1 pad_maximum_fusion.6.refs_2_
  33.9 1.2 pad_maximum_fusion.8.refs_0_
  35.1 9.7 %collective-permute-done.4 = bf16[96,1536]{1,0:T(8,128)(2,1)S(1)} collective-permute-done((bf16[96,1536]{1,0:T(8,128)(2,1)}, bf16[96,1536]{1,0:T(8,128)(2,1)S(1)}, u32[]{:S(2)}, u32[]{:S(2)}) %collective-permute-start.4) | collective-permute-done | bytes 294944 | tf_op jit(solution)/shard_map/ppermute | solution.py:60
  45.7 2.8 %collective-permute-start.11 = (bf16[224,3072]{1,0:T(8,128)(2,1)S(1)}, bf16[224,3072]{1,0:T(8,128)(2,1)S(1)}, u32[]{:S(2)}, u32[]{:S(2)}) collective-permute-start(bf16[224,3072]{1,0:T(8,128)(2,1)S(1)} %pad_maximum_fusion), channel_id=1, source_target_pairs={{0,1},{1,0},{2,3},{3,2},{4,5},{5,4},{6,7},{7,6},{8,9},{9,8},{10,11... | collective-permute-start | bytes 4128776 | tf_op jit(solution)/shard_map/ppermute | solution.py:504
  48.7 2.7 %collective-permute-start.9 = (bf16[56,3072]{1,0:T(8,128)(2,1)S(1)}, bf16[56,3072]{1,0:T(8,128)(2,1)S(1)}, u32[]{:S(2)}, u32[]{:S(2)}) collective-permute-start(bf16[56,3072]{1,0:T(8,128)(2,1)S(1)} %slice.170), channel_id=1, source_target_pairs={{0,6},{1,7},{2,0},{3,1},{4,2},{5,3},{6,4},{7,5},{8,14},{9,15},{10,... | collective-permute-start | bytes 1032200 | tf_op jit(solution)/shard_map/ppermute | solution.py:515
  51.4 1.5 collective-permute-start.14
  52.9 1.0 pad_maximum_fusion.7.refs_3_
  54.0 5.7 %collective-permute-done.10 = bf16[56,3072]{1,0:T(8,128)(2,1)S(1)} collective-permute-done((bf16[56,3072]{1,0:T(8,128)(2,1)S(1)}, bf16[56,3072]{1,0:T(8,128)(2,1)S(1)}, u32[]{:S(2)}, u32[]{:S(2)}) %collective-permute-start.10) | collective-permute-done | bytes 344096 | tf_op jit(solution)/shard_map/ppermute | solution.py:516
  59.7 0.8 collective-permute-start.12
  60.6 2.6 %collective-permute-start.16 = (bf16[192,1536]{1,0:T(8,128)(2,1)S(1)}, bf16[192,1536]{1,0:T(8,128)(2,1)S(1)}, u32[]{:S(2)}, u32[]{:S(2)}) collective-permute-start(bf16[192,1536]{1,0:T(8,128)(2,1)S(1)} %pad_maximum_fusion.7.refs_3_), channel_id=1, source_target_pairs={{0,24},{8,0},{16,8},{24,16},{32,56},{40,32},{48,40},{56,48},{64,88... | collective-permute-start | bytes 1769480 | tf_op jit(solution)/shard_map/ppermute | solution.py:60
  63.6 2.8 %slice-done.1 = s8[2883584]{0:T(1024)(128)(4,1)S(1)} async-done(((s8[7077888]{0:T(1024)(128)(4,1)}), s8[2883584]{0:T(1024)(128)(4,1)S(1)}, s32[]{:S(2)}) %slice-start.1) | async-done | bytes 2883608
  66.4 12.7 %shard_map.247 = (bf16[3,3,768,128]{3,2,1,0:T(8,128)(2,1)S(1)}, bf16[3,3,128,128]{3,2,1,0:T(8,128)(2,1)S(1)}) custom-call(bf16[896,3072]{1,0:T(8,128)(2,1)S(1)} %slice_dynamic-update-slice_fusion.x, bf16[3,3072,384]{2,1,0:T(8,128)(2,1)S(1)} %bitcast.26, f32[2,128]{1,0:T(2,128)S(1)} %pad_maximum_fusion.15.gains, f32[896,128]{1,0:T(8,128)S(1)} %get-tuple-element.137.cosine, ...), custom_call_target="tpu_custom_call" | custom-call | flops 6341787648 | bytes 16777216 | tf_op jit(solution)/shard_map/pallas_call | solution.py:175
  79.2 10.5 %collective-permute-done.15.refs_6_ = bf16[192,1536]{1,0:T(8,128)(2,1)S(1)} collective-permute-done((bf16[192,1536]{1,0:T(8,128)(2,1)S(1)}, bf16[192,1536]{1,0:T(8,128)(2,1)S(1)}, u32[]{:S(2)}, u32[]{:S(2)}) %collective-permute-start.15) | collective-permute-done | bytes 589856 | tf_op jit(solution)/shard_map/ppermute | solution.py:60
  89.8 2.7 %collective-permute-start.18 = (bf16[1,6,128,128]{3,2,1,0:T(8,128)(2,1)S(1)}, bf16[1,6,128,128]{3,2,1,0:T(8,128)(2,1)S(1)}, u32[]{:S(2)}, u32[]{:S(2)}) collective-permute-start(bf16[1,6,128,128]{3,2,1,0:T(8,128)(2,1)S(1)} %bitcast.28), channel_id=1, source_target_pairs={{0,24},{8,0},{16,8},{24,16},{32,56},{40,32},{48,40},{56,48},{64,88... | collective-permute-start | bytes 589832 | tf_op jit(solution)/shard_map/ppermute | solution.py:60
  92.4 1.6 pad_maximum_fusion.1
  94.0 7.7 %collective-permute-done.17 = bf16[1,6,128,128]{3,2,1,0:T(8,128)(2,1)S(1)} collective-permute-done((bf16[1,6,128,128]{3,2,1,0:T(8,128)(2,1)S(1)}, bf16[1,6,128,128]{3,2,1,0:T(8,128)(2,1)S(1)}, u32[]{:S(2)}, u32[]{:S(2)}) %collective-permute-start.17) | collective-permute-done | bytes 196640 | tf_op jit(solution)/shard_map/ppermute | solution.py:60
  102.6 2.7 %collective-permute-start.20 = (bf16[1,3,128,128]{3,2,1,0:T(8,128)(2,1)S(1)}, bf16[1,3,128,128]{3,2,1,0:T(8,128)(2,1)S(1)}, u32[]{:S(2)}, u32[]{:S(2)}) collective-permute-start(bf16[1,3,128,128]{3,2,1,0:T(8,128)(2,1)S(1)} %slice.179), channel_id=1, source_target_pairs={{0,24},{8,0},{16,8},{24,16},{32,56},{40,32},{48,40},{56,48},{64,88... | collective-permute-start | bytes 294920 | tf_op jit(solution)/shard_map/ppermute | solution.py:60
  105.3 4.6 %collective-permute-done.19 = bf16[1,3,128,128]{3,2,1,0:T(8,128)(2,1)S(1)} collective-permute-done((bf16[1,3,128,128]{3,2,1,0:T(8,128)(2,1)S(1)}, bf16[1,3,128,128]{3,2,1,0:T(8,128)(2,1)S(1)}, u32[]{:S(2)}, u32[]{:S(2)}) %collective-permute-start.19) | collective-permute-done | bytes 98336 | tf_op jit(solution)/shard_map/ppermute | solution.py:60
  109.8 1.2 maximum_maximum_fusion.refs_0_.refs_5_
  111.1 2.7 %collective-permute-start.22 = (bf16[4,6,128,128]{3,2,1,0:T(8,128)(2,1)S(1)}, bf16[4,6,128,128]{3,2,1,0:T(8,128)(2,1)}, u32[]{:S(2)}, u32[]{:S(2)}) collective-permute-start(bf16[4,6,128,128]{3,2,1,0:T(8,128)(2,1)S(1)} %maximum_maximum_fusion.refs_0_.refs_5_), channel_id=1, source_target_pairs={{0,96},{8,104},{16,112},{24,120},{32,0},{40,8},{48,16},{56,24},{64... | collective-permute-start | bytes 2359304 | tf_op jit(solution)/shard_map/ppermute | solution.py:60
  114.5 2.9 %shard_map.248.done = bf16[768,384]{1,0:T(8,128)(2,1)S(1)} custom-call(bf16[3,3,768,128]{3,2,1,0:T(8,128)(2,1)S(1)} %get-tuple-element.80.query.keys.values, bf16[3,3,768,128]{3,2,1,0:T(8,128)(2,1)S(1)} %get-tuple-element.80.query.keys.values, bf16[3,3,768,128]{3,2,1,0:T(8,128)(2,1)S(1)} %get-tuple-element.80.query.keys.values), custom_call_target="tpu_custom_call" | custom-call | flops 905969664 | bytes 5242880 | tf_op jit(solution)/shard_map/pallas_call | solution.py:220
  117.4 0.8 copy-done
  118.3 2.6 %pad_maximum_fusion.3 = (bf16[384,1536]{1,0:T(8,128)(2,1)}, bf16[384,1536]{1,0:T(8,128)(2,1)}) fusion(bf16[192,1536]{1,0:T(8,128)(2,1)S(1)} %copy-done.14, bf16[96,1536]{1,0:T(8,128)(2,1)S(1)} %copy-done.43, bf16[96,1536]{1,0:T(8,128)(2,1)S(1)} %copy-done.41, bf16[192,1536]{1,0:T(8,128)(2,1)S(1)} %copy-done.17, bf16[96,1536]{1,0:T(8,128)(2,1)} %collective-permute-done, ...), kind=kLoop, calls=%fused_computation.6 | loop fusion | flops 7077888 | bytes 4718592 | tf_op jit(solution)/shard_map/concatenate | solution.py:548
  120.8 2.7 %collective-permute-start.26 = (bf16[384,1536]{1,0:T(8,128)(2,1)}, bf16[384,1536]{1,0:T(8,128)(2,1)}, u32[]{:S(2)}, u32[]{:S(2)}) collective-permute-start(bf16[384,1536]{1,0:T(8,128)(2,1)} %get-tuple-element.90), channel_id=1, source_target_pairs={{0,24},{8,0},{16,8},{24,16},{32,56},{40,32},{48,40},{56,48},{64,88... | collective-permute-start | bytes 3538952 | tf_op jit(solution)/shard_map/ppermute | solution.py:60
  123.5 7.0 %collective-permute-done.21.refs_1_.refs_6_ = bf16[4,6,128,128]{3,2,1,0:T(8,128)(2,1)S(1)} collective-permute-done((bf16[4,6,128,128]{3,2,1,0:T(8,128)(2,1)S(1)}, bf16[4,6,128,128]{3,2,1,0:T(8,128)(2,1)S(1)}, u32[]{:S(2)}, u32[]{:S(2)}) %collective-permute-start.21) | collective-permute-done | bytes 786464 | tf_op jit(solution)/shard_map/ppermute | solution.py:60
  130.5 0.8 slice.180
  131.8 1.8 slice.181
  133.6 2.7 %collective-permute-start.24 = (bf16[2,6,128,128]{3,2,1,0:T(8,128)(2,1)}, bf16[2,6,128,128]{3,2,1,0:T(8,128)(2,1)S(1)}, u32[]{:S(2)}, u32[]{:S(2)}) collective-permute-start(bf16[2,6,128,128]{3,2,1,0:T(8,128)(2,1)} %slice.181), channel_id=1, source_target_pairs={{0,96},{8,104},{16,112},{24,120},{32,0},{40,8},{48,16},{56,24},{64... | collective-permute-start | bytes 1179656 | tf_op jit(solution)/shard_map/ppermute | solution.py:60
  136.3 5.4 %collective-permute-done.23.refs_3_.refs_8_ = bf16[2,6,128,128]{3,2,1,0:T(8,128)(2,1)S(1)} collective-permute-done((bf16[2,6,128,128]{3,2,1,0:T(8,128)(2,1)}, bf16[2,6,128,128]{3,2,1,0:T(8,128)(2,1)S(1)}, u32[]{:S(2)}, u32[]{:S(2)}) %collective-permute-start.23) | collective-permute-done | bytes 393248 | tf_op jit(solution)/shard_map/ppermute | solution.py:60
  141.7 0.8 collective-permute-start.29
  142.4 2.6 %copy-done.33 = bf16[896,3072]{1,0:T(8,128)(2,1)S(1)} copy-done((bf16[896,3072]{1,0:T(8,128)(2,1)S(1)}, bf16[896,3072]{1,0:T(8,128)(2,1)}, u32[]{:S(2)}) %copy-start.33) | copy-done | bytes 5505048
  145.0 12.0 %shard_map.249.act = bf16[896,1536]{1,0:T(8,128)(2,1)S(1)} custom-call(bf16[896,3072]{1,0:T(8,128)(2,1)S(1)} %copy-done.33, bf16[3072,1536]{1,0:T(8,128)(2,1)} %all-gather.2.cloned.1.call-done.weight), custom_call_target="tpu_custom_call" | custom-call | flops 8455716864 | bytes 18874368 | tf_op jit(solution)/shard_map/pallas_call | solution.py:285
  157.1 3.4 %shard_map.250.attended = bf16[896,384]{1,0:T(8,128)(2,1)S(1)} custom-call(bf16[3,3,128,128]{3,2,1,0:T(8,128)(2,1)S(1)} %copy-done.10, f32[1,2048]{1,0:T(1,128)S(1)} %reshape.232.live, bf16[768,384]{1,0:T(8,128)(2,1)S(1)} %copy-done.1, bf16[4,6,128,128]{3,2,1,0:T(8,128)(2,1)S(1)} %maximum_maximum_fusion.refs_0_.refs_5_, ...), custom_call_target="tpu_custom_call" | custom-call | flops 402653184 | bytes 5242880 | tf_op jit(solution)/shard_map/pallas_call | solution.py:252
  160.5 5.2 %shard_map.251 = bf16[896,768]{1,0:T(8,128)(2,1)S(1)} custom-call(s32[2]{0:T(128)S(1)} %pad_add_fusion.1.ids, bf16[896,1536]{1,0:T(8,128)(2,1)S(1)} %shard_map.249.act, bf16[896,384]{1,0:T(8,128)(2,1)S(1)} %shard_map.250.attended, bf16[3072,384]{1,0:T(8,128)(2,1)S(1)} %bitcast.15, bf16[384,1536]{1,0:T(8,128)(2,1)} %collective-permute-done.25.refs_0_, ...), custom_call_target="tpu_custom_call" | custom-call | flops 2642411520 | bytes 8388608 | tf_op jit(solution)/shard_map/pallas_call | solution.py:324
  165.8 6.0 %collective-permute-start.27 = (bf16[448,768]{1,0:T(8,128)(2,1)S(1)}, bf16[448,768]{1,0:T(8,128)(2,1)S(1)}, u32[]{:S(2)}, u32[]{:S(2)}) collective-permute-start(bf16[448,768]{1,0:T(8,128)(2,1)S(1)} %slice.217), channel_id=1, source_target_pairs={{0,1},{1,0},{2,3},{3,2},{4,5},{5,4},{6,7},{7,6},{8,9},{9,8},{10,11... | collective-permute-start | bytes 2064392 | tf_op jit(solution)/shard_map/ppermute | solution.py:78
  171.8 5.2 %shard_map.252 = bf16[896,768]{1,0:T(8,128)(2,1)S(1)} custom-call(s32[2]{0:T(128)S(1)} %pad_add_fusion.1.ids, bf16[896,1536]{1,0:T(8,128)(2,1)S(1)} %shard_map.249.act, bf16[896,384]{1,0:T(8,128)(2,1)S(1)} %shard_map.250.attended, bf16[3072,384]{1,0:T(8,128)(2,1)S(1)} %bitcast.16, bf16[384,1536]{1,0:T(8,128)(2,1)} %collective-permute-done.28.refs_0_, ...), custom_call_target="tpu_custom_call" | custom-call | flops 2642411520 | bytes 8388608 | tf_op jit(solution)/shard_map/pallas_call | solution.py:324
  177.5 2.7 %collective-permute-start.31 = (bf16[112,384]{1,0:T(8,128)(2,1)S(1)}, bf16[112,384]{1,0:T(8,128)(2,1)S(1)}, u32[]{:S(2)}, u32[]{:S(2)}) collective-permute-start(bf16[112,384]{1,0:T(8,128)(2,1)S(1)} %get-tuple-element.132), channel_id=1, source_target_pairs={{0,6},{1,7},{2,0},{3,1},{4,2},{5,3},{6,4},{7,5},{8,14},{9,15},{10,... | collective-permute-start | bytes 258056 | tf_op jit(solution)/shard_map/ppermute | solution.py:86
  180.2 7.7 %shard_map.253 = bf16[896,1536]{1,0:T(8,128)(2,1)S(1)} custom-call(s32[2]{0:T(128)S(1)} %pad_add_fusion.1.ids, bf16[896,1536]{1,0:T(8,128)(2,1)S(1)} %shard_map.249.act, bf16[896,384]{1,0:T(8,128)(2,1)S(1)} %shard_map.250.attended, bf16[3072,384]{1,0:T(8,128)(2,1)S(1)} %bitcast.17, bf16[192,1536]{1,0:T(8,128)(2,1)S(1)} %copy-done.24, ...), custom_call_target="tpu_custom_call" | custom-call | flops 5284823040 | bytes 8388608 | tf_op jit(solution)/shard_map/pallas_call | solution.py:324
  188.1 1.1 collective-permute-start.35
  189.5 2.7 %collective-permute-start.34 = (bf16[112,384]{1,0:T(8,128)(2,1)S(1)}, bf16[112,384]{1,0:T(8,128)(2,1)S(1)}, u32[]{:S(2)}, u32[]{:S(2)}) collective-permute-start(bf16[112,384]{1,0:T(8,128)(2,1)S(1)} %get-tuple-element.130), channel_id=1, source_target_pairs={{0,6},{1,7},{2,0},{3,1},{4,2},{5,3},{6,4},{7,5},{8,14},{9,15},{10,... | collective-permute-start | bytes 258056 | tf_op jit(solution)/shard_map/ppermute | solution.py:86
  192.4 1.5 collective-permute-start.40
  194.0 0.9 collective-permute-done.33
  195.5 2.7 %collective-permute-start.38 = (bf16[112,768]{1,0:T(8,128)(2,1)S(1)}, bf16[112,768]{1,0:T(8,128)(2,1)S(1)}, u32[]{:S(2)}, u32[]{:S(2)}) collective-permute-start(bf16[112,768]{1,0:T(8,128)(2,1)S(1)} %get-tuple-element.123), channel_id=1, source_target_pairs={{0,6},{1,7},{2,0},{3,1},{4,2},{5,3},{6,4},{7,5},{8,14},{9,15},{10,... | collective-permute-start | bytes 516104 | tf_op jit(solution)/shard_map/ppermute | solution.py:86
  198.3 4.5 %collective-permute-done.36 = bf16[112,768]{1,0:T(8,128)(2,1)S(1)} collective-permute-done((bf16[112,768]{1,0:T(8,128)(2,1)S(1)}, bf16[112,768]{1,0:T(8,128)(2,1)S(1)}, u32[]{:S(2)}, u32[]{:S(2)}) %collective-permute-start.36) | collective-permute-done | bytes 172064 | tf_op jit(solution)/shard_map/ppermute | solution.py:85
  202.8 1.0 collective-permute-start.39
  204.5 2.2 collective-permute-start.43
  207.0 7.7 %collective-permute-done.43.refs_8_ = bf16[112,768]{1,0:T(8,128)(2,1)S(1)} collective-permute-done((bf16[112,768]{1,0:T(8,128)(2,1)S(1)}, bf16[112,768]{1,0:T(8,128)(2,1)S(1)}, u32[]{:S(2)}, u32[]{:S(2)}) %collective-permute-start.43) | collective-permute-done | bytes 172064 | tf_op jit(solution)/shard_map/ppermute | solution.py:96
  214.7 0.7 collective-permute-done.42.refs_7_
  215.4 2.8 %shard_map.254 = (bf16[32,3072]{1,0:T(8,128)(2,1)}, bf16[64,3072]{1,0:T(8,128)(2,1)}, bf16[16,3072]{1,0:T(8,128)(2,1)}, f32[64,64]{1,0:T(8,128)S(1)}) custom-call(s32[2]{0:T(128)S(1)} %pad_add_fusion.1.ids, s32[16]{0:T(128)S(1)} %copy-done.34, s32[17]{0:T(128)S(1)} %copy-done.35, s32[128]{0:T(128)S(1)} %copy-done.36, s32[32]{0:T(128)S(1)} %copy-done.37, ...), custom_call_target="tpu_custom_call" | custom-call | flops 10000000 | bytes 5242880 | tf_op jit(solution)/shard_map/pallas_call | solution.py:400
  218.3 5.1 %collective-permute-start.44 = (f32[32,64]{1,0:T(8,128)S(1)}, f32[32,64]{1,0:T(8,128)S(1)}, u32[]{:S(2)}, u32[]{:S(2)}) collective-permute-start(f32[32,64]{1,0:T(8,128)S(1)} %get-tuple-element.139), channel_id=1, source_target_pairs={{0,1},{1,2},{2,3},{3,4},{4,5},{5,6},{6,7},{8,9},{9,10},{10,11},{11... | collective-permute-start | bytes 24584 | tf_op jit(solution)/shard_map/ppermute | solution.py:600
  223.3 2.1 collective-permute-start.45
  231.2 1.5 shard_map.255
  232.6 1.4 reshape.231
  (259 shorter events, 12.9 us)
Async XLA Ops:
  7.2 135.2 %all-gather.2.cloned.1.call-start = ((), (), s32[]{:S(2)}) async-start(), calls=%async_computation | async-start | bytes 10027008 | tf_op jit(solution)/shard_map/all_gather | solution.py:492
  9.8 24.1 %copy-start.38 = (bf16[96,1536]{1,0:T(8,128)(2,1)}, bf16[96,1536]{1,0:T(8,128)(2,1)S(1)}, u32[]{:S(2)}) copy-start(bf16[96,1536]{1,0:T(8,128)(2,1)S(1)} %get-tuple-element.135) | copy-start | bytes 884740
  9.8 16.9 %collective-permute-start = (bf16[96,1536]{1,0:T(8,128)(2,1)S(1)}, bf16[96,1536]{1,0:T(8,128)(2,1)}, u32[]{:S(2)}, u32[]{:S(2)}) collective-permute-start(bf16[96,1536]{1,0:T(8,128)(2,1)S(1)} %get-tuple-element.135), channel_id=1, source_target_pairs={{0,8},{8,16},{16,24},{24,0},{32,40},{40,48},{48,56},{56,32},{64,72... | collective-permute-start | bytes 884744 | tf_op jit(solution)/shard_map/ppermute | solution.py:60
  11.9 14.8 %collective-permute-start.1 = (bf16[96,1536]{1,0:T(8,128)(2,1)S(1)}, bf16[96,1536]{1,0:T(8,128)(2,1)S(1)}, u32[]{:S(2)}, u32[]{:S(2)}) collective-permute-start(bf16[96,1536]{1,0:T(8,128)(2,1)S(1)} %get-tuple-element.135), channel_id=1, source_target_pairs={{0,24},{8,0},{16,8},{24,16},{32,56},{40,32},{48,40},{56,48},{64,88... | collective-permute-start | bytes 884744 | tf_op jit(solution)/shard_map/ppermute | solution.py:60
  13.3 13.4 %collective-permute-start.2 = (bf16[96,1536]{1,0:T(8,128)(2,1)}, bf16[96,1536]{1,0:T(8,128)(2,1)}, u32[]{:S(2)}, u32[]{:S(2)}) collective-permute-start(bf16[96,1536]{1,0:T(8,128)(2,1)} %get-tuple-element.134), channel_id=1, source_target_pairs={{0,32},{8,40},{16,48},{24,56},{32,64},{40,72},{48,80},{56,88},{64,... | collective-permute-start | bytes 884744 | tf_op jit(solution)/shard_map/ppermute | solution.py:60
  15.0 11.7 %collective-permute-start.3 = (bf16[96,1536]{1,0:T(8,128)(2,1)}, bf16[96,1536]{1,0:T(8,128)(2,1)}, u32[]{:S(2)}, u32[]{:S(2)}) collective-permute-start(bf16[96,1536]{1,0:T(8,128)(2,1)} %get-tuple-element.134), channel_id=1, source_target_pairs={{0,96},{8,104},{16,112},{24,120},{32,0},{40,8},{48,16},{56,24},{64... | collective-permute-start | bytes 884744 | tf_op jit(solution)/shard_map/ppermute | solution.py:60
  26.7 21.8 %copy-start.40 = (bf16[96,1536]{1,0:T(8,128)(2,1)}, bf16[96,1536]{1,0:T(8,128)(2,1)S(1)}, u32[]{:S(2)}) copy-start(bf16[96,1536]{1,0:T(8,128)(2,1)S(1)} %collective-permute-done.1) | copy-start | bytes 884740
  26.7 18.6 %collective-permute-start.6 = (bf16[112,3072]{1,0:T(8,128)(2,1)S(1)}, bf16[112,3072]{1,0:T(8,128)(2,1)S(1)}, u32[]{:S(2)}, u32[]{:S(2)}) collective-permute-start(bf16[112,3072]{1,0:T(8,128)(2,1)S(1)} %shard_map.246), channel_id=1, source_target_pairs={{0,6},{1,7},{2,0},{3,1},{4,2},{5,3},{6,4},{7,5},{8,14},{9,15},{10,... | collective-permute-start | bytes 2064392 | tf_op jit(solution)/shard_map/ppermute | solution.py:506
  29.2 16.4 %collective-permute-start.7 = (bf16[112,3072]{1,0:T(8,128)(2,1)S(1)}, bf16[112,3072]{1,0:T(8,128)(2,1)S(1)}, u32[]{:S(2)}, u32[]{:S(2)}) collective-permute-start(bf16[112,3072]{1,0:T(8,128)(2,1)S(1)} %shard_map.246), channel_id=1, source_target_pairs={{0,2},{1,3},{2,4},{3,5},{4,6},{5,7},{6,0},{7,1},{8,10},{9,11},{10,... | collective-permute-start | bytes 2064392 | tf_op jit(solution)/shard_map/ppermute | solution.py:507
  29.2 16.4 %collective-permute-start.8 = (bf16[112,3072]{1,0:T(8,128)(2,1)S(1)}, bf16[112,3072]{1,0:T(8,128)(2,1)S(1)}, u32[]{:S(2)}, u32[]{:S(2)}) collective-permute-start(bf16[112,3072]{1,0:T(8,128)(2,1)S(1)} %shard_map.246), channel_id=1, source_target_pairs={{0,1},{1,0},{2,3},{3,2},{4,5},{5,4},{6,7},{7,6},{8,9},{9,8},{10,11... | collective-permute-start | bytes 2064392 | tf_op jit(solution)/shard_map/ppermute | solution.py:504
  32.6 12.2 %collective-permute-start.4 = (bf16[96,1536]{1,0:T(8,128)(2,1)}, bf16[96,1536]{1,0:T(8,128)(2,1)S(1)}, u32[]{:S(2)}, u32[]{:S(2)}) collective-permute-start(bf16[96,1536]{1,0:T(8,128)(2,1)} %collective-permute-done), channel_id=1, source_target_pairs={{0,8},{8,16},{16,24},{24,0},{32,40},{40,48},{48,56},{56,32},{64,72... | collective-permute-start | bytes 884744 | tf_op jit(solution)/shard_map/ppermute | solution.py:60
  32.8 12.6 %collective-permute-start.5 = (bf16[96,1536]{1,0:T(8,128)(2,1)}, bf16[96,1536]{1,0:T(8,128)(2,1)S(1)}, u32[]{:S(2)}, u32[]{:S(2)}) collective-permute-start(bf16[96,1536]{1,0:T(8,128)(2,1)} %collective-permute-done.2), channel_id=1, source_target_pairs={{0,32},{8,40},{16,48},{24,56},{32,64},{40,72},{48,80},{56,88},{64,... | collective-permute-start | bytes 884744 | tf_op jit(solution)/shard_map/ppermute | solution.py:60
  33.9 58.5 %copy-start.2 = (bf16[192,1536]{1,0:T(8,128)(2,1)}, bf16[192,1536]{1,0:T(8,128)(2,1)S(1)}, u32[]{:S(2)}) copy-start(bf16[192,1536]{1,0:T(8,128)(2,1)S(1)} %pad_maximum_fusion.6.refs_2_) | copy-start | bytes 1769476
  44.9 34.3 %collective-permute-start.13 = (bf16[192,1536]{1,0:T(8,128)(2,1)S(1)}, bf16[192,1536]{1,0:T(8,128)(2,1)S(1)}, u32[]{:S(2)}, u32[]{:S(2)}) collective-permute-start(bf16[192,1536]{1,0:T(8,128)(2,1)S(1)} %pad_maximum_fusion.8.refs_0_), channel_id=1, source_target_pairs={{0,32},{8,40},{16,48},{24,56},{32,64},{40,72},{48,80},{56,88},{64,... | collective-permute-start | bytes 1769480 | tf_op jit(solution)/shard_map/ppermute | solution.py:60
  45.7 14.0 %collective-permute-start.11 = (bf16[224,3072]{1,0:T(8,128)(2,1)S(1)}, bf16[224,3072]{1,0:T(8,128)(2,1)S(1)}, u32[]{:S(2)}, u32[]{:S(2)}) collective-permute-start(bf16[224,3072]{1,0:T(8,128)(2,1)S(1)} %pad_maximum_fusion), channel_id=1, source_target_pairs={{0,1},{1,0},{2,3},{3,2},{4,5},{5,4},{6,7},{7,6},{8,9},{9,8},{10,11... | collective-permute-start | bytes 4128776 | tf_op jit(solution)/shard_map/ppermute | solution.py:504
  48.5 15.0 %slice-start = ((s8[7077888]{0:T(1024)(128)(4,1)}), s8[4194304]{0:T(1024)(128)(4,1)S(1)}, s32[]{:S(2)}) async-start(s8[7077888]{0:T(1024)(128)(4,1)} %bitcast.25), calls=%async_computation.1 | async-start | bytes 8388608
  48.6 11.1 %collective-permute-start.10 = (bf16[56,3072]{1,0:T(8,128)(2,1)S(1)}, bf16[56,3072]{1,0:T(8,128)(2,1)S(1)}, u32[]{:S(2)}, u32[]{:S(2)}) collective-permute-start(bf16[56,3072]{1,0:T(8,128)(2,1)S(1)} %slice.171), channel_id=1, source_target_pairs={{0,2},{1,3},{2,4},{3,5},{4,6},{5,7},{6,0},{7,1},{8,10},{9,11},{10,... | collective-permute-start | bytes 1032200 | tf_op jit(solution)/shard_map/ppermute | solution.py:516
  48.7 11.0 %collective-permute-start.9 = (bf16[56,3072]{1,0:T(8,128)(2,1)S(1)}, bf16[56,3072]{1,0:T(8,128)(2,1)S(1)}, u32[]{:S(2)}, u32[]{:S(2)}) collective-permute-start(bf16[56,3072]{1,0:T(8,128)(2,1)S(1)} %slice.170), channel_id=1, source_target_pairs={{0,6},{1,7},{2,0},{3,1},{4,2},{5,3},{6,4},{7,5},{8,14},{9,15},{10,... | collective-permute-start | bytes 1032200 | tf_op jit(solution)/shard_map/ppermute | solution.py:515
  51.4 27.7 %collective-permute-start.14 = (bf16[192,1536]{1,0:T(8,128)(2,1)S(1)}, bf16[192,1536]{1,0:T(8,128)(2,1)S(1)}, u32[]{:S(2)}, u32[]{:S(2)}) collective-permute-start(bf16[192,1536]{1,0:T(8,128)(2,1)S(1)} %constant_dynamic-update-slice_fusion.7.refs_1_), channel_id=1, source_target_pairs={{0,96},{8,104},{16,112},{24,120},{32,0},{40,8},{48,16},{56,24},{64... | collective-permute-start | bytes 1769480 | tf_op jit(solution)/shard_map/ppermute | solution.py:60
  53.9 38.5 %copy-start.4 = (bf16[192,1536]{1,0:T(8,128)(2,1)}, bf16[192,1536]{1,0:T(8,128)(2,1)S(1)}, u32[]{:S(2)}) copy-start(bf16[192,1536]{1,0:T(8,128)(2,1)S(1)} %pad_maximum_fusion.7.refs_3_) | copy-start | bytes 1769476
  59.7 3.7 %collective-permute-start.12 = (bf16[112,3072]{1,0:T(8,128)(2,1)S(1)}, bf16[112,3072]{1,0:T(8,128)(2,1)S(1)}, u32[]{:S(2)}, u32[]{:S(2)}) collective-permute-start(bf16[112,3072]{1,0:T(8,128)(2,1)S(1)} %pad_maximum_fusion.5), channel_id=1, source_target_pairs={{0,1},{1,0},{2,3},{3,2},{4,5},{5,4},{6,7},{7,6},{8,9},{9,8},{10,11... | collective-permute-start | bytes 2064392 | tf_op jit(solution)/shard_map/ppermute | solution.py:504
  60.5 29.1 %collective-permute-start.15 = (bf16[192,1536]{1,0:T(8,128)(2,1)S(1)}, bf16[192,1536]{1,0:T(8,128)(2,1)S(1)}, u32[]{:S(2)}, u32[]{:S(2)}) collective-permute-start(bf16[192,1536]{1,0:T(8,128)(2,1)S(1)} %pad_maximum_fusion.6.refs_2_), channel_id=1, source_target_pairs={{0,8},{8,16},{16,24},{24,0},{32,40},{40,48},{48,56},{56,32},{64,72... | collective-permute-start | bytes 1769480 | tf_op jit(solution)/shard_map/ppermute | solution.py:60
  60.6 29.1 %collective-permute-start.16 = (bf16[192,1536]{1,0:T(8,128)(2,1)S(1)}, bf16[192,1536]{1,0:T(8,128)(2,1)S(1)}, u32[]{:S(2)}, u32[]{:S(2)}) collective-permute-start(bf16[192,1536]{1,0:T(8,128)(2,1)S(1)} %pad_maximum_fusion.7.refs_3_), channel_id=1, source_target_pairs={{0,24},{8,0},{16,8},{24,16},{32,56},{40,32},{48,40},{56,48},{64,88... | collective-permute-start | bytes 1769480 | tf_op jit(solution)/shard_map/ppermute | solution.py:60
  63.6 15.5 %copy-start.32 = (bf16[896,3072]{1,0:T(8,128)(2,1)}, bf16[896,3072]{1,0:T(8,128)(2,1)S(1)}, u32[]{:S(2)}) copy-start(bf16[896,3072]{1,0:T(8,128)(2,1)S(1)} %slice_dynamic-update-slice_fusion.x) | copy-start | bytes 16515076
  79.1 14.9 %copy-start.9 = (bf16[3,3,128,128]{3,2,1,0:T(8,128)(2,1)}, bf16[3,3,128,128]{3,2,1,0:T(8,128)(2,1)S(1)}, u32[]{:S(2)}) copy-start(bf16[3,3,128,128]{3,2,1,0:T(8,128)(2,1)S(1)} %get-tuple-element.73.query) | copy-start | bytes 884740
  79.1 14.9 %copy-start.13 = (bf16[192,1536]{1,0:T(8,128)(2,1)}, bf16[192,1536]{1,0:T(8,128)(2,1)S(1)}, u32[]{:S(2)}) copy-start(bf16[192,1536]{1,0:T(8,128)(2,1)S(1)} %collective-permute-done.13.refs_4_) | copy-start | bytes 1769476
  79.2 14.8 %copy-start.16 = (bf16[192,1536]{1,0:T(8,128)(2,1)}, bf16[192,1536]{1,0:T(8,128)(2,1)S(1)}, u32[]{:S(2)}) copy-start(bf16[192,1536]{1,0:T(8,128)(2,1)S(1)} %collective-permute-done.14.refs_5_) | copy-start | bytes 1769476
  89.7 12.1 %copy-start.44 = (bf16[2,3,128,128]{3,2,1,0:T(8,128)(2,1)}, bf16[2,3,128,128]{3,2,1,0:T(8,128)(2,1)S(1)}, u32[]{:S(2)}) copy-start(bf16[2,3,128,128]{3,2,1,0:T(8,128)(2,1)S(1)} %slice.177) | copy-start | bytes 589828
  89.7 12.1 %collective-permute-start.17 = (bf16[1,6,128,128]{3,2,1,0:T(8,128)(2,1)S(1)}, bf16[1,6,128,128]{3,2,1,0:T(8,128)(2,1)S(1)}, u32[]{:S(2)}, u32[]{:S(2)}) collective-permute-start(bf16[1,6,128,128]{3,2,1,0:T(8,128)(2,1)S(1)} %bitcast.27), channel_id=1, source_target_pairs={{0,8},{8,16},{16,24},{24,0},{32,40},{40,48},{48,56},{56,32},{64,72... | collective-permute-start | bytes 589832 | tf_op jit(solution)/shard_map/ppermute | solution.py:60
  89.8 12.0 %collective-permute-start.18 = (bf16[1,6,128,128]{3,2,1,0:T(8,128)(2,1)S(1)}, bf16[1,6,128,128]{3,2,1,0:T(8,128)(2,1)S(1)}, u32[]{:S(2)}, u32[]{:S(2)}) collective-permute-start(bf16[1,6,128,128]{3,2,1,0:T(8,128)(2,1)S(1)} %bitcast.28), channel_id=1, source_target_pairs={{0,24},{8,0},{16,8},{24,16},{32,56},{40,32},{48,40},{56,48},{64,88... | collective-permute-start | bytes 589832 | tf_op jit(solution)/shard_map/ppermute | solution.py:60
  94.0 19.8 %copy-start.56 = (s32[4]{0:T(128)S(1)}, s32[4]{0:T(128)}, u32[]{:S(2)}) copy-start(s32[4]{0:T(128)} %constant.147.clone) | copy-start | bytes 52
  102.5 7.4 %collective-permute-start.19 = (bf16[1,3,128,128]{3,2,1,0:T(8,128)(2,1)S(1)}, bf16[1,3,128,128]{3,2,1,0:T(8,128)(2,1)S(1)}, u32[]{:S(2)}, u32[]{:S(2)}) collective-permute-start(bf16[1,3,128,128]{3,2,1,0:T(8,128)(2,1)S(1)} %slice.178), channel_id=1, source_target_pairs={{0,8},{8,16},{16,24},{24,0},{32,40},{40,48},{48,56},{56,32},{64,72... | collective-permute-start | bytes 294920 | tf_op jit(solution)/shard_map/ppermute | solution.py:60
  102.6 7.3 %collective-permute-start.20 = (bf16[1,3,128,128]{3,2,1,0:T(8,128)(2,1)S(1)}, bf16[1,3,128,128]{3,2,1,0:T(8,128)(2,1)S(1)}, u32[]{:S(2)}, u32[]{:S(2)}) collective-permute-start(bf16[1,3,128,128]{3,2,1,0:T(8,128)(2,1)S(1)} %slice.179), channel_id=1, source_target_pairs={{0,24},{8,0},{16,8},{24,16},{32,56},{40,32},{48,40},{56,48},{64,88... | collective-permute-start | bytes 294920 | tf_op jit(solution)/shard_map/ppermute | solution.py:60
  111.0 19.5 %collective-permute-start.21 = (bf16[4,6,128,128]{3,2,1,0:T(8,128)(2,1)S(1)}, bf16[4,6,128,128]{3,2,1,0:T(8,128)(2,1)S(1)}, u32[]{:S(2)}, u32[]{:S(2)}) collective-permute-start(bf16[4,6,128,128]{3,2,1,0:T(8,128)(2,1)S(1)} %maximum_maximum_fusion.refs_0_.refs_5_), channel_id=1, source_target_pairs={{0,32},{8,40},{16,48},{24,56},{32,64},{40,72},{48,80},{56,88},{64,... | collective-permute-start | bytes 2359304 | tf_op jit(solution)/shard_map/ppermute | solution.py:60
  111.1 19.4 %collective-permute-start.22 = (bf16[4,6,128,128]{3,2,1,0:T(8,128)(2,1)S(1)}, bf16[4,6,128,128]{3,2,1,0:T(8,128)(2,1)}, u32[]{:S(2)}, u32[]{:S(2)}) collective-permute-start(bf16[4,6,128,128]{3,2,1,0:T(8,128)(2,1)S(1)} %maximum_maximum_fusion.refs_0_.refs_5_), channel_id=1, source_target_pairs={{0,96},{8,104},{16,112},{24,120},{32,0},{40,8},{48,16},{56,24},{64... | collective-permute-start | bytes 2359304 | tf_op jit(solution)/shard_map/ppermute | solution.py:60
  118.2 13.1 %copy-start.53 = (s32[16]{0:T(128)S(1)}, s32[16]{0:T(128)}, u32[]{:S(2)}) copy-start(s32[16]{0:T(128)} %mul.109) | copy-start | bytes 196
  118.2 13.1 %copy-start.58 = (s32[8]{0:T(128)S(1)}, s32[8]{0:T(128)}, u32[]{:S(2)}) copy-start(s32[8]{0:T(128)} %copy-done.57) | copy-start | bytes 100
  118.3 13.2 %copy-start.36 = (s32[128]{0:T(128)S(1)}, s32[128]{0:T(128)}, u32[]{:S(2)}) copy-start(s32[128]{0:T(128)} %counts.1) | copy-start | bytes 1540
  120.8 39.6 %collective-permute-start.25 = (bf16[384,1536]{1,0:T(8,128)(2,1)}, bf16[384,1536]{1,0:T(8,128)(2,1)}, u32[]{:S(2)}, u32[]{:S(2)}) collective-permute-start(bf16[384,1536]{1,0:T(8,128)(2,1)} %get-tuple-element.89), channel_id=1, source_target_pairs={{0,8},{8,16},{16,24},{24,0},{32,40},{40,48},{48,56},{56,32},{64,72... | collective-permute-start | bytes 3538952 | tf_op jit(solution)/shard_map/ppermute | solution.py:60
  120.8 39.7 %collective-permute-start.26 = (bf16[384,1536]{1,0:T(8,128)(2,1)}, bf16[384,1536]{1,0:T(8,128)(2,1)}, u32[]{:S(2)}, u32[]{:S(2)}) collective-permute-start(bf16[384,1536]{1,0:T(8,128)(2,1)} %get-tuple-element.90), channel_id=1, source_target_pairs={{0,24},{8,0},{16,8},{24,16},{32,56},{40,32},{48,40},{56,48},{64,88... | collective-permute-start | bytes 3538952 | tf_op jit(solution)/shard_map/ppermute | solution.py:60
  131.3 10.4 %collective-permute-start.23 = (bf16[2,6,128,128]{3,2,1,0:T(8,128)(2,1)}, bf16[2,6,128,128]{3,2,1,0:T(8,128)(2,1)S(1)}, u32[]{:S(2)}, u32[]{:S(2)}) collective-permute-start(bf16[2,6,128,128]{3,2,1,0:T(8,128)(2,1)} %slice.180), channel_id=1, source_target_pairs={{0,32},{8,40},{16,48},{24,56},{32,64},{40,72},{48,80},{56,88},{64,... | collective-permute-start | bytes 1179656 | tf_op jit(solution)/shard_map/ppermute | solution.py:60
  133.6 23.4 %copy-start.1 = (bf16[768,384]{1,0:T(8,128)(2,1)S(1)}, bf16[768,384]{1,0:T(8,128)(2,1)}, u32[]{:S(2)}) copy-start(bf16[768,384]{1,0:T(8,128)(2,1)} %copy-done) | copy-start | bytes 1769476
  133.6 23.4 %copy-start.10 = (bf16[3,3,128,128]{3,2,1,0:T(8,128)(2,1)S(1)}, bf16[3,3,128,128]{3,2,1,0:T(8,128)(2,1)}, u32[]{:S(2)}) copy-start(bf16[3,3,128,128]{3,2,1,0:T(8,128)(2,1)} %copy-done.9) | copy-start | bytes 884740
  133.6 23.4 %collective-permute-start.24 = (bf16[2,6,128,128]{3,2,1,0:T(8,128)(2,1)}, bf16[2,6,128,128]{3,2,1,0:T(8,128)(2,1)S(1)}, u32[]{:S(2)}, u32[]{:S(2)}) collective-permute-start(bf16[2,6,128,128]{3,2,1,0:T(8,128)(2,1)} %slice.181), channel_id=1, source_target_pairs={{0,96},{8,104},{16,112},{24,120},{32,0},{40,8},{48,16},{56,24},{64... | collective-permute-start | bytes 1179656 | tf_op jit(solution)/shard_map/ppermute | solution.py:60
  136.3 35.5 %collective-permute-start.28 = (bf16[384,1536]{1,0:T(8,128)(2,1)}, bf16[384,1536]{1,0:T(8,128)(2,1)}, u32[]{:S(2)}, u32[]{:S(2)}) collective-permute-start(bf16[384,1536]{1,0:T(8,128)(2,1)} %get-tuple-element.91), channel_id=1, source_target_pairs={{0,32},{8,40},{16,48},{24,56},{32,64},{40,72},{48,80},{56,88},{64,... | collective-permute-start | bytes 3538952 | tf_op jit(solution)/shard_map/ppermute | solution.py:60
  141.7 30.1 %collective-permute-start.29 = (bf16[384,1536]{1,0:T(8,128)(2,1)}, bf16[384,1536]{1,0:T(8,128)(2,1)}, u32[]{:S(2)}, u32[]{:S(2)}) collective-permute-start(bf16[384,1536]{1,0:T(8,128)(2,1)} %get-tuple-element.92), channel_id=1, source_target_pairs={{0,96},{8,104},{16,112},{24,120},{32,0},{40,8},{48,16},{56,24},{64... | collective-permute-start | bytes 3538952 | tf_op jit(solution)/shard_map/ppermute | solution.py:60
  165.8 11.2 %collective-permute-start.27 = (bf16[448,768]{1,0:T(8,128)(2,1)S(1)}, bf16[448,768]{1,0:T(8,128)(2,1)S(1)}, u32[]{:S(2)}, u32[]{:S(2)}) collective-permute-start(bf16[448,768]{1,0:T(8,128)(2,1)S(1)} %slice.217), channel_id=1, source_target_pairs={{0,1},{1,0},{2,3},{3,2},{4,5},{5,4},{6,7},{7,6},{8,9},{9,8},{10,11... | collective-permute-start | bytes 2064392 | tf_op jit(solution)/shard_map/ppermute | solution.py:78
  177.3 10.7 %collective-permute-start.32 = (bf16[448,768]{1,0:T(8,128)(2,1)S(1)}, bf16[448,768]{1,0:T(8,128)(2,1)S(1)}, u32[]{:S(2)}, u32[]{:S(2)}) collective-permute-start(bf16[448,768]{1,0:T(8,128)(2,1)S(1)} %slice.186), channel_id=1, source_target_pairs={{0,1},{1,0},{2,3},{3,2},{4,5},{5,4},{6,7},{7,6},{8,9},{9,8},{10,11... | collective-permute-start | bytes 2064392 | tf_op jit(solution)/shard_map/ppermute | solution.py:78
  177.4 10.5 %collective-permute-start.30 = (bf16[112,384]{1,0:T(8,128)(2,1)S(1)}, bf16[112,384]{1,0:T(8,128)(2,1)S(1)}, u32[]{:S(2)}, u32[]{:S(2)}) collective-permute-start(bf16[112,384]{1,0:T(8,128)(2,1)S(1)} %get-tuple-element.133), channel_id=1, source_target_pairs={{0,2},{1,3},{2,4},{3,5},{4,6},{5,7},{6,0},{7,1},{8,10},{9,11},{10,... | collective-permute-start | bytes 258056 | tf_op jit(solution)/shard_map/ppermute | solution.py:85
  177.5 10.5 %collective-permute-start.31 = (bf16[112,384]{1,0:T(8,128)(2,1)S(1)}, bf16[112,384]{1,0:T(8,128)(2,1)S(1)}, u32[]{:S(2)}, u32[]{:S(2)}) collective-permute-start(bf16[112,384]{1,0:T(8,128)(2,1)S(1)} %get-tuple-element.132), channel_id=1, source_target_pairs={{0,6},{1,7},{2,0},{3,1},{4,2},{5,3},{6,4},{7,5},{8,14},{9,15},{10,... | collective-permute-start | bytes 258056 | tf_op jit(solution)/shard_map/ppermute | solution.py:86
  188.1 6.8 %collective-permute-start.35 = (bf16[448,1536]{1,0:T(8,128)(2,1)S(1)}, bf16[448,1536]{1,0:T(8,128)(2,1)S(1)}, u32[]{:S(2)}, u32[]{:S(2)}) collective-permute-start(bf16[448,1536]{1,0:T(8,128)(2,1)S(1)} %slice.191), channel_id=1, source_target_pairs={{0,1},{1,0},{2,3},{3,2},{4,5},{5,4},{6,7},{7,6},{8,9},{9,8},{10,11... | collective-permute-start | bytes 4128776 | tf_op jit(solution)/shard_map/ppermute | solution.py:78
  189.4 5.4 %collective-permute-start.33 = (bf16[112,384]{1,0:T(8,128)(2,1)S(1)}, bf16[112,384]{1,0:T(8,128)(2,1)S(1)}, u32[]{:S(2)}, u32[]{:S(2)}) collective-permute-start(bf16[112,384]{1,0:T(8,128)(2,1)S(1)} %get-tuple-element.131), channel_id=1, source_target_pairs={{0,2},{1,3},{2,4},{3,5},{4,6},{5,7},{6,0},{7,1},{8,10},{9,11},{10,... | collective-permute-start | bytes 258056 | tf_op jit(solution)/shard_map/ppermute | solution.py:85
  189.5 5.4 %collective-permute-start.34 = (bf16[112,384]{1,0:T(8,128)(2,1)S(1)}, bf16[112,384]{1,0:T(8,128)(2,1)S(1)}, u32[]{:S(2)}, u32[]{:S(2)}) collective-permute-start(bf16[112,384]{1,0:T(8,128)(2,1)S(1)} %get-tuple-element.130), channel_id=1, source_target_pairs={{0,6},{1,7},{2,0},{3,1},{4,2},{5,3},{6,4},{7,5},{8,14},{9,15},{10,... | collective-permute-start | bytes 258056 | tf_op jit(solution)/shard_map/ppermute | solution.py:86
  192.3 14.5 %collective-permute-start.41 = (bf16[112,768]{1,0:T(8,128)(2,1)S(1)}, bf16[112,768]{1,0:T(8,128)(2,1)S(1)}, u32[]{:S(2)}, u32[]{:S(2)}) collective-permute-start(bf16[112,768]{1,0:T(8,128)(2,1)S(1)} %pad_maximum_fusion.12), channel_id=1, source_target_pairs={{0,6},{1,7},{2,0},{3,1},{4,2},{5,3},{6,4},{7,5},{8,14},{9,15},{10,... | collective-permute-start | bytes 516104 | tf_op jit(solution)/shard_map/ppermute | solution.py:96
  192.4 14.6 %collective-permute-start.40 = (bf16[112,768]{1,0:T(8,128)(2,1)S(1)}, bf16[112,768]{1,0:T(8,128)(2,1)S(1)}, u32[]{:S(2)}, u32[]{:S(2)}) collective-permute-start(bf16[112,768]{1,0:T(8,128)(2,1)S(1)} %pad_maximum_fusion.11), channel_id=1, source_target_pairs={{0,2},{1,3},{2,4},{3,5},{4,6},{5,7},{6,0},{7,1},{8,10},{9,11},{10,... | collective-permute-start | bytes 516104 | tf_op jit(solution)/shard_map/ppermute | solution.py:95
  195.5 7.3 %collective-permute-start.36 = (bf16[112,768]{1,0:T(8,128)(2,1)S(1)}, bf16[112,768]{1,0:T(8,128)(2,1)S(1)}, u32[]{:S(2)}, u32[]{:S(2)}) collective-permute-start(bf16[112,768]{1,0:T(8,128)(2,1)S(1)} %get-tuple-element.125), channel_id=1, source_target_pairs={{0,2},{1,3},{2,4},{3,5},{4,6},{5,7},{6,0},{7,1},{8,10},{9,11},{10,... | collective-permute-start | bytes 516104 | tf_op jit(solution)/shard_map/ppermute | solution.py:85
  195.5 7.2 %collective-permute-start.38 = (bf16[112,768]{1,0:T(8,128)(2,1)S(1)}, bf16[112,768]{1,0:T(8,128)(2,1)S(1)}, u32[]{:S(2)}, u32[]{:S(2)}) collective-permute-start(bf16[112,768]{1,0:T(8,128)(2,1)S(1)} %get-tuple-element.123), channel_id=1, source_target_pairs={{0,6},{1,7},{2,0},{3,1},{4,2},{5,3},{6,4},{7,5},{8,14},{9,15},{10,... | collective-permute-start | bytes 516104 | tf_op jit(solution)/shard_map/ppermute | solution.py:86
  202.8 12.5 %collective-permute-start.39 = (bf16[112,1536]{1,0:T(8,128)(2,1)S(1)}, bf16[112,1536]{1,0:T(8,128)(2,1)S(1)}, u32[]{:S(2)}, u32[]{:S(2)}) collective-permute-start(bf16[112,1536]{1,0:T(8,128)(2,1)S(1)} %pad_maximum_fusion.10), channel_id=1, source_target_pairs={{0,6},{1,7},{2,0},{3,1},{4,2},{5,3},{6,4},{7,5},{8,14},{9,15},{10,... | collective-permute-start | bytes 1032200 | tf_op jit(solution)/shard_map/ppermute | solution.py:96
  203.9 11.5 %collective-permute-start.37 = (bf16[112,1536]{1,0:T(8,128)(2,1)S(1)}, bf16[112,1536]{1,0:T(8,128)(2,1)S(1)}, u32[]{:S(2)}, u32[]{:S(2)}) collective-permute-start(bf16[112,1536]{1,0:T(8,128)(2,1)S(1)} %pad_maximum_fusion.9), channel_id=1, source_target_pairs={{0,2},{1,3},{2,4},{3,5},{4,6},{5,7},{6,0},{7,1},{8,10},{9,11},{10,... | collective-permute-start | bytes 1032200 | tf_op jit(solution)/shard_map/ppermute | solution.py:95
  204.5 10.2 %collective-permute-start.43 = (bf16[112,768]{1,0:T(8,128)(2,1)S(1)}, bf16[112,768]{1,0:T(8,128)(2,1)S(1)}, u32[]{:S(2)}, u32[]{:S(2)}) collective-permute-start(bf16[112,768]{1,0:T(8,128)(2,1)S(1)} %pad_maximum_fusion.14), channel_id=1, source_target_pairs={{0,6},{1,7},{2,0},{3,1},{4,2},{5,3},{6,4},{7,5},{8,14},{9,15},{10,... | collective-permute-start | bytes 516104 | tf_op jit(solution)/shard_map/ppermute | solution.py:96
  206.8 8.6 %collective-permute-start.42 = (bf16[112,768]{1,0:T(8,128)(2,1)S(1)}, bf16[112,768]{1,0:T(8,128)(2,1)S(1)}, u32[]{:S(2)}, u32[]{:S(2)}) collective-permute-start(bf16[112,768]{1,0:T(8,128)(2,1)S(1)} %pad_maximum_fusion.13), channel_id=1, source_target_pairs={{0,2},{1,3},{2,4},{3,5},{4,6},{5,7},{6,0},{7,1},{8,10},{9,11},{10,... | collective-permute-start | bytes 516104 | tf_op jit(solution)/shard_map/ppermute | solution.py:95
  218.3 11.7 %copy-start.30 = (f32[64,64]{1,0:T(8,128)}, f32[64,64]{1,0:T(8,128)S(1)}, u32[]{:S(2)}) copy-start(f32[64,64]{1,0:T(8,128)S(1)} %get-tuple-element.108.middle) | copy-start | bytes 49156
  218.3 11.7 %collective-permute-start.44 = (f32[32,64]{1,0:T(8,128)S(1)}, f32[32,64]{1,0:T(8,128)S(1)}, u32[]{:S(2)}, u32[]{:S(2)}) collective-permute-start(f32[32,64]{1,0:T(8,128)S(1)} %get-tuple-element.139), channel_id=1, source_target_pairs={{0,1},{1,2},{2,3},{3,4},{4,5},{5,6},{6,7},{8,9},{9,10},{10,11},{11... | collective-permute-start | bytes 24584 | tf_op jit(solution)/shard_map/ppermute | solution.py:600
  223.3 6.6 %collective-permute-start.45 = (f32[32,64]{1,0:T(8,128)S(1)}, f32[32,64]{1,0:T(8,128)S(1)}, u32[]{:S(2)}, u32[]{:S(2)}) collective-permute-start(f32[32,64]{1,0:T(8,128)S(1)} %get-tuple-element.138), channel_id=1, source_target_pairs={{1,0},{2,1},{3,2},{4,3},{5,4},{6,5},{7,6},{9,8},{10,9},{11,10},{12... | collective-permute-start | bytes 24584 | tf_op jit(solution)/shard_map/ppermute | solution.py:601
  (46 other events, 202.7 us)
Sparse Core Ops, SparseCore 0:
  10.2 99.2 all-gather.1
